TPU v7x, 32 devices: a whole 2x2x4 slice. The times are simulated.
32 devices in a mesh: dp: 16 (over z, y, x), seq: 2 (over core).
Axes of the slice: x: 2, y: 2, z: 4, core: 2. Of those that a mesh axis runs over, the one named last changes fastest.
Arguments:
- tokens: bfloat16 [16384, 1024], P(('dp', 'seq')), may hold values from -6 to 6
- seq_lengths: int32 [16, 3], P('dp'), may hold values from 1 to 1022, as said below
- w_query: bfloat16 [1024, 1024], P('dp', 'seq'), may hold values from -0.1875 to 0.1875
- w_key: bfloat16 [1024, 1024], P('dp', 'seq'), may hold values from -0.1875 to 0.1875
- w_value: bfloat16 [1024, 1024], P('dp', 'seq'), may hold values from -0.1875 to 0.1875
- w_out: bfloat16 [1024, 1024], P('dp', 'seq'), may hold values from -1.5 to 1.5
- w_gate: bfloat16 [1024, 2752], P('dp', 'seq'), may hold values from -0.1875 to 0.1875
- w_up: bfloat16 [1024, 2752], P('dp', 'seq'), may hold values from -0.1875 to 0.1875
- w_down: bfloat16 [2752, 1024], P('dp', 'seq'), may hold values from -0.109375 to 0.109375
- gain_attn: bfloat16 [1024], P('dp'), may hold values from 0.099609375 to 1.8984375
- gain_mlp: bfloat16 [1024], P('dp'), may hold values from 0.099609375 to 1.8984375
- cotangent: bfloat16 [16384, 1024], P(('dp', 'seq')), may hold values from -6 to 6
Outputs:
- mixed: bfloat16 [16384, 1024], P(('dp', 'seq'))
- grad_tokens: float32 [16384, 1024], P(('dp', 'seq'))
- grad_query: float32 [1024, 1024], P('dp', 'seq')
- grad_key: float32 [1024, 1024], P('dp', 'seq')
- grad_value: float32 [1024, 1024], P('dp', 'seq')
- grad_out: float32 [1024, 1024], P('dp', 'seq')
- grad_gate: float32 [1024, 2752], P('dp', 'seq')
- grad_up: float32 [1024, 2752], P('dp', 'seq')
- grad_down: float32 [2752, 1024], P('dp', 'seq')
- grad_gain_attn: float32 [1024], P('dp')
- grad_gain_mlp: float32 [1024], P('dp')
Inputs may be any that keep to these rules, and one draw needn't show every extreme that they name: `seq_lengths`: each group's row holds three lengths in order: a first sequence of 1 to 256 tokens, a middle one that reaches from the group's first device to its last, and a last one of 1 to 256 tokens; the three sum to 1024; in some group the first and last sequences have one token each.
All inputs are finite; a program needn't handle non-finite values.
Results may differ from a plain program's by a relative error of at most 0.02.
Values may be sent and summed in bfloat16 or wider, within the bound.
A program may use at most 192 MiB of HBM per device.

v0:
```python
import jax
import jax.numpy as jnp
from jax import lax
from jax.sharding import PartitionSpec as P

HEADS = 16
HEAD_DIM = 64
WINDOW = 64


eps_norm = 1e-05


def from_behind(block, axis, distance):
    devices = range(lax.axis_size(axis))
    route = [(i - distance, i) for i in devices if i - distance in devices]
    return lax.ppermute(block, axis, route)


def inverse_rms(values):
    return lax.rsqrt(jnp.mean(values * values, axis=-1, keepdims=True) + eps_norm)


def doc_numbers(lengths_row, positions):
    first_end = lengths_row[0]
    second_end = lengths_row[0] + lengths_row[1]
    return (positions >= first_end).astype(jnp.int32) + (positions >= second_end).astype(jnp.int32)


def window_mask(query_pos, query_doc, key_pos, key_doc, window):
    after = key_pos[None, :] >= query_pos[:, None] - window
    before = key_pos[None, :] <= query_pos[:, None]
    inside = (key_pos[None, :] >= 0) & (key_doc[None, :] == query_doc[:, None])
    return after & before & inside


def norm_back(values, inverse, gain, grad_norm):
    scaled = grad_norm * gain
    mean_term = jnp.mean(values * scaled, axis=-1, keepdims=True)
    grad_values = inverse * scaled - values * (inverse * inverse * inverse) * mean_term
    grad_gain = jnp.sum(values * inverse * grad_norm, axis=0)
    return (grad_values, grad_gain)


def project(left, right):
    return jnp.dot(left, right, preferred_element_type=jnp.float32)


def project_back(grad_rows, weight):
    return jnp.einsum("tf,df->td", grad_rows, weight, preferred_element_type=jnp.float32)


def weight_grad(inputs, grad_rows):
    return jnp.einsum("td,tf->df", inputs, grad_rows, preferred_element_type=jnp.float32)


def shards(
    tokens,
    seq_lengths,
    w_query,
    w_key,
    w_value,
    w_out,
    w_gate,
    w_up,
    w_down,
    gain_attn,
    gain_mlp,
    cotangent,
):
    row_count = tokens.shape[0]
    block_rows = min(512, row_count)
    head_group = HEADS // 2
    score_scale = HEAD_DIM ** (-0.5)
    row_parts = (
        lax.all_gather(w_query, "dp", axis=0, tiled=True),
        lax.all_gather(w_key, "dp", axis=0, tiled=True),
        lax.all_gather(w_value, "dp", axis=0, tiled=True),
        lax.all_gather(w_out, "dp", axis=0, tiled=True),
        lax.all_gather(w_gate, "dp", axis=0, tiled=True),
        lax.all_gather(w_up, "dp", axis=0, tiled=True),
        lax.all_gather(w_down, "dp", axis=0, tiled=True),
        lax.all_gather(gain_attn, "dp", axis=0, tiled=True),
        lax.all_gather(gain_mlp, "dp", axis=0, tiled=True),
    )
    full_mats = (
        lax.all_gather(row_parts[0], "seq", axis=1, tiled=True),
        lax.all_gather(row_parts[1], "seq", axis=1, tiled=True),
        lax.all_gather(row_parts[2], "seq", axis=1, tiled=True),
        lax.all_gather(row_parts[3], "seq", axis=1, tiled=True),
        lax.all_gather(row_parts[4], "seq", axis=1, tiled=True),
        lax.all_gather(row_parts[5], "seq", axis=1, tiled=True),
        lax.all_gather(row_parts[6], "seq", axis=1, tiled=True),
    )
    query_w, key_w, value_w, out_w, gate_w, up_w, down_full = full_mats
    gain_one = row_parts[7].astype(jnp.float32)
    gain_two = row_parts[8].astype(jnp.float32)
    inputs = tokens.astype(jnp.float32)
    inv_one = inverse_rms(inputs)
    normed_one = (inputs * inv_one * gain_one).astype(jnp.bfloat16)
    query_low = project(normed_one, query_w).astype(jnp.bfloat16)
    key_low = project(normed_one, key_w).astype(jnp.bfloat16)
    value_low = project(normed_one, value_w).astype(jnp.bfloat16)
    rim_pairs = from_behind(
        (key_low[row_count - WINDOW :], value_low[row_count - WINDOW :]), "seq", 1
    )
    keys_ext = jnp.concatenate([rim_pairs[0], key_low], axis=0).reshape(
        row_count + WINDOW, HEADS, HEAD_DIM
    )
    values_ext = jnp.concatenate([rim_pairs[1], value_low], axis=0).reshape(
        row_count + WINDOW, HEADS, HEAD_DIM
    )
    query_heads = query_low.reshape(row_count, HEADS, HEAD_DIM)
    span_start = lax.axis_index("seq") * row_count
    query_pos = span_start + jnp.arange(row_count, dtype=jnp.int32)
    key_pos = span_start - WINDOW + jnp.arange(row_count + WINDOW, dtype=jnp.int32)
    query_doc = doc_numbers(seq_lengths[0], query_pos)
    key_doc = doc_numbers(seq_lengths[0], key_pos)

    def tile_scores(row_start, head_start):
        visible = window_mask(query_pos, query_doc, key_pos, key_doc, WINDOW)
        scores_raw = (
            jnp.einsum(
                "qhd,khd->hqk",
                query_heads[
                    row_start : row_start + block_rows, head_start : head_start + head_group
                ],
                keys_ext[
                    row_start : row_start + block_rows + WINDOW,
                    head_start : head_start + head_group,
                ],
                preferred_element_type=jnp.float32,
            )
            * score_scale
        )
        return jnp.where(visible[None], scores_raw, -1e30)

    log_totals = {}
    row_start = 0
    head_parts = []
    for head_start in range(0, HEADS, head_group):
        masked_scores = tile_scores(row_start, head_start)
        top_score = jnp.max(masked_scores, axis=-1, keepdims=True)
        log_total = top_score + jnp.log(
            jnp.sum(jnp.exp(masked_scores - top_score), axis=-1, keepdims=True)
        )
        prob_low = jnp.exp(masked_scores - log_total).astype(jnp.bfloat16)
        value_tile = values_ext[
            row_start : row_start + block_rows + WINDOW, head_start : head_start + head_group
        ]
        head_parts.append(
            jnp.einsum("hqk,khd->qhd", prob_low, value_tile, preferred_element_type=jnp.float32)
        )
        log_totals[row_start, head_start] = log_total
    attn_blocks = jnp.concatenate(head_parts, axis=1)
    attended = attn_blocks.reshape(row_count, HEADS * HEAD_DIM).astype(jnp.bfloat16)
    middle = inputs + project(attended, out_w)
    inv_two = inverse_rms(middle)
    normed_two = (middle * inv_two * gain_two).astype(jnp.bfloat16)
    gate_pre = project(normed_two, gate_w)
    up_pre = project(normed_two, up_w)
    gate_act = jax.nn.silu(gate_pre)
    hidden = (gate_act * up_pre).astype(jnp.bfloat16)
    block_out = (middle + project(hidden, down_full)).astype(jnp.bfloat16)
    rows_again = (
        lax.all_gather(w_query, "dp", axis=0, tiled=True),
        lax.all_gather(w_key, "dp", axis=0, tiled=True),
        lax.all_gather(w_value, "dp", axis=0, tiled=True),
        lax.all_gather(w_out, "dp", axis=0, tiled=True),
        lax.all_gather(w_gate, "dp", axis=0, tiled=True),
        lax.all_gather(w_up, "dp", axis=0, tiled=True),
        lax.all_gather(w_down, "dp", axis=0, tiled=True),
        lax.all_gather(gain_attn, "dp", axis=0, tiled=True),
        lax.all_gather(gain_mlp, "dp", axis=0, tiled=True),
    )
    mats_again = (
        lax.all_gather(rows_again[0], "seq", axis=1, tiled=True),
        lax.all_gather(rows_again[1], "seq", axis=1, tiled=True),
        lax.all_gather(rows_again[2], "seq", axis=1, tiled=True),
        lax.all_gather(rows_again[3], "seq", axis=1, tiled=True),
        lax.all_gather(rows_again[4], "seq", axis=1, tiled=True),
        lax.all_gather(rows_again[5], "seq", axis=1, tiled=True),
        lax.all_gather(rows_again[6], "seq", axis=1, tiled=True),
    )
    back_query, back_key, back_value, back_out, back_gate, back_up, back_down = mats_again
    back_gain_one = rows_again[7].astype(jnp.float32)
    back_gain_two = rows_again[8].astype(jnp.float32)
    grad_final = cotangent.astype(jnp.float32)
    d_down = weight_grad(hidden, cotangent)
    grad_hidden = project_back(cotangent, back_down)
    sigmoid_gate = jax.nn.sigmoid(gate_pre)
    grad_gate_low = (
        grad_hidden * up_pre * sigmoid_gate * (1.0 + gate_pre * (1.0 - sigmoid_gate))
    ).astype(jnp.bfloat16)
    grad_up_low = (grad_hidden * gate_act).astype(jnp.bfloat16)
    d_gate = weight_grad(normed_two, grad_gate_low)
    d_up = weight_grad(normed_two, grad_up_low)
    grad_normed_two = project_back(grad_gate_low, back_gate) + project_back(grad_up_low, back_up)
    grad_mid_norm, d_gain_two = norm_back(middle, inv_two, back_gain_two, grad_normed_two)
    grad_middle = grad_final + grad_mid_norm
    grad_proj = grad_middle.astype(jnp.bfloat16)
    d_out = weight_grad(attended, grad_proj)
    grad_attended = (
        project_back(grad_proj, back_out).astype(jnp.bfloat16).reshape(row_count, HEADS, HEAD_DIM)
    )
    grad_keys_ext = jnp.zeros((row_count + WINDOW, HEADS, HEAD_DIM), jnp.float32)
    grad_values_ext = jnp.zeros((row_count + WINDOW, HEADS, HEAD_DIM), jnp.float32)
    row_start = 0
    head_parts = []
    for head_start in range(0, HEADS, head_group):
        head_end = head_start + head_group
        masked_scores = tile_scores(row_start, head_start)
        prob_full = jnp.exp(masked_scores - log_totals[row_start, head_start])
        grad_tile = grad_attended[row_start : row_start + block_rows, head_start:head_end]
        key_tile = keys_ext[row_start : row_start + block_rows + WINDOW, head_start:head_end]
        value_tile = values_ext[row_start : row_start + block_rows + WINDOW, head_start:head_end]
        query_tile = query_heads[row_start : row_start + block_rows, head_start:head_end]
        grad_prob = jnp.einsum(
            "qhd,khd->hqk", grad_tile, value_tile, preferred_element_type=jnp.float32
        )
        inner = jnp.sum(prob_full * grad_prob, axis=-1, keepdims=True)
        grad_score = (prob_full * (grad_prob - inner)).astype(jnp.bfloat16)
        head_parts.append(
            jnp.einsum("hqk,khd->qhd", grad_score, key_tile, preferred_element_type=jnp.float32)
            * score_scale
        )
        key_term = (
            jnp.einsum("hqk,qhd->khd", grad_score, query_tile, preferred_element_type=jnp.float32)
            * score_scale
        )
        value_term = jnp.einsum(
            "hqk,qhd->khd",
            prob_full.astype(jnp.bfloat16),
            grad_tile,
            preferred_element_type=jnp.float32,
        )
        grad_keys_ext = grad_keys_ext.at[
            row_start : row_start + block_rows + WINDOW, head_start:head_end
        ].add(key_term)
        grad_values_ext = grad_values_ext.at[
            row_start : row_start + block_rows + WINDOW, head_start:head_end
        ].add(value_term)
    grad_query_blocks = jnp.concatenate(head_parts, axis=1)
    rim_back = (
        from_behind(
            grad_keys_ext[:WINDOW].reshape(WINDOW, HEADS * HEAD_DIM).astype(jnp.bfloat16), "seq", -1
        ).astype(jnp.float32),
        from_behind(
            grad_values_ext[:WINDOW].reshape(WINDOW, HEADS * HEAD_DIM).astype(jnp.bfloat16),
            "seq",
            -1,
        ).astype(jnp.float32),
    )
    grad_keys = (
        grad_keys_ext[WINDOW:]
        .reshape(row_count, HEADS * HEAD_DIM)
        .at[row_count - WINDOW :]
        .add(rim_back[0])
    )
    grad_values = (
        grad_values_ext[WINDOW:]
        .reshape(row_count, HEADS * HEAD_DIM)
        .at[row_count - WINDOW :]
        .add(rim_back[1])
    )
    grad_query_low = grad_query_blocks.reshape(row_count, HEADS * HEAD_DIM).astype(jnp.bfloat16)
    grad_key_low = grad_keys.astype(jnp.bfloat16)
    grad_value_low = grad_values.astype(jnp.bfloat16)
    d_query = weight_grad(normed_one, grad_query_low)
    d_key = weight_grad(normed_one, grad_key_low)
    d_value = weight_grad(normed_one, grad_value_low)
    grad_normed_one = (
        project_back(grad_query_low, back_query)
        + project_back(grad_key_low, back_key)
        + project_back(grad_value_low, back_value)
    )
    grad_in_norm, d_gain_one = norm_back(inputs, inv_one, back_gain_one, grad_normed_one)
    grad_inputs = grad_middle + grad_in_norm
    row_sums = (
        lax.psum_scatter(
            d_query.astype(jnp.bfloat16), "dp", scatter_dimension=0, tiled=True
        ).astype(jnp.float32),
        lax.psum_scatter(d_key.astype(jnp.bfloat16), "dp", scatter_dimension=0, tiled=True).astype(
            jnp.float32
        ),
        lax.psum_scatter(
            d_value.astype(jnp.bfloat16), "dp", scatter_dimension=0, tiled=True
        ).astype(jnp.float32),
        lax.psum_scatter(d_out.astype(jnp.bfloat16), "dp", scatter_dimension=0, tiled=True).astype(
            jnp.float32
        ),
        lax.psum_scatter(d_gate.astype(jnp.bfloat16), "dp", scatter_dimension=0, tiled=True).astype(
            jnp.float32
        ),
        lax.psum_scatter(d_up.astype(jnp.bfloat16), "dp", scatter_dimension=0, tiled=True).astype(
            jnp.float32
        ),
        lax.psum_scatter(d_down.astype(jnp.bfloat16), "dp", scatter_dimension=0, tiled=True).astype(
            jnp.float32
        ),
        lax.psum_scatter(
            d_gain_one.astype(jnp.bfloat16), "dp", scatter_dimension=0, tiled=True
        ).astype(jnp.float32),
        lax.psum_scatter(
            d_gain_two.astype(jnp.bfloat16), "dp", scatter_dimension=0, tiled=True
        ).astype(jnp.float32),
    )
    owned_mats = (
        lax.psum_scatter(
            row_sums[0].astype(jnp.bfloat16), "seq", scatter_dimension=1, tiled=True
        ).astype(jnp.float32),
        lax.psum_scatter(
            row_sums[1].astype(jnp.bfloat16), "seq", scatter_dimension=1, tiled=True
        ).astype(jnp.float32),
        lax.psum_scatter(
            row_sums[2].astype(jnp.bfloat16), "seq", scatter_dimension=1, tiled=True
        ).astype(jnp.float32),
        lax.psum_scatter(
            row_sums[3].astype(jnp.bfloat16), "seq", scatter_dimension=1, tiled=True
        ).astype(jnp.float32),
        lax.psum_scatter(
            row_sums[4].astype(jnp.bfloat16), "seq", scatter_dimension=1, tiled=True
        ).astype(jnp.float32),
        lax.psum_scatter(
            row_sums[5].astype(jnp.bfloat16), "seq", scatter_dimension=1, tiled=True
        ).astype(jnp.float32),
        lax.psum_scatter(
            row_sums[6].astype(jnp.bfloat16), "seq", scatter_dimension=1, tiled=True
        ).astype(jnp.float32),
    )
    owned_gains = lax.psum((row_sums[7], row_sums[8]), "seq")
    return (
        block_out,
        grad_inputs,
        owned_mats[0],
        owned_mats[1],
        owned_mats[2],
        owned_mats[3],
        owned_mats[4],
        owned_mats[5],
        owned_mats[6],
        owned_gains[0],
        owned_gains[1],
    )


def solution(mesh):
    in_specs = (
        P(("dp", "seq"), None),
        P("dp", None),
        P("dp", "seq"),
        P("dp", "seq"),
        P("dp", "seq"),
        P("dp", "seq"),
        P("dp", "seq"),
        P("dp", "seq"),
        P("dp", "seq"),
        P("dp"),
        P("dp"),
        P(("dp", "seq"), None),
    )
    out_specs = (
        P(("dp", "seq"), None),
        P(("dp", "seq"), None),
        P("dp", "seq"),
        P("dp", "seq"),
        P("dp", "seq"),
        P("dp", "seq"),
        P("dp", "seq"),
        P("dp", "seq"),
        P("dp", "seq"),
        P("dp"),
        P("dp"),
    )
    return jax.shard_map(shards, mesh=mesh, in_specs=in_specs, out_specs=out_specs, check_vma=False)
```

profile of v0, /device:TPU:0, one launch (start us, length us, event | category | flops | bytes accessed | tf_op | source)
XLA Modules:
  0.0 1327.3 jit_solution(2838047656169959704)
XLA Ops:
  11.2 57.6 %all-gather.16.cloned.1.call-done = bf16[1024,512]{1,0:T(8,128)(2,1)} async-done(((bf16[64,512]{1,0:T(8,128)(2,1)}), bf16[1024,512]{1,0:T(8,128)(2,1)}) %all-gather.16.cloned.1.call-update) | async-done | bytes 1048592 | tf_op jit(solution)/shard_map/all_gather | solution.py:78
  68.8 56.8 %all-gather.20.cloned.1.call-done = bf16[1024,512]{1,0:T(8,128)(2,1)} async-done(((bf16[64,512]{1,0:T(8,128)(2,1)}), bf16[1024,512]{1,0:T(8,128)(2,1)}) %all-gather.20.cloned.1.call-update) | async-done | bytes 1048592 | tf_op jit(solution)/shard_map/all_gather | solution.py:76
  125.7 56.8 %all-gather.24.cloned.1.call-done = bf16[1024,512]{1,0:T(8,128)(2,1)} async-done(((bf16[64,512]{1,0:T(8,128)(2,1)}), bf16[1024,512]{1,0:T(8,128)(2,1)}) %all-gather.24.cloned.1.call-update) | async-done | bytes 1048592 | tf_op jit(solution)/shard_map/all_gather | solution.py:77
  183.2 56.1 %all-gather.28.cloned.1.call-done = bf16[1024,512]{1,0:T(8,128)(2,1)} async-done(((bf16[64,512]{1,0:T(8,128)(2,1)}), bf16[1024,512]{1,0:T(8,128)(2,1)}) %all-gather.28.cloned.1.call-update) | async-done | bytes 1048592 | tf_op jit(solution)/shard_map/all_gather | solution.py:79
  239.3 67.3 %all-gather.32.cloned.1.call-done = bf16[1024,1376]{1,0:T(8,128)(2,1)} async-done(((bf16[64,1376]{1,0:T(8,128)(2,1)}), bf16[1024,1376]{1,0:T(8,128)(2,1)}) %all-gather.32.cloned.1.call-update) | async-done | bytes 2818064 | tf_op jit(solution)/shard_map/all_gather | solution.py:80
  306.6 4.6 copy.44
  311.3 62.9 %all-gather.36.cloned.1.call-done = bf16[1024,1376]{1,0:T(8,128)(2,1)} async-done(((bf16[64,1376]{1,0:T(8,128)(2,1)}), bf16[1024,1376]{1,0:T(8,128)(2,1)}) %all-gather.36.cloned.1.call-update) | async-done | bytes 2818064 | tf_op jit(solution)/shard_map/all_gather | solution.py:81
  374.2 4.6 copy.45
  381.2 39.8 %all-reduce.8 = (bf16[1024]{0:T(1024)(128)(2,1)S(1)}, bf16[1024]{0:T(1024)(128)(2,1)S(1)}) all-reduce(bf16[1024]{0:T(1024)(128)(2,1)S(1)} %dynamic-update-slice.18, bf16[1024]{0:T(1024)(128)(2,1)S(1)} %dynamic-update-slice.19), channel_id=1, replica_groups=mesh['dp'=16,'seq'=2] {'dp'}, use_global_device_ids=true, to_apply=%add | all-reduce | flops 2048 | bytes 8192
  449.3 3.6 copy-done.1
  453.0 6.3 exponential_reduce_fusion.1
  459.3 22.5 %all-gather.42.cloned.1.call-done = bf16[16,172,512]{2,1,0:T(8,128)(2,1)} async-done(((bf16[1,172,512]{2,1,0:T(8,128)(2,1)}), bf16[16,172,512]{2,1,0:T(8,128)(2,1)}) %all-gather.42.cloned.1.call-update) | async-done | bytes 2818064 | tf_op jit(solution)/shard_map/all_gather | solution.py:82
  481.8 4.2 reshape.422
  486.3 6.4 exponential_reduce_fusion
  504.8 6.5 all-gather.34.cloned.1.call-done
  511.4 8.5 fusion.62
  519.8 10.1 all-gather.38.cloned.1.call-done
  529.9 8.7 fusion.63
  538.6 9.7 all-gather.40.cloned.1.call-done
  548.3 11.4 multiply_convert_fusion.2
  559.7 7.3 fusion.64
  577.0 6.5 fusion.25
  583.5 15.0 %multiply_reduce_fusion.1 = (f32[8,512]{1,0:T(8,128)S(1)}, f32[8,512]{1,0:T(8,128)S(1)}, f32[8,512,576]{1,2,0:T(8,128)}) fusion(f32[8,512,576]{1,2,0:T(8,128)} %copy-done.1, f32[8,512]{1,0:T(8,128)S(1)} %log_add_fusion.1, pred[512,576]{0,1:T(8,128)(4,1)S(1)} %and_and_fusion, f32[8,512,576]{1,2,0:T(8,128)} %fusion.25, f32[8,512]{1,0:T(8,128)S(1)} %log_add_fusion, ...), kind=kOutput, calls=%fused_computation.3 | convolution fusion | flops 325574656 | bytes 39813120 | tf_op jit(solution)/shard_map/qhd,khd->hqk/dot_general | solution.py:218
  598.5 14.1 %multiply_convert_fusion.1 = (bf16[8,512,576]{1,2,0:T(8,128)(2,1)}, bf16[8,512,576]{1,2,0:T(8,128)(2,1)S(1)}) fusion(f32[8,512,576]{1,2,0:T(8,128)} %get-tuple-element.117, f32[8,512,576]{1,2,0:T(8,128)} %copy-done.1, f32[8,512]{1,0:T(8,128)S(1)} %get-tuple-element.87, f32[8,512]{1,0:T(8,128)S(1)} %log_add_fusion.1, pred[512,576]{0,1:T(8,128)(4,1)S(1)} %and_and_fusion, ...), kind=kLoop, calls=%fused_computation.2 | loop fusion | flops 28311552 | bytes 47546368 | tf_op jit(solution)/shard_map/convert_element_type | solution.py:222
  621.5 4.5 convolution_convert_fusion.3
  626.1 4.1 fusion.18
  630.3 3.9 fusion.17
  641.9 4.0 convolution_convert_fusion.5
  646.0 6.3 convolution_bitcast_fusion.1
  652.3 6.0 convolution_bitcast_fusion
  665.0 4.0 convolution_convert_fusion.4
  669.1 7.8 convolution_convert_fusion.2
  677.2 7.8 convolution_convert_fusion.1
  685.1 7.6 convolution_convert_fusion
  692.7 215.0 %fusion = bf16[176,1024]{1,0:T(8,128)(2,1)S(1)} fusion(bf16[2752,1024]{1,0:T(8,128)(2,1)} %convolution_convert_fusion), kind=kCustom, calls=%all-reduce-scatter | all-reduce-scatter fusion | flops 2883585 | bytes 5997056
  914.3 4.3 concatenate.32
  922.8 7.6 add_convert_fusion
  930.4 53.0 %reduce-scatter.28.cloned.1.call-done = bf16[64,1024]{1,0:T(8,128)(2,1)} async-done(((bf16[1024,1024]{1,0:T(8,128)(2,1)}), bf16[64,1024]{1,0:T(8,128)(2,1)}) %reduce-scatter.28.cloned.1.call-update) | async-done | bytes 131088 | tf_op jit(solution)/shard_map/reduce_scatter | solution.py:286
  983.5 4.6 fusion.65
  988.1 121.5 %reduce-scatter.36.cloned.1.call-done = bf16[64,2752]{1,0:T(8,128)(2,1)} async-done(((bf16[1024,2752]{1,0:T(8,128)(2,1)}), bf16[64,2752]{1,0:T(8,128)(2,1)}) %reduce-scatter.36.cloned.1.call-update) | async-done | bytes 352272 | tf_op jit(solution)/shard_map/reduce_scatter | solution.py:292
  1118.4 41.8 %all-reduce.7 = (bf16[1024]{0:T(1024)(128)(2,1)S(1)}, bf16[1024]{0:T(1024)(128)(2,1)S(1)}) all-reduce(bf16[1024]{0:T(1024)(128)(2,1)S(1)} %get-tuple-element.85, bf16[1024]{0:T(1024)(128)(2,1)S(1)} %get-tuple-element.83), channel_id=16, replica_groups=mesh['dp'=16,'seq'=2] {'dp'}, use_global_device_ids=true, to_apply=%region_25.26.clone | all-reduce | flops 2048 | bytes 8192
  1160.4 79.8 %reduce-scatter.38.cloned.1.call-done = bf16[64,2752]{1,0:T(8,128)(2,1)} async-done(((bf16[1024,2752]{1,0:T(8,128)(2,1)}), bf16[64,2752]{1,0:T(8,128)(2,1)}) %reduce-scatter.38.cloned.1.call-update) | async-done | bytes 352272 | tf_op jit(solution)/shard_map/reduce_scatter | solution.py:295
  1253.3 9.2 reduce-scatter.22.cloned.1.call-done
  1264.0 9.4 reduce-scatter.34.cloned.1.call-done
  1274.9 9.2 reduce-scatter.26.cloned.1.call-done
  1285.7 9.4 reduce-scatter.30.cloned.1.call-done
  1296.6 10.0 reduce-scatter.42.cloned.1.call-done
  1308.5 9.6 reduce-scatter.44.cloned.1.call-done
  (220 shorter events, 120.7 us)
Async XLA Ops:
  7.2 61.6 %all-gather.16.cloned.1.call-start = ((), (), s32[]{:S(2)}) async-start(), calls=%async_computation.13 | async-start | bytes 1114112 | tf_op jit(solution)/shard_map/all_gather | solution.py:78
  7.9 117.7 %all-gather.20.cloned.1.call-start = ((), (), s32[]{:S(2)}) async-start(), calls=%async_computation.15 | async-start | bytes 1114112 | tf_op jit(solution)/shard_map/all_gather | solution.py:76
  8.7 173.9 %all-gather.24.cloned.1.call-start = ((), (), s32[]{:S(2)}) async-start(), calls=%async_computation.17 | async-start | bytes 1114112 | tf_op jit(solution)/shard_map/all_gather | solution.py:77
  9.4 229.8 %all-gather.28.cloned.1.call-start = ((), (), s32[]{:S(2)}) async-start(), calls=%async_computation.19 | async-start | bytes 1114112 | tf_op jit(solution)/shard_map/all_gather | solution.py:79
  10.0 296.6 %all-gather.32.cloned.1.call-start = ((), (), s32[]{:S(2)}) async-start(), calls=%async_computation.21 | async-start | bytes 3063808 | tf_op jit(solution)/shard_map/all_gather | solution.py:80
  10.6 363.6 %all-gather.36.cloned.1.call-start = ((), (), s32[]{:S(2)}) async-start(), calls=%async_computation.23 | async-start | bytes 3063808 | tf_op jit(solution)/shard_map/all_gather | solution.py:81
  11.1 414.5 %all-gather.18.cloned.1.call-start = ((), (), s32[]{:S(2)}) async-start(), calls=%async_computation.14 | async-start | bytes 3145728 | tf_op jit(solution)/shard_map/all_gather | solution.py:89
  68.8 363.3 %all-gather.22.cloned.1.call-start = ((), (), s32[]{:S(2)}) async-start(), calls=%async_computation.16 | async-start | bytes 3145728 | tf_op jit(solution)/shard_map/all_gather | solution.py:87
  125.7 309.3 %all-gather.26.cloned.1.call-start = ((), (), s32[]{:S(2)}) async-start(), calls=%async_computation.18 | async-start | bytes 3145728 | tf_op jit(solution)/shard_map/all_gather | solution.py:88
  182.5 299.2 %all-gather.42.cloned.1.call-start = ((), (), s32[]{:S(2)}) async-start(), calls=%async_computation.37 | async-start | bytes 3063808 | tf_op jit(solution)/shard_map/all_gather | solution.py:82
  183.1 316.9 %all-gather.30.cloned.1.call-start = ((), (), s32[]{:S(2)}) async-start(), calls=%async_computation.20 | async-start | bytes 3145728 | tf_op jit(solution)/shard_map/all_gather | solution.py:90
  239.3 272.1 %all-gather.34.cloned.1.call-start = ((), (), s32[]{:S(2)}) async-start(), calls=%async_computation.22 | async-start | bytes 8454144 | tf_op jit(solution)/shard_map/all_gather | solution.py:91
  311.2 218.7 %all-gather.38.cloned.1.call-start = ((), (), s32[]{:S(2)}) async-start(), calls=%async_computation.24 | async-start | bytes 8454144 | tf_op jit(solution)/shard_map/all_gather | solution.py:92
  378.8 42.2 %copy-start.27 = (s32[1,3]{1,0:T(1,128)S(1)}, s32[1,3]{1,0:T(1,128)}, u32[]{:S(2)}) copy-start(s32[1,3]{1,0:T(1,128)} %param.25) | copy-start | bytes 40
  378.8 45.5 %copy-start.2 = (bf16[512,1024]{1,0:T(8,128)(2,1)S(1)}, bf16[512,1024]{1,0:T(8,128)(2,1)}, u32[]{:S(2)}) copy-start(bf16[512,1024]{1,0:T(8,128)(2,1)} %param.24) | copy-start | bytes 3145732
  378.8 169.5 %all-gather.40.cloned.1.call-start = ((), (), s32[]{:S(2)}) async-start(), calls=%async_computation.25 | async-start | bytes 8454144 | tf_op jit(solution)/shard_map/all_gather | solution.py:93
  430.2 10.4 collective-permute-start
  439.3 4.2 collective-permute-start.1
  446.3 6.7 copy-start.23
  486.0 6.7 copy-start.12
  486.0 434.5 %reduce-scatter.20.cloned.1.call-start = ((), (), s32[]{:S(2)}) async-start(), calls=%async_computation.26 | async-start | bytes 2228224 | tf_op jit(solution)/shard_map/reduce_scatter | solution.py:280
  486.3 7.7 copy-start
  486.3 9.9 slice-start.3
  559.7 7.3 copy-start.30
  559.7 7.3 copy-start.8
  559.7 7.3 copy-start.3
  577.0 21.4 %slice-start = ((s8[9437184]{0:T(1024)(128)(4,1)}), s8[4194304]{0:T(1024)(128)(4,1)S(1)}, s32[]{:S(2)}) async-start(s8[9437184]{0:T(1024)(128)(4,1)} %bitcast.91), calls=%async_computation.40 | async-start | bytes 8388608
  583.4 15.0 %slice-start.1 = ((s8[9437184]{0:T(1024)(128)(4,1)}), s8[4194304]{0:T(1024)(128)(4,1)S(1)}, s32[]{:S(2)}) async-start(s8[9437184]{0:T(1024)(128)(4,1)} %bitcast.91), calls=%async_computation.41 | async-start | bytes 8388608
  583.5 15.0 %slice-start.2 = ((s8[9437184]{0:T(1024)(128)(4,1)}), s8[1048576]{0:T(1024)(128)(4,1)S(1)}, s32[]{:S(2)}) async-start(s8[9437184]{0:T(1024)(128)(4,1)} %bitcast.91), calls=%async_computation.42 | async-start | bytes 2097152
  598.4 14.1 %copy-start.19 = (bf16[576,1024]{0,1:T(8,128)(2,1)S(1)}, bf16[576,1024]{0,1:T(8,128)(2,1)}, u32[]{:S(2)}) copy-start(bf16[576,1024]{0,1:T(8,128)(2,1)} %copy.43) | copy-start | bytes 3538948
  621.5 299.8 %reduce-scatter.32.cloned.1.call-start = ((), (), s32[]{:S(2)}) async-start(), calls=%async_computation.32 | async-start | bytes 2228224 | tf_op jit(solution)/shard_map/reduce_scatter | solution.py:289
  626.1 296.6 %reduce-scatter.24.cloned.1.call-start = ((), (), s32[]{:S(2)}) async-start(), calls=%async_computation.28 | async-start | bytes 2228224 | tf_op jit(solution)/shard_map/reduce_scatter | solution.py:283
  634.2 3.4 collective-permute-start.2
  645.9 337.5 %reduce-scatter.28.cloned.1.call-start = ((), (), s32[]{:S(2)}) async-start(), calls=%async_computation.30 | async-start | bytes 2228224 | tf_op jit(solution)/shard_map/reduce_scatter | solution.py:286
  658.3 3.4 collective-permute-start.3
  669.1 440.6 %reduce-scatter.36.cloned.1.call-start = ((), (), s32[]{:S(2)}) async-start(), calls=%async_computation.34 | async-start | bytes 6127616 | tf_op jit(solution)/shard_map/reduce_scatter | solution.py:292
  676.9 563.2 %reduce-scatter.38.cloned.1.call-start = ((), (), s32[]{:S(2)}) async-start(), calls=%async_computation.35 | async-start | bytes 6127616 | tf_op jit(solution)/shard_map/reduce_scatter | solution.py:295
  685.1 566.5 %reduce-scatter.40.cloned.1.call-start = ((), (), s32[]{:S(2)}) async-start(), calls=%async_computation.36 | async-start | bytes 540672 | tf_op jit(solution)/shard_map/reduce_scatter | solution.py:327
  908.4 5.9 collective-permute-start.4
  920.5 342.0 %reduce-scatter.22.cloned.1.call-start = ((), (), s32[]{:S(2)}) async-start(), calls=%async_computation.27 | async-start | bytes 196608 | tf_op jit(solution)/shard_map/reduce_scatter | solution.py:309
  921.2 352.2 %reduce-scatter.34.cloned.1.call-start = ((), (), s32[]{:S(2)}) async-start(), calls=%async_computation.33 | async-start | bytes 196608 | tf_op jit(solution)/shard_map/reduce_scatter | solution.py:318
  922.0 362.2 %reduce-scatter.26.cloned.1.call-start = ((), (), s32[]{:S(2)}) async-start(), calls=%async_computation.29 | async-start | bytes 196608 | tf_op jit(solution)/shard_map/reduce_scatter | solution.py:312
  922.7 372.4 %reduce-scatter.30.cloned.1.call-start = ((), (), s32[]{:S(2)}) async-start(), calls=%async_computation.31 | async-start | bytes 196608 | tf_op jit(solution)/shard_map/reduce_scatter | solution.py:315
  983.4 128.7 %copy-start.21 = (bf16[512,1024]{0,1:T(8,128)(2,1)S(1)}, bf16[512,1024]{0,1:T(8,128)(2,1)}, u32[]{:S(2)}) copy-start(bf16[512,1024]{0,1:T(8,128)(2,1)} %scatter-add.15) | copy-start | bytes 3145732
  983.4 323.1 %reduce-scatter.42.cloned.1.call-start = ((), (), s32[]{:S(2)}) async-start(), calls=%async_computation.38 | async-start | bytes 1056768
  1111.8 206.3 %reduce-scatter.44.cloned.1.call-start = ((), (), s32[]{:S(2)}) async-start(), calls=%async_computation.39 | async-start | bytes 1056768
  1115.3 130.0 %copy-start.7 = (f32[512,1024]{1,0:T(8,128)S(1)}, f32[512,1024]{1,0:T(8,128)}, u32[]{:S(2)}) copy-start(f32[512,1024]{1,0:T(8,128)} %copy-done.6) | copy-start | bytes 6291460
  1115.3 130.0 %copy-start.25 = (f32[512]{0:T(512)S(1)}, f32[512]{0:T(512)}, u32[]{:S(2)}) copy-start(f32[512]{0:T(512)} %get-tuple-element.102) | copy-start | bytes 6148
  (21 other events, 64.4 us)
Sparse Core Ops, SparseCore 0:
  10.8 57.9 all-gather.15
  71.5 54.0 all-gather.19
  128.4 54.0 all-gather.23
  185.1 54.0 all-gather.27
  241.8 64.6 all-gather.31
  309.2 64.9 all-gather.35
  375.7 9.6 all-gather.17
  387.0 11.7 all-gather.21
  400.3 11.7 all-gather.25
  414.7 67.0 all-gather.41
  483.3 9.6 all-gather.29
  494.4 16.9 all-gather.33
  512.9 16.9 all-gather.37
  531.3 16.9 all-gather.39
  621.6 81.7 reduce-scatter.19
  705.6 95.7 reduce-scatter.31
  803.5 97.0 reduce-scatter.23
  902.7 80.6 reduce-scatter.27
  985.7 123.8 reduce-scatter.35
  1111.8 128.2 reduce-scatter.37
  1242.9 8.5 reduce-scatter.39
  1253.8 8.6 reduce-scatter.21
  1264.7 8.6 reduce-scatter.33
  1275.5 8.6 reduce-scatter.25
  1286.4 8.6 reduce-scatter.29
  1297.2 9.3 reduce-scatter.41
  1308.7 9.3 reduce-scatter.43
where the time goes:
time: 1340 us; the launch traced here: 1330 us
  waiting for transfers between devices  731 us (55%)
  blocking collectives  300 us (22%)
  matrix products  168 us (13%)
  local copies, waits for them, and re-layouts  54.9 us (4%)
  other arithmetic  45.3 us (3%)
  between operations  18.8 us (1%)
    unnamed x3, blocking collectives  297 us
    reduce_scatter x1, waiting for transfers between devices, shards(): lax.psum_scatter(d_gate.astype(jnp.bfloat16), 'dp', scatter_dimension=0,...  122 us
    reduce_scatter x1, waiting for transfers between devices, shards(): lax.psum_scatter(d_up.astype(jnp.bfloat16), 'dp', scatter_dimension=0, ti...  79.8 us
    all_gather x1, waiting for transfers between devices, shards(): lax.all_gather(w_gate, 'dp', axis=0, tiled=True)  67.3 us
    all_gather x1, waiting for transfers between devices, shards(): lax.all_gather(w_up, 'dp', axis=0, tiled=True)  62.9 us
    all_gather x1, waiting for transfers between devices, shards(): lax.all_gather(w_value, 'dp', axis=0, tiled=True)  57.6 us
    all_gather x1, waiting for transfers between devices, shards(): lax.all_gather(w_key, 'dp', axis=0, tiled=True)  56.8 us
    all_gather x1, waiting for transfers between devices, shards(): lax.all_gather(w_query, 'dp', axis=0, tiled=True)  56.8 us
  transfers between devices with their start and end apart: 32, of which 23 were waited for; matrix products, arithmetic and copies ran while one was open for 30% of the time, Pallas kernels for 0%

commit v1 on v0

--- a/solution.py
+++ b/solution.py
@@ -1,6 +1,10 @@
+import functools
+
 import jax
 import jax.numpy as jnp
 from jax import lax
+from jax.experimental import pallas as pl
+from jax.experimental.pallas import tpu as pltpu
 from jax.sharding import PartitionSpec as P
 
 HEADS = 16
@@ -54,7 +58,7 @@
     return jnp.einsum("td,tf->df", inputs, grad_rows, preferred_element_type=jnp.float32)
 
 
-def shards(
+def plain_block(
     tokens,
     seq_lengths,
     w_query,
@@ -344,7 +348,571 @@
     )
 
 
+MESH = pl.DeviceIdType.MESH
+NZ, NY, NX = 4, 2, 2
+SEQUENCE = {"zfx": "zxy", "zfy": "zyx", "zmx": "xzy", "zmy": "yzx"}
+ALL_Z, ALL_Y, ALL_X = pl.ds(0, NZ), pl.ds(0, NY), pl.ds(0, NX)
+
+
+class Plan:
+    def __init__(self, tensors):
+        self.tensors = tensors
+        self.items, self.of_tensor = [], []
+        for t, (rows, _, kind, splits, _) in enumerate(tensors):
+            begin, mine = 0, []
+            for half, count in enumerate(splits):
+                mine.append(len(self.items))
+                self.items.append((t, SEQUENCE[kind + "xy"[half]], begin, count))
+                begin += count
+            self.of_tensor.append(mine)
+
+
+class Place:
+    def __init__(self):
+        self.c, self.s = lax.axis_index("dp"), lax.axis_index("seq")
+        self.z, self.y, self.x = self.c // 4, (self.c // 2) % 2, self.c % 2
+
+    def at(self, z, y, x):
+        return (z * 4 + y * 2 + x, self.s)
+
+    def to_x(self):
+        return self.at(self.z, self.y, 1 - self.x)
+
+    def to_y(self):
+        return self.at(self.z, 1 - self.y, self.x)
+
+    def to_z(self, step):
+        return self.at((self.z + step) % NZ, self.y, self.x)
+
+    def to_core(self):
+        return (self.c, 1 - self.s)
+
+    def greet(self):
+        barrier = pltpu.get_barrier_semaphore()
+        peers = [self.to_x(), self.to_y(), self.to_core()] + [self.to_z(k) for k in (1, 2, 3)]
+        for peer in peers:
+            pl.semaphore_signal(barrier, inc=1, device_id=peer, device_id_type=MESH)
+        pl.semaphore_wait(barrier, len(peers))
+
+
+def remote(src, dst, send, recv, device):
+    return pltpu.make_async_remote_copy(
+        src_ref=src, dst_ref=dst, send_sem=send, recv_sem=recv, device_id=device, device_id_type=MESH
+    )
+
+
+class Gather:
+    def __init__(self, plan, place, shards, bufs, send, recv, local):
+        self.plan, self.me, self.shards, self.bufs = plan, place, shards, bufs
+        self.send, self.recv, self.local = send, recv, local
+
+    def own_copy(self, t):
+        me = self.me
+        return pltpu.make_async_copy(
+            self.shards[t], self.bufs[t].at[me.s, me.z, me.y, me.x], self.local.at[t]
+        )
+
+    def moves(self, i, phase):
+        t, seq, begin, count = self.plan.items[i]
+        me, buf = self.me, self.bufs[t]
+        rows = pl.ds(begin, count)
+
+        def view(z, y, x, half=me.s):
+            return buf.at[half, z, y, x, rows, :]
+
+        if phase == 3:
+            whole = view(ALL_Z, ALL_Y, ALL_X)
+            return [(whole, whole, me.to_core(), view(ALL_Z, ALL_Y, ALL_X, 1 - me.s), 0)]
+        done, axis = seq[:phase], seq[phase]
+        z = ALL_Z if "z" in done else me.z
+        y = ALL_Y if "y" in done else me.y
+        x = ALL_X if "x" in done else me.x
+        there = view(z, y, x)
+        here = self.shards[t].at[rows, :] if phase == 0 else there
+        if axis == "x":
+            return [(here, there, me.to_x(), view(z, y, 1 - me.x), 0)]
+        if axis == "y":
+            return [(here, there, me.to_y(), view(z, 1 - me.y, x), 0)]
+        return [
+            (here, there, me.to_z(k), view((me.z + NZ - k) % NZ, y, x), k - 1) for k in (1, 2, 3)
+        ]
+
+    def copy(self, i, phase, src, dst, device, k):
+        return remote(src, dst, self.send.at[i, phase, k], self.recv.at[i, phase, k], device)
+
+    def start(self, i, phase):
+        for here, there, device, _, k in self.moves(i, phase):
+            self.copy(i, phase, here, there, device, k).start()
+
+    def wait(self, i, phase):
+        for _, _, device, arrived, k in self.moves(i, phase):
+            self.copy(i, phase, arrived, arrived, device, k).wait_recv()
+
+    def finish(self, i):
+        for phase in range(4):
+            for here, there, device, _, k in self.moves(i, phase):
+                self.copy(i, phase, here, there, device, k).wait_send()
+
+
+def staged_order(tensors, lags):
+    order = []
+    for step in range(tensors + max(lags)):
+        for phase, lag in enumerate(lags):
+            if 0 <= step - lag < tensors:
+                order.append((step - lag, phase))
+    return order
+
+
+def got_shapes(plan):
+    shapes = []
+    for rows, columns, kind, _, dtype in plan.tensors:
+        second, third = ((1, NZ), (3,)) if kind == "zf" else ((3, 2), (1,))
+        shapes.append([(d + (rows, columns), dtype) for d in ((NZ, 2), second, third)])
+    return shapes
+
+
+class Scatter:
+    def __init__(self, plan, place, total, got, out, send, recv):
+        self.plan, self.me, self.total, self.got, self.out = plan, place, total, got, out
+        self.send, self.recv = send, recv
+
+    def moves(self, i, phase):
+        t, seq, begin, count = self.plan.items[i]
+        me, total, got = self.me, self.total[t], self.got[t][phase]
+        rows = pl.ds(begin, count)
+        axis, done = seq[2 - phase], seq[3 - phase :]
+        z = me.z if "z" in done else ALL_Z
+        y = me.y if "y" in done else ALL_Y
+        x = me.x if "x" in done else ALL_X
+        if phase == 0:
+            lands = [got.at[ALL_Z, pl.ds(0, 2), rows, :]]
+        elif phase == 1:
+            lands = [got.at[k, pl.ds(0, got.shape[1]), rows, :] for k in range(got.shape[0])]
+        else:
+            lands = [got.at[k, rows, :] for k in range(got.shape[0])]
+        if axis == "x":
+            return [(total.at[z, y, 1 - me.x, rows, :], lands[0], me.to_x(), 0)]
+        if axis == "y":
+            return [(total.at[z, 1 - me.y, x, rows, :], lands[0], me.to_y(), 0)]
+        return [
+            (total.at[(me.z + k) % NZ, y, x, rows, :], lands[k - 1], me.to_z(k), k - 1)
+            for k in (1, 2, 3)
+        ]
+
+    def copy(self, i, phase, src, dst, device, k):
+        return remote(src, dst, self.send.at[i, phase, k], self.recv.at[i, phase, k], device)
+
+    def start(self, i, phase):
+        for here, there, device, k in self.moves(i, phase):
+            self.copy(i, phase, here, there, device, k).start()
+
+    def wait(self, i, phase):
+        for here, there, device, k in self.moves(i, phase):
+            self.copy(i, phase, there, there, device, k).wait_recv()
+
+    def add(self, i, phase):
+        t, seq, begin, count = self.plan.items[i]
+        me, total, got = self.me, self.total[t], self.got[t][phase]
+        rows = pl.ds(begin, count)
+        if phase == 0:
+            for z in range(NZ):
+                for o in range(2):
+                    at = (z, me.y, o) if seq[2] == "y" else (z, o, me.x)
+                    total[at + (rows,)] += got[z, o, rows]
+        elif phase == 1 and seq[1] != "z":
+            for z in range(NZ):
+                total[z, me.y, me.x, rows] += got[0, z, rows]
+        elif phase == 1:
+            for o in range(2):
+                at = (me.z, me.y, o) if seq[2] == "y" else (me.z, o, me.x)
+                part = total[at + (rows,)].astype(jnp.float32)
+                for k in range(3):
+                    part += got[k, o, rows].astype(jnp.float32)
+                total[at + (rows,)] = part.astype(total.dtype)
+        else:
+            part = total[me.z, me.y, me.x, rows].astype(jnp.float32)
+            for k in range(got.shape[0]):
+                part += got[k, rows].astype(jnp.float32)
+            self.out[t][rows] = part
+
+    def finish(self, i):
+        for phase in range(3):
+            for here, there, device, k in self.moves(i, phase):
+                self.copy(i, phase, here, there, device, k).wait_send()
+
+
+def gather_kernel(plan, *refs):
+    n = len(plan.tensors)
+    shards, bufs = refs[:n], refs[n : 2 * n]
+    send, recv, local = refs[2 * n :]
+    me = Place()
+    me.greet()
+    gather = Gather(plan, me, shards, bufs, send, recv, local)
+    for t in range(n):
+        gather.own_copy(t).start()
+    for i in range(len(plan.items)):
+        gather.start(i, 0)
+    for t in range(n):
+        gather.own_copy(t).wait()
+    for t, phase in staged_order(n, (0, 2, 4)):
+        for i in plan.of_tensor[t]:
+            gather.wait(i, phase)
+            gather.start(i, phase + 1)
+    for i in range(len(plan.items)):
+        gather.wait(i, 3)
+    for i in range(len(plan.items)):
+        gather.finish(i)
+
+
+def gather_all(plan, shards):
+    n, k = len(plan.tensors), len(plan.items)
+    anywhere = pl.BlockSpec(memory_space=pl.ANY)
+    return pl.pallas_call(
+        functools.partial(gather_kernel, plan),
+        out_shape=[
+            jax.ShapeDtypeStruct((2, NZ, NY, NX) + t[:2], jnp.bfloat16) for t in plan.tensors
+        ],
+        in_specs=[anywhere] * n,
+        out_specs=[anywhere] * n,
+        scratch_shapes=[
+            pltpu.SemaphoreType.DMA((k, 4, 3)),
+            pltpu.SemaphoreType.DMA((k, 4, 3)),
+            pltpu.SemaphoreType.DMA((n,)),
+        ],
+        compiler_params=pltpu.CompilerParams(collective_id=0, has_side_effects=True),
+        name="gather_all",
+    )(*shards)
+
+
+def scatter_kernel(plan, *refs):
+    n = len(plan.tensors)
+    parts, outs, refs = refs[:n], refs[n : 2 * n], refs[2 * n :]
+    total, other, refs = refs[:n], refs[n : 2 * n], refs[2 * n :]
+    got, refs = [refs[3 * t : 3 * t + 3] for t in range(n)], refs[3 * n :]
+    send, recv, core_send, core_recv, local = refs
+    me = Place()
+    me.greet()
+    scatter = Scatter(plan, me, total, got, outs, send, recv)
+    own, across = [], []
+    for t in range(n):
+        across.append(
+            remote(parts[t].at[1 - me.s], other[t], core_send.at[t], core_recv.at[t], me.to_core())
+        )
+        across[t].start()
+        own.append(pltpu.make_async_copy(parts[t].at[me.s], total[t], local.at[t]))
+        own[t].start()
+    for t, step in staged_order(n, (0, 2, 4, 6)):
+        if step == 0:
+            own[t].wait()
+            across[t].wait_recv()
+
+            def add(j, _):
+                at = (j // (NY * NX), (j // NX) % NY, j % NX)
+                total[t][at] += other[t][at]
+                return 0
+
+            lax.fori_loop(0, NZ * NY * NX, add, 0)
+        for i in plan.of_tensor[t]:
+            if step:
+                scatter.wait(i, step - 1)
+                scatter.add(i, step - 1)
+            if step < 3:
+                scatter.start(i, step)
+    for i in range(len(plan.items)):
+        scatter.finish(i)
+    for t in range(n):
+        across[t].wait_send()
+
+
+def scatter_all(plan, parts):
+    n, k = len(plan.tensors), len(plan.items)
+    anywhere = pl.BlockSpec(memory_space=pl.ANY)
+    inside = pl.BlockSpec(memory_space=pltpu.VMEM)
+    halves = [pltpu.VMEM((NZ, NY, NX) + t[:2], t[4]) for t in plan.tensors]
+    got = [pltpu.VMEM(*shape) for shapes in got_shapes(plan) for shape in shapes]
+    return pl.pallas_call(
+        functools.partial(scatter_kernel, plan),
+        out_shape=[jax.ShapeDtypeStruct(t[:2], jnp.float32) for t in plan.tensors],
+        in_specs=[anywhere] * n,
+        out_specs=[inside] * n,
+        scratch_shapes=halves
+        + halves
+        + got
+        + [
+            pltpu.SemaphoreType.DMA((k, 3, 3)),
+            pltpu.SemaphoreType.DMA((k, 3, 3)),
+            pltpu.SemaphoreType.DMA((n,)),
+            pltpu.SemaphoreType.DMA((n,)),
+            pltpu.SemaphoreType.DMA((n,)),
+        ],
+        compiler_params=pltpu.CompilerParams(
+            collective_id=1, has_side_effects=True, vmem_limit_bytes=60 * 2**20
+        ),
+        name="scatter_all",
+    )(*parts)
+
+
+def swift_block(
+    tokens,
+    seq_lengths,
+    w_query,
+    w_key,
+    w_value,
+    w_out,
+    w_gate,
+    w_up,
+    w_down,
+    gain_attn,
+    gain_mlp,
+    cotangent,
+):
+    row_count, width = tokens.shape
+    chips = NZ * NY * NX
+    rows, columns = w_query.shape
+    ff_part = w_down.shape[0]
+    ff_tile = -(-ff_part // 16) * 16
+    wide = w_gate.shape[1] // ff_part * ff_tile
+    low = jnp.bfloat16
+    square = (rows, columns, "zf", (rows // 2, rows // 2), low)
+    square_m = (rows, columns, "zm", (rows // 2, rows // 2), low)
+    broad = (rows, wide, "zf", (rows // 2, rows // 2), low)
+    first = ff_tile // 32 * 16 + 16 * (ff_tile // 16 % 2)
+    tall = (ff_tile, columns, "zm", (first, ff_tile - first), low)
+    place = lax.axis_index("dp")
+
+    def pad_columns(w):
+        return jnp.pad(w.reshape(rows, -1, ff_part), ((0, 0), (0, 0), (0, ff_tile - ff_part))).reshape(rows, wide)
+
+    def unpad_columns(w):
+        return w.reshape(rows, -1, ff_tile)[:, :, :ff_part].reshape(rows, -1)
+
+    pair = jnp.zeros((2, 16, 2 * rows), low).at[0, 0:2, :rows].set(jnp.stack([gain_attn, gain_mlp]))
+    pair = pair.at[1, 0:2, rows:].set(jnp.stack([gain_attn, gain_mlp]))[place % 2]
+    plan = Plan([(16, 2 * rows, "zf", (16,), low), square, square, square_m, square, broad, broad, tall])
+    bufs = gather_all(
+        plan,
+        [pair, w_query, w_key, w_value, w_out, pad_columns(w_gate), pad_columns(w_up), jnp.pad(w_down, ((0, ff_tile - ff_part), (0, 0)))],
+    )
+    gains = bufs[0][0, ..., 0:2, :].reshape(chips // 2, 2, 2, 2 * rows).sum(1).transpose(1, 0, 2).reshape(2, width)
+    gain_one, gain_two = gains[0].astype(jnp.float32), gains[1].astype(jnp.float32)
+    query_w, key_w, value_w, out_w, gate_w, up_w, down_full = [
+        b.reshape(2, -1, b.shape[-1]).transpose(1, 0, 2).reshape(b.shape[-2] * chips, -1) for b in bufs[1:]
+    ]
+    outs = compute_block(
+        tokens, seq_lengths, query_w, key_w, value_w, out_w, gate_w, up_w, down_full, gain_one, gain_two, cotangent
+    )
+    block_out, grad_inputs, d_query, d_key, d_value, d_out, d_gate, d_up, d_down, d_gain_one, d_gain_two = outs
+
+    def halves(d):
+        d = d.astype(low)
+        return d.reshape(d.shape[0], 2, -1).transpose(1, 0, 2).reshape(2, NZ, NY, NX, d.shape[0] // chips, -1)
+
+    d_gains = jnp.stack([d_gain_one, d_gain_two]).reshape(2, chips // 2, 1, 2 * rows)
+    d_gains = jnp.broadcast_to(d_gains, (2, chips // 2, 2, 2 * rows)).reshape(2, chips, 2 * rows).transpose(1, 0, 2)
+    d_gains = jnp.pad(d_gains, ((0, 0), (0, 6), (0, 0))).reshape(1, NZ, NY, NX, 8, 2 * rows)
+    d_gains = jnp.concatenate([d_gains, d_gains], axis=0)
+    plan_back = Plan([tall, broad, broad, square, square, square, square_m, (8, 2 * rows, "zf", (8,), jnp.float32)])
+    sums = scatter_all(
+        plan_back, [halves(d) for d in (d_down, d_up, d_gate, d_out, d_query, d_key, d_value)] + [d_gains]
+    )
+    own = lax.dynamic_slice_in_dim(sums[7], (place % 2) * rows, rows, 1)
+    return (
+        block_out,
+        grad_inputs,
+        sums[4],
+        sums[5],
+        sums[6],
+        sums[3],
+        unpad_columns(sums[2]),
+        unpad_columns(sums[1]),
+        sums[0][:ff_part],
+        own[0],
+        own[1],
+    )
+
+
+def compute_block(
+    tokens,
+    seq_lengths,
+    query_w,
+    key_w,
+    value_w,
+    out_w,
+    gate_w,
+    up_w,
+    down_full,
+    gain_one,
+    gain_two,
+    cotangent,
+):
+    row_count = tokens.shape[0]
+    block_rows = min(512, row_count)
+    head_group = HEADS // 2
+    score_scale = HEAD_DIM ** (-0.5)
+    inputs = tokens.astype(jnp.float32)
+    inv_one = inverse_rms(inputs)
+    normed_one = (inputs * inv_one * gain_one).astype(jnp.bfloat16)
+    query_low = project(normed_one, query_w).astype(jnp.bfloat16)
+    key_low = project(normed_one, key_w).astype(jnp.bfloat16)
+    value_low = project(normed_one, value_w).astype(jnp.bfloat16)
+    rim_pairs = from_behind(
+        (key_low[row_count - WINDOW :], value_low[row_count - WINDOW :]), "seq", 1
+    )
+    keys_ext = jnp.concatenate([rim_pairs[0], key_low], axis=0).reshape(
+        row_count + WINDOW, HEADS, HEAD_DIM
+    )
+    values_ext = jnp.concatenate([rim_pairs[1], value_low], axis=0).reshape(
+        row_count + WINDOW, HEADS, HEAD_DIM
+    )
+    query_heads = query_low.reshape(row_count, HEADS, HEAD_DIM)
+    span_start = lax.axis_index("seq") * row_count
+    query_pos = span_start + jnp.arange(row_count, dtype=jnp.int32)
+    key_pos = span_start - WINDOW + jnp.arange(row_count + WINDOW, dtype=jnp.int32)
+    query_doc = doc_numbers(seq_lengths[0], query_pos)
+    key_doc = doc_numbers(seq_lengths[0], key_pos)
+
+    def tile_scores(row_start, head_start):
+        visible = window_mask(query_pos, query_doc, key_pos, key_doc, WINDOW)
+        scores_raw = (
+            jnp.einsum(
+                "qhd,khd->hqk",
+                query_heads[
+                    row_start : row_start + block_rows, head_start : head_start + head_group
+                ],
+                keys_ext[
+                    row_start : row_start + block_rows + WINDOW,
+                    head_start : head_start + head_group,
+                ],
+                preferred_element_type=jnp.float32,
+            )
+            * score_scale
+        )
+        return jnp.where(visible[None], scores_raw, -1e30)
+
+    log_totals = {}
+    row_start = 0
+    head_parts = []
+    for head_start in range(0, HEADS, head_group):
+        masked_scores = tile_scores(row_start, head_start)
+        top_score = jnp.max(masked_scores, axis=-1, keepdims=True)
+        log_total = top_score + jnp.log(
+            jnp.sum(jnp.exp(masked_scores - top_score), axis=-1, keepdims=True)
+        )
+        prob_low = jnp.exp(masked_scores - log_total).astype(jnp.bfloat16)
+        value_tile = values_ext[
+            row_start : row_start + block_rows + WINDOW, head_start : head_start + head_group
+        ]
+        head_parts.append(
+            jnp.einsum("hqk,khd->qhd", prob_low, value_tile, preferred_element_type=jnp.float32)
+        )
+        log_totals[row_start, head_start] = log_total
+    attn_blocks = jnp.concatenate(head_parts, axis=1)
+    attended = attn_blocks.reshape(row_count, HEADS * HEAD_DIM).astype(jnp.bfloat16)
+    middle = inputs + project(attended, out_w)
+    inv_two = inverse_rms(middle)
+    normed_two = (middle * inv_two * gain_two).astype(jnp.bfloat16)
+    gate_pre = project(normed_two, gate_w)
+    up_pre = project(normed_two, up_w)
+    gate_act = jax.nn.silu(gate_pre)
+    hidden = (gate_act * up_pre).astype(jnp.bfloat16)
+    block_out = (middle + project(hidden, down_full)).astype(jnp.bfloat16)
+    grad_final = cotangent.astype(jnp.float32)
+    d_down = weight_grad(hidden, cotangent)
+    grad_hidden = project_back(cotangent, down_full)
+    sigmoid_gate = jax.nn.sigmoid(gate_pre)
+    grad_gate_low = (
+        grad_hidden * up_pre * sigmoid_gate * (1.0 + gate_pre * (1.0 - sigmoid_gate))
+    ).astype(jnp.bfloat16)
+    grad_up_low = (grad_hidden * gate_act).astype(jnp.bfloat16)
+    d_gate = weight_grad(normed_two, grad_gate_low)
+    d_up = weight_grad(normed_two, grad_up_low)
+    grad_normed_two = project_back(grad_gate_low, gate_w) + project_back(grad_up_low, up_w)
+    grad_mid_norm, d_gain_two = norm_back(middle, inv_two, gain_two, grad_normed_two)
+    grad_middle = grad_final + grad_mid_norm
+    grad_proj = grad_middle.astype(jnp.bfloat16)
+    d_out = weight_grad(attended, grad_proj)
+    grad_attended = (
+        project_back(grad_proj, out_w).astype(jnp.bfloat16).reshape(row_count, HEADS, HEAD_DIM)
+    )
+    grad_keys_ext = jnp.zeros((row_count + WINDOW, HEADS, HEAD_DIM), jnp.float32)
+    grad_values_ext = jnp.zeros((row_count + WINDOW, HEADS, HEAD_DIM), jnp.float32)
+    row_start = 0
+    head_parts = []
+    for head_start in range(0, HEADS, head_group):
+        head_end = head_start + head_group
+        masked_scores = tile_scores(row_start, head_start)
+        prob_full = jnp.exp(masked_scores - log_totals[row_start, head_start])
+        grad_tile = grad_attended[row_start : row_start + block_rows, head_start:head_end]
+        key_tile = keys_ext[row_start : row_start + block_rows + WINDOW, head_start:head_end]
+        value_tile = values_ext[row_start : row_start + block_rows + WINDOW, head_start:head_end]
+        query_tile = query_heads[row_start : row_start + block_rows, head_start:head_end]
+        grad_prob = jnp.einsum(
+            "qhd,khd->hqk", grad_tile, value_tile, preferred_element_type=jnp.float32
+        )
+        inner = jnp.sum(prob_full * grad_prob, axis=-1, keepdims=True)
+        grad_score = (prob_full * (grad_prob - inner)).astype(jnp.bfloat16)
+        head_parts.append(
+            jnp.einsum("hqk,khd->qhd", grad_score, key_tile, preferred_element_type=jnp.float32)
+            * score_scale
+        )
+        key_term = (
+            jnp.einsum("hqk,qhd->khd", grad_score, query_tile, preferred_element_type=jnp.float32)
+            * score_scale
+        )
+        value_term = jnp.einsum(
+            "hqk,qhd->khd",
+            prob_full.astype(jnp.bfloat16),
+            grad_tile,
+            preferred_element_type=jnp.float32,
+        )
+        grad_keys_ext = grad_keys_ext.at[
+            row_start : row_start + block_rows + WINDOW, head_start:head_end
+        ].add(key_term)
+        grad_values_ext = grad_values_ext.at[
+            row_start : row_start + block_rows + WINDOW, head_start:head_end
+        ].add(value_term)
+    grad_query_blocks = jnp.concatenate(head_parts, axis=1)
+    rim_back = (
+        from_behind(
+            grad_keys_ext[:WINDOW].reshape(WINDOW, HEADS * HEAD_DIM).astype(jnp.bfloat16), "seq", -1
+        ).astype(jnp.float32),
+        from_behind(
+            grad_values_ext[:WINDOW].reshape(WINDOW, HEADS * HEAD_DIM).astype(jnp.bfloat16),
+            "seq",
+            -1,
+        ).astype(jnp.float32),
+    )
+    grad_keys = (
+        grad_keys_ext[WINDOW:]
+        .reshape(row_count, HEADS * HEAD_DIM)
+        .at[row_count - WINDOW :]
+        .add(rim_back[0])
+    )
+    grad_values = (
+        grad_values_ext[WINDOW:]
+        .reshape(row_count, HEADS * HEAD_DIM)
+        .at[row_count - WINDOW :]
+        .add(rim_back[1])
+    )
+    grad_query_low = grad_query_blocks.reshape(row_count, HEADS * HEAD_DIM).astype(jnp.bfloat16)
+    grad_key_low = grad_keys.astype(jnp.bfloat16)
+    grad_value_low = grad_values.astype(jnp.bfloat16)
+    d_query = weight_grad(normed_one, grad_query_low)
+    d_key = weight_grad(normed_one, grad_key_low)
+    d_value = weight_grad(normed_one, grad_value_low)
+    grad_normed_one = (
+        project_back(grad_query_low, query_w)
+        + project_back(grad_key_low, key_w)
+        + project_back(grad_value_low, value_w)
+    )
+    grad_in_norm, d_gain_one = norm_back(inputs, inv_one, gain_one, grad_normed_one)
+    grad_inputs = grad_middle + grad_in_norm
+    return (block_out, grad_inputs, d_query, d_key, d_value, d_out, d_gate, d_up, d_down, d_gain_one, d_gain_two)
+
+
 def solution(mesh):
+    fast = (mesh.shape["dp"], mesh.shape["seq"]) == (NZ * NY * NX, 2)
+    shards = swift_block if fast else plain_block
     in_specs = (
         P(("dp", "seq"), None),
         P("dp", None),

time: 1340 us -> 580 us (0.43)
  waiting for transfers between devices: 731 us -> 0.01 us
  blocking collectives: 300 us -> 0 us
  Pallas kernels: 0 us -> 275 us
  local copies, waits for them, and re-layouts: 54.9 us -> 115 us
  matrix products: 168 us -> 126 us
  between operations: 18.8 us -> 3.37 us
    all_gather x14 -> x0, waiting for transfers between devices: 406 us -> none  [the longest x1 67.3 us: shards(): lax.all_gather(w_gate, 'dp', axis=0, tiled=True)]
    unnamed x3 -> x0, blocking collectives: 297 us -> none
    reduce_scatter x11 -> x0, waiting for transfers between devices: 294 us -> none  [the longest x1 122 us: shards(): lax.psum_scatter(d_gate.astype(jnp.bfloat16), 'dp', scatter_dimension=0,...]
    pallas_call x0 -> x2, Pallas kernels: none -> 275 us  [the longest x1 138 us: gather_all(): pl.pallas_call(functools.partial(gather_kernel, plan), out_shape=[jax.Sha...]
    reshape x0 -> x22, local copies, waits for them, and re-layouts: none -> 84.8 us  [the longest x7 37.8 us: swift_block(): b.reshape(2, -1, b.shape[-1]).transpose(1, 0, 2)]
    unnamed x30 -> x0, waiting for transfers between devices: 28.7 us -> none
    unnamed x87 -> x141, local copies, waits for them, and re-layouts: 31.1 us -> 14 us
    dot_general x7, matrix products: 37 us -> 20.4 us  [project(): return jnp.dot(left, right, preferred_element_type=jnp.float32)]
  transfers between devices with their start and end apart: 32 -> 4, of which waited for: 23 -> 0; matrix products, arithmetic and copies ran while one was open for 30% -> 15% of each run, Pallas kernels for 0% -> 0%
where the time goes in v1:
time: 580 us; the launch traced here: 570 us
  Pallas kernels  275 us (47%)
  matrix products  126 us (22%)
  local copies, waits for them, and re-layouts  115 us (20%)
  other arithmetic  44 us (8%)
  starting transfers between devices  6.91 us (1%)
    pallas_call x1, Pallas kernels, gather_all(): pl.pallas_call(functools.partial(gather_kernel, plan), out_shape=[jax.Sha...  138 us
    pallas_call x1, Pallas kernels, scatter_all(): pl.pallas_call(functools.partial(scatter_kernel, plan), out_shape=[jax.Sh...  137 us
    reshape x7, local copies, waits for them, and re-layouts, swift_block(): b.reshape(2, -1, b.shape[-1]).transpose(1, 0, 2)  37.8 us
    reshape x7, local copies, waits for them, and re-layouts, halves(): d.reshape(d.shape[0], 2, -1).transpose(1, 0, 2)  34 us
    dot_general x7, matrix products, project_back(): jnp.einsum('tf,df->td', grad_rows, weight, preferred_element_type=jnp.flo...  29.9 us
    dot_general x7, matrix products, weight_grad(): jnp.einsum('td,tf->df', inputs, grad_rows, preferred_element_type=jnp.flo...  27.4 us
    dot_general x7, matrix products, project(): return jnp.dot(left, right, preferred_element_type=jnp.float32)  20.4 us
    dot_general x2, matrix products, compute_block(): jnp.einsum('qhd,khd->hqk', grad_tile, value_tile, preferred_element_type=...  16.9 us
  transfers between devices with their start and end apart: 4, of which 0 were waited for; matrix products, arithmetic and copies ran while one was open for 15% of the time, Pallas kernels for 0%

profile of v1, /device:TPU:0, one launch (start us, length us, event | category | flops | bytes accessed | tf_op | source)
XLA Modules:
  0.0 570.0 jit_solution(17341245578544075349)
XLA Ops:
  7.2 138.3 %gather_all.1 = (bf16[2,4,2,2,16,128]{5,4,3,2,1,0:T(8,128)(2,1)}, bf16[2,4,2,2,64,512]{5,4,3,2,1,0:T(8,128)(2,1)}, bf16[2,4,2,2,64,512]{5,4,3,2,1,0:T(8,128)(2,1...) custom-call(bf16[16,128]{1,0:T(8,128)(2,1)} %dynamic-slice_bitcast_f, ...), custom_call_target="tpu_custom_call" | custom-call | tf_op jit(solution)/shard_map/gather_all/pallas_call | solution.py:570
  145.6 3.0 copy.39
  152.4 3.1 collective-permute-start
  155.4 3.0 copy.43
  165.4 3.0 copy.41
  168.4 2.3 convolution_convert_fusion.9
  170.7 2.3 copy.42
  173.0 3.9 copy.45
  176.9 8.4 %copy.46 = bf16[2,1024,1408]{1,2,0:T(8,128)(2,1)} copy(bf16[2,1024,1408]{2,1,0:T(8,128)(2,1)} %bitcast.216) | data formatting | bytes 11534336 | tf_op jit(solution)/shard_map/reshape | solution.py:699
  185.3 8.2 %copy.47 = bf16[2,1024,1408]{1,2,0:T(8,128)(2,1)} copy(bf16[2,1024,1408]{2,1,0:T(8,128)(2,1)} %bitcast.215) | data formatting | bytes 11534336 | tf_op jit(solution)/shard_map/reshape | solution.py:699
  193.5 8.3 %copy.48 = bf16[2,2816,512]{1,2,0:T(8,128)(2,1)} copy(bf16[2,2816,512]{2,1,0:T(8,128)(2,1)} %bitcast.214) | data formatting | bytes 11534336 | tf_op jit(solution)/shard_map/reshape | solution.py:699
  208.1 3.0 fusion
  211.2 3.8 exponential_reduce_fusion.1
  221.0 2.3 convolution_bitcast_fusion.3
  223.2 9.6 %maximum_convert_fusion = bf16[512,16,64]{0,2,1:T(8,128)(2,1)S(1)} fusion(bf16[512,8,64]{0,2,1:T(8,128)(2,1)S(1)} %convolution_bitcast_fusion.2, bf16[512,8,64]{0,2,1:T(8,128)(2,1)S(1)} %convolution_bitcast_fusion.3), kind=kLoop, calls=%fused_computation.52 | loop fusion | flops 524288 | bytes 2097152 | tf_op jit(solution)/shard_map/convert_element_type | solution.py:810
  237.1 5.0 fusion.69
  242.2 5.0 fusion.70
  247.2 10.1 %fusion.5 = (bf16[512,2816]{1,0:T(8,128)(2,1)}, bf16[512,2816]{1,0:T(8,128)(2,1)}, bf16[512,2816]{1,0:T(8,128)(2,1)}) fusion(f32[512,2816]{1,0:T(8,128)} %fusion.69, f32[512,2816]{1,0:T(8,128)} %fusion.70, bf16[512,1024]{1,0:T(8,128)(2,1)S(1)} %copy-done.29, bf16[2816,1024]{0,1:T(8,128)(2,1)S(1)} %bitcast.202), kind=kOutput, calls=%fused_computation.19 | convolution fusion | flops 2974416896 | bytes 27000832 | tf_op jit(solution)/shard_map/tf,df->td/dot_general | solution.py:54
  257.3 5.1 fusion.71
  262.4 3.5 multiply_reduce_fusion.2
  270.0 5.9 %convolution_bitcast_fusion.1 = f32[576,8,64]{0,2,1:T(8,128)S(1)} fusion(bf16[512,16,64]{0,2,1:T(8,128)(2,1)S(1)} %bitcast.188, f32[8,512,576]{1,2,0:T(8,128)} %copy-done.1, f32[8,512]{1,0:T(8,128)S(1)} %log_add_fusion.1, pred[512,576]{0,1:T(8,128)(4,1)S(1)} %and_and_fusion), kind=kOutput, calls=%fused_computation.75 | convolution fusion | flops 311427072 | bytes 11976704 | tf_op jit(solution)/shard_map/hqk,qhd->khd/dot_general | solution.py:862
  276.0 6.1 %convolution_bitcast_fusion = f32[576,8,64]{0,2,1:T(8,128)S(1)} fusion(bf16[512,16,64]{0,2,1:T(8,128)(2,1)S(1)} %bitcast.189, f32[8,512,576]{1,2,0:T(8,128)} %copy-done, f32[8,512]{1,0:T(8,128)S(1)} %log_add_fusion, pred[512,576]{0,1:T(8,128)(4,1)S(1)} %and_and_fusion), kind=kOutput, calls=%fused_computation.74 | convolution fusion | flops 311427072 | bytes 11976704 | tf_op jit(solution)/shard_map/hqk,qhd->khd/dot_general | solution.py:862
  284.9 5.0 fusion.24
  290.0 11.9 %multiply_reduce_fusion.1 = (f32[8,512]{1,0:T(8,128)S(1)}, f32[8,512]{1,0:T(8,128)S(1)}, f32[8,512,576]{1,2,0:T(8,128)}) fusion(f32[8,512,576]{1,2,0:T(8,128)} %copy-done.1, f32[8,512]{1,0:T(8,128)S(1)} %log_add_fusion.1, pred[512,576]{0,1:T(8,128)(4,1)S(1)} %and_and_fusion, f32[8,512,576]{1,2,0:T(8,128)} %fusion.24, f32[8,512]{1,0:T(8,128)S(1)} %log_add_fusion, ...), kind=kOutput, calls=%fused_computation.3 | convolution fusion | flops 325574656 | bytes 39813120 | tf_op jit(solution)/shard_map/qhd,khd->hqk/dot_general | solution.py:849
  301.9 14.1 %multiply_convert_fusion.1 = (bf16[8,512,576]{1,2,0:T(8,128)(2,1)}, bf16[8,512,576]{1,2,0:T(8,128)(2,1)S(1)}) fusion(f32[8,512,576]{1,2,0:T(8,128)} %get-tuple-element.168, f32[8,512,576]{1,2,0:T(8,128)} %copy-done.1, f32[8,512]{1,0:T(8,128)S(1)} %get-tuple-element.143, f32[8,512]{1,0:T(8,128)S(1)} %log_add_fusion.1, pred[512,576]{0,1:T(8,128)(4,1)S(1)} %and_and_fusion, ...), kind=kLoop, calls=%fused_computation.2 | loop fusion | flops 28311552 | bytes 47546368 | tf_op jit(solution)/shard_map/convert_element_type | solution.py:853
  316.0 3.6 fusion.23
  327.4 4.1 add_convert_fusion
  331.5 5.1 convolution_convert_fusion.2
  336.6 5.1 convolution_convert_fusion.1
  341.7 5.1 convolution_convert_fusion
  346.8 2.7 convolution_convert_fusion.6
  351.1 2.6 fusion.72
  353.7 2.7 convolution_convert_fusion.5
  359.7 8.6 %copy.51 = bf16[2816,2,512]{2,0,1:T(8,128)(2,1)} copy(bf16[2816,2,512]{0,2,1:T(8,128)(2,1)} %bitcast.217) | data formatting | bytes 11534336 | tf_op jit(solution)/shard_map/reshape | solution.py:708
  368.3 5.5 copy.64
  373.8 5.5 copy.63
  379.3 3.9 copy.54
  383.2 4.0 copy.55
  391.1 4.3 fusion.73
  395.4 2.8 convolution_convert_fusion.4
  399.2 3.2 scatter-add.19
  402.5 4.0 convolution_convert_fusion.3
  406.5 3.0 fusion.12
  409.6 2.5 copy.56
  412.1 3.9 copy.57
  416.8 136.7 %scatter_all.1 = (f32[176,512]{1,0:T(8,128)}, f32[64,1408]{1,0:T(8,128)}, f32[64,1408]{1,0:T(8,128)}, f32[64,512]{1,0:T(8,128)}, f32[64,512]{1,0:T(8,128)}, /*in...) custom-call(bf16[2,4,2,2,176,512]{5,4,3,2,1,0:T(8,128)(2,1)} %bitcast.185, ...), custom_call_target="tpu_custom_call" | custom-call | tf_op jit(solution)/shard_map/scatter_all/pallas_call | solution.py:633
  553.5 2.3 reshape.672
  562.6 3.5 fusion.18
  (216 shorter events, 67.4 us)
Async XLA Ops:
  0.6 4.7 copy-start.39
  0.7 5.4 copy-start.51
  0.7 5.4 copy-start.52
  7.2 142.2 %copy-start.12 = (bf16[512,1024]{1,0:T(8,128)(2,1)S(1)}, bf16[512,1024]{1,0:T(8,128)(2,1)}, u32[]{:S(2)}) copy-start(bf16[512,1024]{1,0:T(8,128)(2,1)} %param.28) | copy-start | bytes 3145732
  149.4 19.0 %copy-start.44 = (f32[1,8,128]{2,0,1:T(1,128)}, f32[1,8,128]{2,0,1:T(1,128)S(1)}, u32[]{:S(2)}) copy-start(f32[1,8,128]{2,0,1:T(1,128)S(1)} %get-tuple-element.155) | copy-start | bytes 12292
  150.3 18.1 %copy-start.47 = (f32[512]{0:T(512)}, f32[512]{0:T(512)S(1)}, u32[]{:S(2)}) copy-start(f32[512]{0:T(512)S(1)} %get-tuple-element.157) | copy-start | bytes 6148
  151.6 3.8 copy-start.26
  152.4 49.9 %collective-permute-start = (bf16[64,1024]{1,0:T(8,128)(2,1)}, bf16[64,1024]{1,0:T(8,128)(2,1)}, u32[]{:S(2)}, u32[]{:S(2)}) collective-permute-start(bf16[64,1024]{1,0:T(8,128)(2,1)} %slice.301), channel_id=1, source_target_pairs={{0,1},{2,3},{4,5},{6,7},{8,9},{10,11},{12,13},{14,15},{16,17},{18,... | collective-permute-start | bytes 393224 | tf_op jit(solution)/shard_map/ppermute | solution.py:21
  158.4 3.7 copy-start.50
  160.9 44.2 %collective-permute-start.1 = (bf16[64,1024]{1,0:T(8,128)(2,1)}, bf16[64,1024]{1,0:T(8,128)(2,1)S(1)}, u32[]{:S(2)}, u32[]{:S(2)}) collective-permute-start(bf16[64,1024]{1,0:T(8,128)(2,1)} %slice.302), channel_id=1, source_target_pairs={{0,1},{2,3},{4,5},{6,7},{8,9},{10,11},{12,13},{14,15},{16,17},{18,... | collective-permute-start | bytes 393224 | tf_op jit(solution)/shard_map/ppermute | solution.py:21
  211.2 9.8 %copy-start.1 = (f32[8,512,576]{1,2,0:T(8,128)}, f32[8,512,576]{1,2,0:T(8,128)S(1)}, u32[]{:S(2)}) copy-start(f32[8,512,576]{1,2,0:T(8,128)S(1)} %get-tuple-element.163) | copy-start | bytes 28311556
  221.0 12.0 %copy-start.20 = (bf16[2,1024,512]{1,2,0:T(8,128)(2,1)S(1)}, bf16[2,1024,512]{1,2,0:T(8,128)(2,1)}, u32[]{:S(2)}) copy-start(bf16[2,1024,512]{1,2,0:T(8,128)(2,1)} %copy.45) | copy-start | bytes 6291460
  232.9 4.2 slice-start.10
  234.4 31.5 %copy-start.6 = (f32[512,1024]{1,0:T(8,128)}, f32[512,1024]{1,0:T(8,128)S(1)}, u32[]{:S(2)}) copy-start(f32[512,1024]{1,0:T(8,128)S(1)} %get-tuple-element.166) | copy-start | bytes 6291460
  234.4 7.8 %slice-start.7 = ((s8[5767168]{0:T(1024)(128)(4,1)}), s8[4194304]{0:T(1024)(128)(4,1)S(1)}, s32[]{:S(2)}) async-start(s8[5767168]{0:T(1024)(128)(4,1)} %bitcast.206), calls=%async_computation.7 | async-start | bytes 8388608
  234.6 7.5 %copy-start.36 = (bf16[512,1024]{1,0:T(8,128)(2,1)}, bf16[512,1024]{1,0:T(8,128)(2,1)S(1)}, u32[]{:S(2)}) copy-start(bf16[512,1024]{1,0:T(8,128)(2,1)S(1)} %multiply_convert_fusion.3) | copy-start | bytes 3145732
  237.1 5.1 slice-start.8
  237.1 10.1 %slice-start.3 = ((s8[5767168]{0:T(1024)(128)(4,1)}), s8[4194304]{0:T(1024)(128)(4,1)S(1)}, s32[]{:S(2)}) async-start(s8[5767168]{0:T(1024)(128)(4,1)} %bitcast.200), calls=%async_computation.3 | async-start | bytes 8388608
  242.1 5.0 slice-start.4
  242.2 5.0 copy-start.29
  257.3 5.1 copy-start.54
  275.9 14.0 %slice-start = ((s8[9437184]{0:T(1024)(128)(4,1)}), s8[4194304]{0:T(1024)(128)(4,1)S(1)}, s32[]{:S(2)}) async-start(s8[9437184]{0:T(1024)(128)(4,1)} %bitcast.183), calls=%async_computation | async-start | bytes 8388608
  276.0 14.0 %slice-start.1 = ((s8[9437184]{0:T(1024)(128)(4,1)}), s8[4194304]{0:T(1024)(128)(4,1)S(1)}, s32[]{:S(2)}) async-start(s8[9437184]{0:T(1024)(128)(4,1)} %bitcast.183), calls=%async_computation.1 | async-start | bytes 8388608
  283.4 6.6 %slice-start.2 = ((s8[9437184]{0:T(1024)(128)(4,1)}), s8[1048576]{0:T(1024)(128)(4,1)S(1)}, s32[]{:S(2)}) async-start(s8[9437184]{0:T(1024)(128)(4,1)} %bitcast.183), calls=%async_computation.2 | async-start | bytes 2097152
  316.0 3.9 copy-start.11
  316.0 4.2 copy-start.33
  321.8 3.7 slice-start.5
  327.3 4.1 copy-start.30
  331.5 5.1 copy-start.37
  331.5 5.1 copy-start.55
  336.6 5.1 copy-start.53
  341.7 5.1 copy-start.4
  341.7 5.1 copy-start.35
  356.4 31.8 %collective-permute-start.2 = (bf16[64,1024]{0,1:T(8,128)(2,1)}, bf16[64,1024]{0,1:T(8,128)(2,1)}, u32[]{:S(2)}, u32[]{:S(2)}) collective-permute-start(bf16[64,1024]{0,1:T(8,128)(2,1)} %bitcast.54), channel_id=1, source_target_pairs={{1,0},{3,2},{5,4},{7,6},{9,8},{11,10},{13,12},{15,14},{17,16},{19,... | collective-permute-start | bytes 393224 | tf_op jit(solution)/shard_map/ppermute | solution.py:21
  358.4 39.8 %collective-permute-start.3 = (bf16[64,1024]{0,1:T(8,128)(2,1)}, bf16[64,1024]{0,1:T(8,128)(2,1)}, u32[]{:S(2)}, u32[]{:S(2)}) collective-permute-start(bf16[64,1024]{0,1:T(8,128)(2,1)} %bitcast.60), channel_id=1, source_target_pairs={{1,0},{3,2},{5,4},{7,6},{9,8},{11,10},{13,12},{15,14},{17,16},{19,... | collective-permute-start | bytes 393224 | tf_op jit(solution)/shard_map/ppermute | solution.py:21
  391.1 4.3 copy-start.14
  402.5 4.1 copy-start.19
  402.5 4.1 copy-start.21
  402.5 4.1 copy-start.23
  402.5 4.1 copy-start.31
  553.5 8.5 %copy-start.49 = (f32[8,128]{1,0:T(8,128)S(1)}, f32[8,128]{1,0:T(8,128)}, u32[]{:S(2)}) copy-start(f32[8,128]{1,0:T(8,128)} %get-tuple-element.138) | copy-start | bytes 12292
  553.5 9.1 %copy-start.5 = (f32[512,1024]{1,0:T(8,128)S(1)}, f32[512,1024]{1,0:T(8,128)}, u32[]{:S(2)}) copy-start(f32[512,1024]{1,0:T(8,128)} %copy-done.3) | copy-start | bytes 6291460
  553.5 9.1 %copy-start.15 = (bf16[512,1024]{1,0:T(8,128)(2,1)S(1)}, bf16[512,1024]{1,0:T(8,128)(2,1)}, u32[]{:S(2)}) copy-start(bf16[512,1024]{1,0:T(8,128)(2,1)} %param.28) | copy-start | bytes 3145732
  553.5 9.1 %copy-start.46 = (f32[512]{0:T(512)S(1)}, f32[512]{0:T(512)}, u32[]{:S(2)}) copy-start(f32[512]{0:T(512)} %get-tuple-element.156) | copy-start | bytes 6148
  562.6 4.2 copy-start.42
  562.6 4.9 copy-start.41
  562.6 5.5 copy-start.40
  562.6 6.2 %copy-start.38 = (f32[176,512]{1,0:T(8,128)S(1)}, f32[176,512]{1,0:T(8,128)}, u32[]{:S(2)}) copy-start(f32[176,512]{1,0:T(8,128)} %get-tuple-element.137) | copy-start | bytes 1081348
  (24 other events, 57.9 us)

commit v2 on v0

--- a/solution.py
+++ b/solution.py
@@ -1,6 +1,10 @@
+import functools
+
 import jax
 import jax.numpy as jnp
 from jax import lax
+from jax.experimental import pallas as pl
+from jax.experimental.pallas import tpu as pltpu
 from jax.sharding import PartitionSpec as P
 
 HEADS = 16
@@ -54,7 +58,7 @@
     return jnp.einsum("td,tf->df", inputs, grad_rows, preferred_element_type=jnp.float32)
 
 
-def shards(
+def plain_block(
     tokens,
     seq_lengths,
     w_query,
@@ -344,7 +348,1027 @@
     )
 
 
+MESH = pl.DeviceIdType.MESH
+NZ, NY, NX = 4, 2, 2
+SEQUENCE = {"zfx": "zxy", "zfy": "zyx", "zmx": "xzy", "zmy": "yzx"}
+ALL_Z, ALL_Y, ALL_X = pl.ds(0, NZ), pl.ds(0, NY), pl.ds(0, NX)
+
+
+class Plan:
+    def __init__(self, tensors):
+        self.tensors = tensors
+        self.items, self.of_tensor = [], []
+        for t, (rows, _, kind, splits, _) in enumerate(tensors):
+            begin, mine = 0, []
+            for half, count in enumerate(splits):
+                mine.append(len(self.items))
+                self.items.append((t, SEQUENCE[kind + "xy"[half]], begin, count))
+                begin += count
+            self.of_tensor.append(mine)
+
+
+class Place:
+    def __init__(self):
+        self.c, self.s = lax.axis_index("dp"), lax.axis_index("seq")
+        self.z, self.y, self.x = self.c // 4, (self.c // 2) % 2, self.c % 2
+
+    def at(self, z, y, x):
+        return (z * 4 + y * 2 + x, self.s)
+
+    def to_x(self):
+        return self.at(self.z, self.y, 1 - self.x)
+
+    def to_y(self):
+        return self.at(self.z, 1 - self.y, self.x)
+
+    def to_z(self, step):
+        return self.at((self.z + step) % NZ, self.y, self.x)
+
+    def to_core(self):
+        return (self.c, 1 - self.s)
+
+    def greet(self):
+        barrier = pltpu.get_barrier_semaphore()
+        peers = [self.to_x(), self.to_y(), self.to_core()] + [self.to_z(k) for k in (1, 2, 3)]
+        for peer in peers:
+            pl.semaphore_signal(barrier, inc=1, device_id=peer, device_id_type=MESH)
+        pl.semaphore_wait(barrier, len(peers))
+
+
+def remote(src, dst, send, recv, device):
+    return pltpu.make_async_remote_copy(
+        src_ref=src, dst_ref=dst, send_sem=send, recv_sem=recv, device_id=device, device_id_type=MESH
+    )
+
+
+class Gather:
+    def __init__(self, plan, place, shards, bufs, send, recv, local):
+        self.plan, self.me, self.shards, self.bufs = plan, place, shards, bufs
+        self.send, self.recv, self.local = send, recv, local
+
+    def own_copy(self, t):
+        me = self.me
+        return pltpu.make_async_copy(
+            self.shards[t], self.bufs[t].at[me.s, me.z, me.y, me.x], self.local.at[t]
+        )
+
+    def moves(self, i, phase):
+        t, seq, begin, count = self.plan.items[i]
+        me, buf = self.me, self.bufs[t]
+        rows = pl.ds(begin, count)
+
+        def view(z, y, x, half=me.s):
+            return buf.at[half, z, y, x, rows, :]
+
+        if phase == 3:
+            whole = view(ALL_Z, ALL_Y, ALL_X)
+            return [(whole, whole, me.to_core(), view(ALL_Z, ALL_Y, ALL_X, 1 - me.s), 0)]
+        done, axis = seq[:phase], seq[phase]
+        z = ALL_Z if "z" in done else me.z
+        y = ALL_Y if "y" in done else me.y
+        x = ALL_X if "x" in done else me.x
+        there = view(z, y, x)
+        here = self.shards[t].at[rows, :] if phase == 0 else there
+        if axis == "x":
+            return [(here, there, me.to_x(), view(z, y, 1 - me.x), 0)]
+        if axis == "y":
+            return [(here, there, me.to_y(), view(z, 1 - me.y, x), 0)]
+        return [
+            (here, there, me.to_z(k), view((me.z + NZ - k) % NZ, y, x), k - 1) for k in (1, 2, 3)
+        ]
+
+    def copy(self, i, phase, src, dst, device, k):
+        return remote(src, dst, self.send.at[i, phase, k], self.recv.at[i, phase, k], device)
+
+    def start(self, i, phase):
+        for here, there, device, _, k in self.moves(i, phase):
+            self.copy(i, phase, here, there, device, k).start()
+
+    def wait(self, i, phase):
+        for _, _, device, arrived, k in self.moves(i, phase):
+            self.copy(i, phase, arrived, arrived, device, k).wait_recv()
+
+    def finish(self, i):
+        for phase in range(4):
+            for here, there, device, _, k in self.moves(i, phase):
+                self.copy(i, phase, here, there, device, k).wait_send()
+
+
+def staged_order(tensors, lags):
+    order = []
+    for step in range(tensors + max(lags)):
+        for phase, lag in enumerate(lags):
+            if 0 <= step - lag < tensors:
+                order.append((step - lag, phase))
+    return order
+
+
+def got_shapes(plan):
+    shapes = []
+    for rows, columns, kind, _, dtype in plan.tensors:
+        second, third = ((1, NZ), (3,)) if kind == "zf" else ((3, 2), (1,))
+        shapes.append([(d + (rows, columns), dtype) for d in ((NZ, 2), second, third)])
+    return shapes
+
+
+class Scatter:
+    def __init__(self, plan, place, total, got, out, send, recv):
+        self.plan, self.me, self.total, self.got, self.out = plan, place, total, got, out
+        self.send, self.recv = send, recv
+
+    def moves(self, i, phase):
+        t, seq, begin, count = self.plan.items[i]
+        me, total, got = self.me, self.total[t], self.got[t][phase]
+        rows = pl.ds(begin, count)
+        axis, done = seq[2 - phase], seq[3 - phase :]
+        z = me.z if "z" in done else ALL_Z
+        y = me.y if "y" in done else ALL_Y
+        x = me.x if "x" in done else ALL_X
+        if phase == 0:
+            lands = [got.at[ALL_Z, pl.ds(0, 2), rows, :]]
+        elif phase == 1:
+            lands = [got.at[k, pl.ds(0, got.shape[1]), rows, :] for k in range(got.shape[0])]
+        else:
+            lands = [got.at[k, rows, :] for k in range(got.shape[0])]
+        if axis == "x":
+            return [(total.at[z, y, 1 - me.x, rows, :], lands[0], me.to_x(), 0)]
+        if axis == "y":
+            return [(total.at[z, 1 - me.y, x, rows, :], lands[0], me.to_y(), 0)]
+        return [
+            (total.at[(me.z + k) % NZ, y, x, rows, :], lands[k - 1], me.to_z(k), k - 1)
+            for k in (1, 2, 3)
+        ]
+
+    def copy(self, i, phase, src, dst, device, k):
+        return remote(src, dst, self.send.at[i, phase, k], self.recv.at[i, phase, k], device)
+
+    def start(self, i, phase):
+        for here, there, device, k in self.moves(i, phase):
+            self.copy(i, phase, here, there, device, k).start()
+
+    def wait(self, i, phase):
+        for here, there, device, k in self.moves(i, phase):
+            self.copy(i, phase, there, there, device, k).wait_recv()
+
+    def add(self, i, phase):
+        t, seq, begin, count = self.plan.items[i]
+        me, total, got = self.me, self.total[t], self.got[t][phase]
+        rows = pl.ds(begin, count)
+        if phase == 0:
+            for z in range(NZ):
+                for o in range(2):
+                    at = (z, me.y, o) if seq[2] == "y" else (z, o, me.x)
+                    total[at + (rows,)] += got[z, o, rows]
+        elif phase == 1 and seq[1] != "z":
+            for z in range(NZ):
+                total[z, me.y, me.x, rows] += got[0, z, rows]
+        elif phase == 1:
+            for o in range(2):
+                at = (me.z, me.y, o) if seq[2] == "y" else (me.z, o, me.x)
+                part = total[at + (rows,)].astype(jnp.float32)
+                for k in range(3):
+                    part += got[k, o, rows].astype(jnp.float32)
+                total[at + (rows,)] = part.astype(total.dtype)
+        else:
+            part = total[me.z, me.y, me.x, rows].astype(jnp.float32)
+            for k in range(got.shape[0]):
+                part += got[k, rows].astype(jnp.float32)
+            self.out[t][rows] = part
+
+    def finish(self, i):
+        for phase in range(3):
+            for here, there, device, k in self.moves(i, phase):
+                self.copy(i, phase, here, there, device, k).wait_send()
+
+
+EPS = 1e-05
+PAIR = 2 * HEAD_DIM
+SPAN = 2 * WINDOW
+LOW = jnp.bfloat16
+F32 = jnp.float32
+
+
+def mm(left, right):
+    return jnp.dot(left, right, preferred_element_type=F32)
+
+
+def mm_nt(left, right):
+    return lax.dot_general(left, right, (((1,), (1,)), ((), ())), preferred_element_type=F32)
+
+
+def mm_tn(left, right):
+    return lax.dot_general(left, right, (((0,), (0,)), ((), ())), preferred_element_type=F32)
+
+
+def column_tiles(columns, size):
+    full = columns // size
+    tiles = [(0, size, full)]
+    if columns % size:
+        tiles.append((full * size, columns % size, 1))
+    return tiles
+
+
+def each_tile(columns, size, body):
+    for begin, width, count in column_tiles(columns, size):
+        if count == 1:
+            body(begin, width)
+        else:
+
+            def step(j, _, begin=begin, width=width):
+                body(pl.multiple_of(begin + j * width, 128), width)
+                return 0
+
+            lax.fori_loop(0, count, step, 0)
+
+
+def each_rows(rows, size, body):
+    def step(j, _):
+        body(pl.ds(pl.multiple_of(j * size, size), size))
+        return 0
+
+    lax.fori_loop(0, rows // size, step, 0)
+
+
+def both_heads(block):
+    first = lax.broadcasted_iota(jnp.int32, block.shape, 1) < HEAD_DIM
+    zero = jnp.zeros_like(block)
+    return jnp.concatenate([jnp.where(first, block, zero), jnp.where(first, zero, block)], axis=0)
+
+
+def merge_heads(stacked):
+    rows = stacked.shape[0] // 2
+    first = lax.broadcasted_iota(jnp.int32, (rows, PAIR), 1) < HEAD_DIM
+    return jnp.where(first, stacked[:rows], stacked[rows:])
+
+
+class Copies:
+    def __init__(self, sems):
+        self.sems, self.made = sems, []
+
+    def start(self, src, dst):
+        copy = pltpu.make_async_copy(src, dst, self.sems.at[len(self.made)])
+        copy.start()
+        self.made.append(copy)
+        return copy
+
+    def wait_all(self):
+        for copy in self.made:
+            copy.wait()
+
+
+FORWARD_ORDER = staged_order(8, (0, 2, 4))
+
+
+def forward_kernel(plan, *refs):
+    n = len(plan.tensors)
+    lens, x_in, dy_in, refs = refs[0], refs[1], refs[2], refs[3:]
+    shards, refs = refs[:n], refs[n:]
+    w_out, refs = refs[: n - 1], refs[n - 1 :]
+    (mixed_o, q_o, k_o, v_o, p_o, x1_o, ha_o, ho_o, hm_o, hid_o, dact_o, act_o, dyh_o, gain_o), refs = refs[:14], refs[14:]
+    bufs, refs = refs[:n], refs[n:]
+    (gains, h1, q, kx, vx, probs, o, x1, h2, hid, act, dact, ha, ho, hm, hidt, mixed), refs = refs[:17], refs[17:]
+    send, recv, own_sem, out_sem, rim_send, rim_recv, half_send, half_recv = refs
+    rows, width = x_in.shape
+    chips = NZ * NY * NX
+    me = Place()
+    me.greet()
+    gather = Gather(plan, me, shards, bufs, send, recv, own_sem)
+    copies = Copies(out_sem)
+    sends = []
+
+    def to_partner(k, src, dst):
+        copy = remote(src, dst, half_send.at[k], half_recv.at[k], me.to_core())
+        copy.start()
+        sends.append(copy)
+
+    def lanes(ref):
+        return ref.at[:, pl.ds(pl.multiple_of(me.s * rows, 128), rows)]
+
+    def share(k, mine, whole):
+        copies.start(mine, lanes(whole))
+        to_partner(k, mine, lanes(whole))
+
+    for t in range(n):
+        gather.own_copy(t).start()
+    for i in range(len(plan.items)):
+        gather.start(i, 0)
+    for t in range(n):
+        gather.own_copy(t).wait()
+    half = dyh_o.shape[1]
+    mine = pl.ds(pl.multiple_of(me.s * rows, 16), rows)
+    copies.start(dy_in.at[:, pl.ds(pl.multiple_of(me.s * half, 128), half)], dyh_o.at[mine, :])
+    to_partner(0, dy_in.at[:, pl.ds(pl.multiple_of((1 - me.s) * half, 128), half)], dyh_o.at[mine, :])
+
+    def weight(t, side, cols):
+        w = bufs[t][side, :, :, :, :, cols]
+        return w.reshape(chips * w.shape[3], w.shape[4])
+
+    def norm(values, gain):
+        inverse = lax.rsqrt(jnp.mean(values * values, axis=-1, keepdims=True) + EPS)
+        return (values * inverse * gain).astype(LOW)
+
+    def first_norm():
+        parts = []
+        for z in range(NZ):
+            for y in range(NY):
+                pair = [bufs[0][me.s, z, y, x].astype(F32) for x in range(NX)]
+                parts.append(pair[0] + pair[1])
+        gains[...] = jnp.concatenate(parts, axis=1)[0:8]
+        copies.start(gains, gain_o)
+
+        def body(at):
+            h1[at, :] = norm(x_in[at, :].astype(F32), gains[0:1, :])
+
+        each_rows(rows, 64, body)
+        turn(h1, ha)
+        share(1, ha, ha_o)
+
+    def turn(src, dst):
+        def body(j, _):
+            at = pl.ds(pl.multiple_of(j * 128, 128), 128)
+            dst[at, :] = src[:, at].T
+            return 0
+
+        lax.fori_loop(0, src.shape[1] // 128, body, 0)
+
+    def project_to(t, src, dst, skip):
+        columns = plan.tensors[t][1]
+        for side in range(2):
+
+            def body(begin, size, side=side):
+                part = mm(src[...], weight(t, side, pl.ds(begin, size)))
+                dst[pl.ds(skip, rows), pl.ds(side * columns + begin, size)] = part.astype(LOW)
+
+            each_tile(columns, 256, body)
+
+    def rim(k, ref):
+        return remote(ref.at[pl.ds(rows, WINDOW), :], ref.at[pl.ds(0, WINDOW), :], rim_send.at[k], rim_recv.at[k], me.to_core())
+
+    def do_query():
+        project_to(1, h1, q, 0)
+        copies.start(q, q_o)
+
+    def do_key():
+        project_to(2, h1, kx, WINDOW)
+        rim(0, kx).start()
+
+    def do_value():
+        project_to(3, h1, vx, WINDOW)
+        rim(1, vx).start()
+
+    def rims():
+        for k, ref in ((0, kx), (1, vx)):
+            rim(k, ref).wait_recv()
+        copies.start(kx, k_o)
+        copies.start(vx, v_o)
+
+    first_end = lens[0, 0]
+    second_end = first_end + lens[0, 1]
+
+    def attend(b):
+        base = me.s * rows + b * WINDOW
+        at = pl.ds(pl.multiple_of(b * WINDOW, WINDOW), WINDOW)
+        over = pl.ds(pl.multiple_of(b * WINDOW, WINDOW), SPAN)
+        row = lax.broadcasted_iota(jnp.int32, (WINDOW, SPAN), 0)
+        col = lax.broadcasted_iota(jnp.int32, (WINDOW, SPAN), 1)
+        q_pos, k_pos = base + row, base - WINDOW + col
+
+        def doc(pos):
+            return (pos >= first_end).astype(jnp.int32) + (pos >= second_end).astype(jnp.int32)
+
+        visible = (col >= row) & (col <= row + WINDOW) & (k_pos >= 0) & (doc(q_pos) == doc(k_pos))
+        bias = jnp.where(visible, 0.0, -1e30)
+        bias = jnp.concatenate([bias, bias], axis=0)
+        for p in range(HEADS // 2):
+            cols = slice(p * PAIR, (p + 1) * PAIR)
+            q2 = both_heads(q[at, cols])
+            s = mm_nt(q2, kx[over, cols]) * HEAD_DIM ** (-0.5) + bias
+            e = jnp.exp(s - jnp.max(s, axis=-1, keepdims=True))
+            prob = (e / jnp.sum(e, axis=-1, keepdims=True)).astype(LOW)
+            probs[at, 2 * p * SPAN : (2 * p + 1) * SPAN] = prob[:WINDOW]
+            probs[at, (2 * p + 1) * SPAN : (2 * p + 2) * SPAN] = prob[WINDOW:]
+            o[at, cols] = merge_heads(mm(prob, vx[over, cols])).astype(LOW)
+
+    def attend_some(begin, count):
+        def step(b, _):
+            attend(b)
+            return 0
+
+        lax.fori_loop(begin, begin + count, step, 0)
+
+    def after_attention():
+        copies.start(probs, p_o)
+        turn(o, ho)
+        share(2, ho, ho_o)
+
+    def add_out():
+        columns = plan.tensors[4][1]
+        for side in range(2):
+
+            def body(begin, size, side=side):
+                cols = pl.ds(side * columns + begin, size)
+                x1[:, cols] = x_in[:, cols].astype(F32) + mm(o[...], weight(4, side, pl.ds(begin, size)))
+
+            each_tile(columns, 256, body)
+        copies.start(x1, x1_o)
+
+        def body(at):
+            h2[at, :] = norm(x1[at, :], gains[1:2, :])
+
+        each_rows(rows, 64, body)
+        turn(h2, hm)
+        share(3, hm, hm_o)
+
+    wide = plan.tensors[5][1]
+
+    def mlp(side, begin, size):
+        cols = pl.ds(begin, size)
+        a = mm(h2[...], weight(5, side, cols))
+        b = mm(h2[...], weight(6, side, cols))
+        sig = 1.0 / (1.0 + jnp.exp(-a))
+        silu = a * sig
+        to = pl.ds(side * wide + begin, size)
+        act[:, to] = silu.astype(LOW)
+        dact[:, to] = (b * sig * (1.0 + a * (1.0 - sig))).astype(LOW)
+        hidden = (silu * b).astype(LOW)
+        hid[:, to] = hidden
+        hidt[to, :] = hidden.T
+
+    def mlp_some(side, begin, size, count):
+        def step(j, _):
+            mlp(side, pl.multiple_of(begin + j * size, 128), size)
+            return 0
+
+        lax.fori_loop(0, count, step, 0)
+
+    def after_mlp():
+        copies.start(act, act_o)
+        copies.start(dact, dact_o)
+        share(4, hidt, hid_o)
+
+    def add_down():
+        columns = plan.tensors[7][1]
+        for side in range(2):
+
+            def body(begin, size, side=side):
+                cols = pl.ds(side * columns + begin, size)
+                part = mm(hid[...], weight(7, side, pl.ds(begin, size)))
+                mixed[:, cols] = (x1[:, cols] + part).astype(LOW)
+
+            each_tile(columns, 256, body)
+        copies.start(mixed, mixed_o)
+
+    blocks = rows // WINDOW
+    whole = wide // 256
+    rest = wide - whole * 256
+    work = [(0, first_norm), (1, do_query), (2, do_key), (3, do_value), (3, rims)]
+    work += [(3, functools.partial(attend_some, b, 2)) for b in range(0, blocks, 2)]
+    work += [(3, after_attention), (4, add_out)]
+    for side in range(2):
+        work += [(6, functools.partial(mlp_some, side, 0, 256, whole))]
+        work += [(6, functools.partial(mlp, side, whole * 256, rest))] if rest else []
+    work += [(6, after_mlp), (7, add_down)]
+    passed, done = set(), set()
+
+    def arrive(t):
+        if t in passed:
+            return
+        passed.add(t)
+        for i in plan.of_tensor[t]:
+            gather.wait(i, 3)
+        if t:
+            copies.start(bufs[t], w_out[t - 1])
+
+    for t, phase in FORWARD_ORDER:
+        for i in plan.of_tensor[t]:
+            gather.wait(i, phase)
+            gather.start(i, phase + 1)
+        if phase == 2:
+            done.add(t)
+        for _ in range(2):
+            if work and all(k in done for k in range(work[0][0] + 1)) and not (phase == 2 and t == work[0][0]):
+                need, piece = work.pop(0)
+                for k in range(need + 1):
+                    arrive(k)
+                piece()
+    for need, piece in work:
+        for k in range(need + 1):
+            arrive(k)
+        piece()
+    for i in range(len(plan.items)):
+        gather.finish(i)
+    for k, ref in ((0, kx), (1, vx)):
+        rim(k, ref).wait_send()
+    for copy in sends:
+        copy.wait()
+    copies.wait_all()
+
+
+def forward_all(plan, lens, tokens, cotangent, shards):
+    n, k = len(plan.tensors), len(plan.items)
+    rows, width = tokens.shape
+    wide = 2 * plan.tensors[5][1]
+    anywhere = pl.BlockSpec(memory_space=pl.ANY)
+    inside = pl.BlockSpec(memory_space=pltpu.VMEM)
+    shape = jax.ShapeDtypeStruct
+    bufs = [(2, NZ, NY, NX) + t[:2] for t in plan.tensors]
+    over = WINDOW + rows
+    kept = [
+        ((rows, width), LOW),
+        ((rows, width), LOW),
+        ((over, width), LOW),
+        ((over, width), LOW),
+        ((rows, HEADS * SPAN), LOW),
+        ((rows, width), F32),
+        ((width, 2 * rows), LOW),
+        ((width, 2 * rows), LOW),
+        ((width, 2 * rows), LOW),
+        ((wide, 2 * rows), LOW),
+        ((rows, wide), LOW),
+        ((rows, wide), LOW),
+        ((2 * rows, width // 2), LOW),
+        ((8, width), F32),
+    ]
+    scratch = [
+        ((8, width), F32),
+        ((rows, width), LOW),
+        ((rows, width), LOW),
+        ((over, width), LOW),
+        ((over, width), LOW),
+        ((rows, HEADS * SPAN), LOW),
+        ((rows, width), LOW),
+        ((rows, width), F32),
+        ((rows, width), LOW),
+        ((rows, wide), LOW),
+        ((rows, wide), LOW),
+        ((rows, wide), LOW),
+        ((width, rows), LOW),
+        ((width, rows), LOW),
+        ((width, rows), LOW),
+        ((wide, rows), LOW),
+        ((rows, width), LOW),
+    ]
+    dma = pltpu.SemaphoreType.DMA
+    outs = pl.pallas_call(
+        functools.partial(forward_kernel, plan),
+        out_shape=[shape(b, LOW) for b in bufs[1:]] + [shape(*s) for s in kept],
+        in_specs=[pl.BlockSpec(memory_space=pltpu.SMEM), inside, anywhere] + [anywhere] * n,
+        out_specs=[anywhere] * (n - 1 + len(kept)),
+        scratch_shapes=[pltpu.VMEM(b, LOW) for b in bufs]
+        + [pltpu.VMEM(*s) for s in scratch]
+        + [dma((k, 4, 3)), dma((k, 4, 3)), dma((n,)), dma((24,)), dma((2,)), dma((2,)), dma((5,)), dma((5,))],
+        compiler_params=pltpu.CompilerParams(
+            collective_id=0, has_side_effects=True, vmem_limit_bytes=62 * 2**20
+        ),
+        name="forward_all",
+    )(lens, tokens, cotangent, *shards)
+    return outs[: n - 1], outs[n - 1 :]
+
+
+class Stream:
+    def __init__(self, count, sems, fetch):
+        self.count, self.sems, self.fetch = count, sems, fetch
+
+    def copies(self, j, slot):
+        return [
+            pltpu.make_async_copy(src, dst, self.sems.at[slot, k])
+            for k, (src, dst) in enumerate(self.fetch(j, slot))
+        ]
+
+    def prime(self):
+        for copy in self.copies(0, 0):
+            copy.start()
+
+    def run(self, body):
+        def step(j, _):
+            slot = j % 2
+
+            @pl.when(j + 1 < self.count)
+            def _():
+                for copy in self.copies(j + 1, 1 - slot):
+                    copy.start()
+
+            for copy in self.copies(j, slot):
+                copy.wait()
+            body(j, slot)
+            return 0
+
+        lax.fori_loop(0, self.count, step, 0)
+
+
+BACKWARD_EVENTS = {
+    "hidden": [],
+    "up": [(0, 0)],
+    "gate": [],
+    "dh2": [(0, 1), (1, 0)],
+    "norm2": [],
+    "out": [(0, 2), (2, 0)],
+    "attend": [(1, 1), (2, 1), (1, 2), (3, 0)],
+    "qkv": [(2, 2), (3, 1)],
+    "dh1": [(3, 2), (4, 0)],
+    "end": [(5, 0), (4, 1), (6, 0), (5, 1), (7, 0), (4, 2), (6, 1), (7, 1), (5, 2), (6, 2), (7, 2)],
+}
+
+
+def backward_kernel(plan, *refs):
+    n = len(plan.tensors)
+    ws, refs = refs[:7], refs[7:]
+    (x_h, dy_h, q_h, k_h, v_h, p_h, x1_h, ha_h, ho_h, hm_h, hid_h, dact_h, act_h, dyh_h, gains), refs = refs[:15], refs[15:]
+    (gtok_o,), outs, refs = refs[:1], refs[1 : 1 + n], refs[1 + n :]
+    total, refs = refs[:n], refs[n:]
+    got, refs = [refs[3 * t : 3 * t + 3] for t in range(n)], refs[3 * n :]
+    (da, db, kx, vx, dar, dbr, dxr_r, qr, kr, vr, dyh, turned, small, broad, dy, x1, dh, dxr, do), refs = refs[:19], refs[19:]
+    (kc, vc, rim_k, rim_v, gain_sum, gain_other), refs = refs[:6], refs[6:]
+    send, recv, load_sem, small_sem, broad_sem, turn_sem, half_send, half_recv, out_sem = refs
+    wq, wk, wv, wo, wg, wu, wd = ws
+    rows, width = dy.shape
+    wide = wg.shape[2]
+    columns = wq.shape[2]
+    me = Place()
+    me.greet()
+    scatter = Scatter(plan, me, total, got, outs, send, recv)
+    halves = []
+
+    def to_partner(k, src, dst):
+        copy = remote(src, dst, half_send.at[k], half_recv.at[k], me.to_core())
+        copy.start()
+        halves.append(copy)
+        return copy
+
+    loads = [0]
+
+    def load(src, dst):
+        copy = pltpu.make_async_copy(src, dst, load_sem.at[loads[0]])
+        loads[0] += 1
+        copy.start()
+        return copy
+
+    def own(size, side=0):
+        return pl.ds(pl.multiple_of((me.s if side == 0 else 1 - me.s) * size, 128), size)
+
+    tall = plan.tensors[0][0] * NY * NX
+    hid_tiles = Stream(
+        NZ, turn_sem, lambda j, slot: [(hid_h.at[pl.ds(pl.multiple_of(j * tall, 16), tall), :], turned.at[slot, pl.ds(0, tall), :])]
+    )
+    tile = 256
+
+    def weight_tiles(w, k=0, slots=small):
+        return lambda j, slot: (w.at[:, pl.ds(pl.multiple_of(j * tile, tile), tile), :], slots.at[slot, k])
+
+    def stream_of(fetchers, count, sems):
+        return Stream(count, sems, lambda j, slot: [f(j, slot) for f in fetchers])
+
+    down_tiles = stream_of([weight_tiles(wd)], wd.shape[1] // tile, small_sem)
+    mlp_tiles = stream_of([weight_tiles(wg, 0, broad), weight_tiles(wu, 1, broad)], width // tile, broad_sem)
+    out_tiles = stream_of([weight_tiles(wo)], width // tile, small_sem)
+    qkv_tiles = stream_of([weight_tiles(w, k) for k, w in enumerate((wq, wk, wv))], width // tile, small_sem)
+
+    get_dyh = load(dyh_h, dyh)
+    hid_tiles.prime()
+    get_dy = load(dy_h, dy)
+    down_tiles.prime()
+    get_dact = load(dact_h, da)
+    get_act = load(act_h, db)
+    mlp_tiles.prime()
+    get_x1 = load(x1_h, x1)
+    get_k, get_v = load(k_h, kx), load(v_h, vx)
+
+    def events(name):
+        for t, phase in BACKWARD_EVENTS[name]:
+            for i in plan.of_tensor[t]:
+                scatter.wait(i, phase)
+                scatter.add(i, phase)
+                if phase < 2:
+                    scatter.start(i, phase + 1)
+
+    def begin(t):
+        for i in plan.of_tensor[t]:
+            scatter.start(i, 0)
+
+    def put(t, z, part):
+        row_count, column_count = plan.tensors[t][:2]
+        total[t][z] = part.reshape(NY, NX, row_count, column_count).astype(total[t].dtype)
+
+    get_dyh.wait()
+
+    def down_body(z, slot):
+        put(0, z, mm(turned[slot, :tall], dyh[...]))
+
+    hid_tiles.run(down_body)
+    begin(0)
+    get_hm = load(hm_h, turned.at[0])
+    get_ho = load(ho_h, turned.at[1])
+    events("hidden")
+
+    for copy in (get_dy, get_dact, get_act):
+        copy.wait()
+
+    def hidden_body(j, slot):
+        part = mm_nt(dy[:, :columns], small[slot, 0, 0]) + mm_nt(dy[:, columns:], small[slot, 0, 1])
+        at = pl.ds(pl.multiple_of(j * tile, tile), tile)
+        da[:, at] = (part * da[:, at].astype(F32)).astype(LOW)
+        db[:, at] = (part * db[:, at].astype(F32)).astype(LOW)
+
+    down_tiles.run(hidden_body)
+    out_tiles.prime()
+    got_db = to_partner(0, db.at[:, own(wide, 1)], dbr)
+    got_da = to_partner(1, da.at[:, own(wide, 1)], dar)
+    events("up")
+
+    def weight_grad_to(t, slot, mine, theirs):
+        row_count = plan.tensors[t][0] * NY * NX
+
+        def step(z, _):
+            at = pl.ds(pl.multiple_of(z * row_count, 16), row_count)
+            put(t, z, mm(turned[slot, at, own(rows)], mine()) + mm(turned[slot, at, own(rows, 1)], theirs[...]))
+            return 0
+
+        lax.fori_loop(0, NZ, step, 0)
+        begin(t)
+
+    get_hm.wait()
+    got_db.wait_recv()
+    weight_grad_to(1, 0, lambda: db[:, own(wide)], dbr)
+    events("gate")
+    got_da.wait_recv()
+    weight_grad_to(2, 0, lambda: da[:, own(wide)], dar)
+    get_ha = load(ha_h, turned.at[0])
+    events("dh2")
+
+    def dh2_body(j, slot):
+        part = None
+        for k, grad in ((0, da), (1, db)):
+            for side in range(2):
+                term = mm_nt(grad[:, side * wide : (side + 1) * wide], broad[slot, k, side])
+                part = term if part is None else part + term
+        dh[:, pl.ds(pl.multiple_of(j * tile, tile), tile)] = part
+
+    mlp_tiles.run(dh2_body)
+    for copy in halves[:2]:
+        copy.wait_send()
+    get_q = load(q_h, da.at[:, pl.ds(0, width)])
+    get_p = load(p_h, db.at[:, pl.ds(0, HEADS * SPAN)])
+    get_x = load(x_h, da.at[:, pl.ds(width, width)])
+    events("norm2")
+
+    def norm_grad(values, grad_norm, gain):
+        inverse = lax.rsqrt(jnp.mean(values * values, axis=-1, keepdims=True) + EPS)
+        scaled = grad_norm * gain
+        mean_term = jnp.mean(values * scaled, axis=-1, keepdims=True)
+        back = inverse * scaled - values * (inverse * inverse * inverse) * mean_term
+        return back, jnp.sum(values * inverse * grad_norm, axis=0, keepdims=True)
+
+    gain_sum[...] = jnp.zeros_like(gain_sum)
+    get_x1.wait()
+
+    def norm2_body(at):
+        back, gain_part = norm_grad(x1[at, :], dh[at, :], gains[1:2, :])
+        gain_sum[1:2, :] += gain_part
+        grad = dy[at, :].astype(F32) + back
+        x1[at, :] = grad
+        dxr[at, :] = grad.astype(LOW)
+
+    each_rows(rows, 64, norm2_body)
+    got_dxr = to_partner(2, dxr.at[:, own(columns, 1)], dxr_r)
+    events("out")
+
+    def out_body(j, slot):
+        part = mm_nt(dxr[:, :columns], small[slot, 0, 0]) + mm_nt(dxr[:, columns:], small[slot, 0, 1])
+        do[:, pl.ds(pl.multiple_of(j * tile, tile), tile)] = part.astype(LOW)
+
+    out_tiles.run(out_body)
+    qkv_tiles.prime()
+    get_ho.wait()
+    got_dxr.wait_recv()
+    weight_grad_to(3, 1, lambda: dxr[:, own(columns)], dxr_r)
+    events("attend")
+
+    kc[...] = jnp.zeros_like(kc)
+    vc[...] = jnp.zeros_like(vc)
+    for copy in (get_q, get_p, get_k, get_v):
+        copy.wait()
+    scale = HEAD_DIM ** (-0.5)
+
+    def attend(b, _):
+        at = pl.ds(pl.multiple_of(b * WINDOW, WINDOW), WINDOW)
+        over = pl.ds(pl.multiple_of(b * WINDOW, WINDOW), SPAN)
+        for p in range(HEADS // 2):
+            cols = slice(p * PAIR, (p + 1) * PAIR)
+            q2, do2 = both_heads(da[at, cols]), both_heads(do[at, cols])
+            keys, values = kx[over, cols], vx[over, cols]
+            prob = jnp.concatenate(
+                [db[at, 2 * p * SPAN : (2 * p + 1) * SPAN], db[at, (2 * p + 1) * SPAN : (2 * p + 2) * SPAN]], axis=0
+            )
+            wide_prob = prob.astype(F32)
+            grad_prob = mm_nt(do2, values)
+            inner = jnp.sum(wide_prob * grad_prob, axis=-1, keepdims=True)
+            grad_score = (wide_prob * (grad_prob - inner)).astype(LOW)
+            da[at, cols] = (merge_heads(mm(grad_score, keys)) * scale).astype(LOW)
+            grad_keys = mm_tn(grad_score, q2) * scale
+            grad_values = mm_tn(prob, do2)
+            kx[at, cols] = (kc[:, cols] + grad_keys[:WINDOW]).astype(LOW)
+            vx[at, cols] = (vc[:, cols] + grad_values[:WINDOW]).astype(LOW)
+            kc[:, cols] = grad_keys[WINDOW:]
+            vc[:, cols] = grad_values[WINDOW:]
+        return 0
+
+    lax.fori_loop(0, rows // WINDOW, attend, 0)
+    rims = [to_partner(3, kx.at[pl.ds(0, WINDOW), :], rim_k), to_partner(4, vx.at[pl.ds(0, WINDOW), :], rim_v)]
+    got_q = to_partner(5, da.at[:, own(columns, 1)], qr)
+    events("qkv")
+    got_q.wait_recv()
+    get_ha.wait()
+    weight_grad_to(4, 0, lambda: da[:, own(columns)], qr)
+    for copy, ref, carry, rim in ((rims[0], kx, kc, rim_k), (rims[1], vx, vc, rim_v)):
+        copy.wait_recv()
+        ref[pl.ds(rows, WINDOW), :] = (carry[...] + rim[...].astype(F32)).astype(LOW)
+    later = pl.ds(WINDOW, rows)
+    got_k = to_partner(6, kx.at[later, own(columns, 1)], kr)
+    got_v = to_partner(7, vx.at[later, own(columns, 1)], vr)
+    got_k.wait_recv()
+    weight_grad_to(5, 0, lambda: kx[later, own(columns)], kr)
+    got_v.wait_recv()
+    weight_grad_to(6, 0, lambda: vx[later, own(columns)], vr)
+    events("dh1")
+
+    def dh1_body(j, slot):
+        part = None
+        for k, (grad, skip) in enumerate(((da, 0), (kx, WINDOW), (vx, WINDOW))):
+            for side in range(2):
+                left = grad[pl.ds(skip, rows), side * columns : (side + 1) * columns]
+                term = mm_nt(left, small[slot, k, side])
+                part = term if part is None else part + term
+        dh[:, pl.ds(pl.multiple_of(j * tile, tile), tile)] = part
+
+    qkv_tiles.run(dh1_body)
+    get_x.wait()
+
+    def norm1_body(at):
+        back, gain_part = norm_grad(da[at, pl.ds(width, width)].astype(F32), dh[at, :], gains[0:1, :])
+        gain_sum[0:1, :] += gain_part
+        x1[at, :] = x1[at, :] + back
+
+    each_rows(rows, 64, norm1_body)
+    give = pltpu.make_async_copy(x1, gtok_o, out_sem)
+    give.start()
+    got_gain = to_partner(8, gain_sum, gain_other)
+    got_gain.wait_recv()
+    lanes = plan.tensors[7][1]
+    for c in range(NZ * NY * NX):
+        at = slice(c // 2 * lanes, (c // 2 + 1) * lanes)
+        total[7][c // 4, c // 2 % 2, c % 2] = gain_sum[:, at] + gain_other[:, at]
+    begin(7)
+    events("end")
+    for i in range(len(plan.items)):
+        scatter.finish(i)
+    for k, copy in enumerate(halves):
+        if k >= 2:
+            copy.wait_send()
+    give.wait()
+
+
+def backward_all(plan, ws, tokens, cotangent, acts):
+    n, k = len(plan.tensors), len(plan.items)
+    rows, width = tokens.shape
+    columns, wide = ws[0].shape[2], ws[4].shape[2]
+    anywhere = pl.BlockSpec(memory_space=pl.ANY)
+    inside = pl.BlockSpec(memory_space=pltpu.VMEM)
+    over = WINDOW + rows
+    scratch = [
+        ((rows, 2 * wide), LOW),
+        ((rows, 2 * wide), LOW),
+        ((over, width), LOW),
+        ((over, width), LOW),
+        ((rows, wide), LOW),
+        ((rows, wide), LOW),
+        ((rows, columns), LOW),
+        ((rows, columns), LOW),
+        ((rows, columns), LOW),
+        ((rows, columns), LOW),
+        ((2 * rows, columns), LOW),
+        ((2, width, 2 * rows), LOW),
+        ((2, 3, 2, 256, columns), LOW),
+        ((2, 2, 2, 256, wide), LOW),
+        ((rows, width), LOW),
+        ((rows, width), F32),
+        ((rows, width), F32),
+        ((rows, width), LOW),
+        ((rows, width), LOW),
+        ((WINDOW, width), F32),
+        ((WINDOW, width), F32),
+        ((WINDOW, width), LOW),
+        ((WINDOW, width), LOW),
+        ((8, width), F32),
+        ((8, width), F32),
+    ]
+    totals = [((NZ, NY, NX) + t[:2], t[4]) for t in plan.tensors]
+    got = [shape for shapes in got_shapes(plan) for shape in shapes]
+    dma = pltpu.SemaphoreType.DMA
+    return pl.pallas_call(
+        functools.partial(backward_kernel, plan),
+        out_shape=[jax.ShapeDtypeStruct((rows, width), F32)]
+        + [jax.ShapeDtypeStruct(t[:2], F32) for t in plan.tensors],
+        in_specs=[anywhere] * (7 + 14) + [inside],
+        out_specs=[anywhere] + [inside] * n,
+        scratch_shapes=[pltpu.VMEM(*s) for s in totals + got + scratch]
+        + [dma((k, 3, 3)), dma((k, 3, 3)), dma((16,)), dma((2, 3)), dma((2, 2)), dma((2, 1)), dma((9,)), dma((9,)), dma],
+        compiler_params=pltpu.CompilerParams(
+            collective_id=1, has_side_effects=True, vmem_limit_bytes=63 * 2**20
+        ),
+        name="backward_all",
+    )(*ws, tokens, cotangent, *acts)
+
+
+def pad_columns(w, part, tile):
+    rows = w.shape[0]
+    return jnp.pad(w.reshape(rows, -1, part), ((0, 0), (0, 0), (0, tile - part))).reshape(rows, -1)
+
+
+def unpad_columns(w, part, tile):
+    rows = w.shape[0]
+    return w.reshape(rows, -1, tile)[:, :, :part].reshape(rows, -1)
+
+
+def kinds(w_query, w_gate, w_down):
+    rows, columns = w_query.shape
+    part = w_down.shape[0]
+    tile = -(-part // 16) * 16
+    wide = w_gate.shape[1] // part * tile
+    first = -(-tile // 32) * 16
+    halves = (rows // 2, rows // 2)
+    return {
+        "square": (rows, columns, "zf", halves, LOW),
+        "square_m": (rows, columns, "zm", halves, LOW),
+        "broad": (rows, wide, "zf", halves, LOW),
+        "tall": (tile, columns, "zm", (first, tile - first), LOW),
+        "gain": (16, 2 * rows, "zf", (16,), LOW),
+        "gain_grad": (8, 2 * rows, "zf", (8,), F32),
+    }
+
+
+def gather_plan(w_query, w_key, w_value, w_out, w_gate, w_up, w_down, gain_attn, gain_mlp):
+    kind = kinds(w_query, w_gate, w_down)
+    names = ("gain", "square", "square", "square_m", "square", "broad", "broad", "tall")
+    plan = Plan([kind[name] for name in names])
+    rows, part, tile = w_query.shape[0], w_down.shape[0], kind["tall"][0]
+    both = jnp.stack([gain_attn, gain_mlp])
+    left = jnp.pad(both, ((0, 14), (0, rows)))
+    right = jnp.pad(both, ((0, 14), (rows, 0)))
+    pair = jnp.where(lax.axis_index("dp") % 2 == 0, left, right)
+    shards = [
+        pair,
+        w_query,
+        w_key,
+        w_value,
+        w_out,
+        pad_columns(w_gate, part, tile),
+        pad_columns(w_up, part, tile),
+        jnp.pad(w_down, ((0, tile - part), (0, 0))),
+    ]
+    return plan, shards
+
+
+def swift_block(
+    tokens,
+    seq_lengths,
+    w_query,
+    w_key,
+    w_value,
+    w_out,
+    w_gate,
+    w_up,
+    w_down,
+    gain_attn,
+    gain_mlp,
+    cotangent,
+):
+    plan, shards = gather_plan(w_query, w_key, w_value, w_out, w_gate, w_up, w_down, gain_attn, gain_mlp)
+    ws, acts = forward_all(plan, seq_lengths, tokens, cotangent, shards)
+    ws = [w.reshape(2, -1, w.shape[-1]) for w in ws]
+    kind = kinds(w_query, w_gate, w_down)
+    names = ("tall", "broad", "broad", "square", "square", "square", "square_m", "gain_grad")
+    back = Plan([kind[name] for name in names])
+    grad_tokens, *sums = backward_all(back, ws, tokens, cotangent, acts[1:])
+    rows, part, tile = w_query.shape[0], w_down.shape[0], kind["tall"][0]
+    own = lax.dynamic_slice_in_dim(sums[7], (lax.axis_index("dp") % 2) * rows, rows, 1)
+    return (
+        acts[0],
+        grad_tokens,
+        sums[4],
+        sums[5],
+        sums[6],
+        sums[3],
+        unpad_columns(sums[2], part, tile),
+        unpad_columns(sums[1], part, tile),
+        sums[0][:part],
+        own[0],
+        own[1],
+    )
+
+
 def solution(mesh):
+    fast = (mesh.shape["dp"], mesh.shape["seq"]) == (NZ * NY * NX, 2)
+    shards = swift_block if fast else plain_block
     in_specs = (
         P(("dp", "seq"), None),
         P("dp", None),

time: 1340 us -> 349 us (0.26)
  waiting for transfers between devices: 731 us -> 0 us
  Pallas kernels: 0 us -> 327 us
  blocking collectives: 300 us -> 0 us
  matrix products: 168 us -> 0 us
  other arithmetic: 45.3 us -> 1.35 us
  local copies, waits for them, and re-layouts: 54.9 us -> 19.2 us
  between operations: 18.8 us -> 0.76 us
    all_gather x14 -> x0, waiting for transfers between devices: 406 us -> none  [the longest x1 67.3 us: shards(): lax.all_gather(w_gate, 'dp', axis=0, tiled=True)]
    pallas_call x0 -> x2, Pallas kernels: none -> 327 us  [the longest x1 176 us: backward_all(): pl.pallas_call(functools.partial(backward_kernel, plan), out_shape=[jax.S...]
    unnamed x3 -> x0, blocking collectives: 297 us -> none
    reduce_scatter x11 -> x0, waiting for transfers between devices: 294 us -> none  [the longest x1 122 us: shards(): lax.psum_scatter(d_gate.astype(jnp.bfloat16), 'dp', scatter_dimension=0,...]
    dot_general x33 -> x0, matrix products: 168 us -> none  [the longest x7 38.7 us: weight_grad(): jnp.einsum('td,tf->df', inputs, grad_rows, preferred_element_type=jnp.flo...]
    unnamed x30 -> x0, waiting for transfers between devices: 28.7 us -> none
    convert_element_type x13 -> x0, other arithmetic: 24.7 us -> none  [the longest x1 14.1 us: shards(): grad_score = (prob_full * (grad_prob - inner)).astype(jnp.bfloat16)]
    unnamed x87 -> x19, local copies, waits for them, and re-layouts: 31.1 us -> 6.96 us
  transfers between devices with their start and end apart: 32 -> 0, of which waited for: 23 -> 0; matrix products, arithmetic and copies ran while one was open for 30% -> 0% of each run, Pallas kernels for 0% -> 0%
where the time goes in v2:
time: 349 us; the launch traced here: 348 us
  Pallas kernels  327 us (94%)
  local copies, waits for them, and re-layouts  19.2 us (6%)
    pallas_call x1, Pallas kernels, backward_all(): pl.pallas_call(functools.partial(backward_kernel, plan), out_shape=[jax.S...  176 us
    pallas_call x1, Pallas kernels, forward_all(): pl.pallas_call(functools.partial(forward_kernel, plan), out_shape=[shape(...  150 us

profile of v2, /device:TPU:0, one launch (start us, length us, event | category | flops | bytes accessed | tf_op | source)
XLA Modules:
  0.0 348.2 jit_solution(9694217152562656925)
XLA Ops:
  0.7 0.7 pad_maximum_fusion
  1.3 0.7 pad_select_fusion.refs_3_
  2.0 1.6 pad.23.refs_10_
  3.6 1.3 reshape.67
  5.0 0.9 reshape.68.refs_8_
  5.9 1.3 reshape.69
  7.3 0.9 reshape.70.refs_9_
  8.2 150.4 %forward_all.1 = (bf16[2,4,2,2,64,512]{5,4,3,2,1,0:T(8,128)(2,1)}, bf16[2,4,2,2,64,512]{5,4,3,2,1,0:T(8,128)(2,1)}, bf16[2,4,2,2,64,512]{5,4,3,2,1,0:T(8,128)(2,...) custom-call(s32[1,3]{1,0:T(1,128)} %refs_0_.1, ...), custom_call_target="tpu_custom_call" | custom-call | tf_op jit(solution)/shard_map/forward_all/pallas_call | solution.py:912
  158.7 176.4 %backward_all.1 = (f32[512,1024]{1,0:T(8,128)}, f32[176,512]{1,0:T(8,128)}, f32[64,1408]{1,0:T(8,128)}, f32[64,1408]{1,0:T(8,128)}, f32[64,512]{1,0:T(8,128)}, /...) custom-call(bf16[2,1024,512]{2,1,0:T(8,128)(2,1)} %bitcast.19, ...), custom_call_target="tpu_custom_call" | custom-call | tf_op jit(solution)/shard_map/backward_all/pallas_call | solution.py:1267
  335.1 0.7 constant_dynamic-slice_fusion
  335.8 0.5 slice_bitcast_fusion
  336.4 1.3 reshape.78
  337.7 1.0 reshape.79
  338.7 0.0 copy-start
  338.7 1.5 reshape.80
  340.2 1.0 reshape.81
  341.2 2.3 copy.30
  343.4 0.0 copy-done
  343.4 0.0 copy-start.5
  343.4 0.0 copy-start.4
  343.4 0.0 copy-start.3
  343.4 0.0 copy-start.2
  343.5 0.0 copy-start.1
  343.5 1.3 copy.31
  344.8 0.0 copy-done.5
  344.8 0.7 copy.32
  345.4 0.0 copy-done.4
  345.4 0.7 copy.33
  346.1 0.0 copy-done.3
  346.1 0.7 copy.34
  346.8 0.0 copy-done.2
  346.8 0.7 copy.35
  347.4 0.0 copy-done.1
  347.4 0.7 copy.36
  (2 shorter events, 0.1 us)
Async XLA Ops:
  338.7 4.7 %copy-start = (f32[512,1024]{1,0:T(8,128)S(1)}, f32[512,1024]{1,0:T(8,128)}, u32[]{:S(2)}) copy-start(f32[512,1024]{1,0:T(8,128)} %get-tuple-element.85) | copy-start | bytes 6291460
  343.4 1.4 copy-start.5
  343.4 2.0 copy-start.4
  343.4 2.7 copy-start.3
  343.4 3.3 copy-start.2
  343.5 4.0 %copy-start.1 = (f32[176,512]{1,0:T(8,128)S(1)}, f32[176,512]{1,0:T(8,128)}, u32[]{:S(2)}) copy-start(f32[176,512]{1,0:T(8,128)} %get-tuple-element.69) | copy-start | bytes 1081348

commit v3 on v2

--- a/solution.py
+++ b/solution.py
@@ -358,11 +358,11 @@
     def __init__(self, tensors):
         self.tensors = tensors
         self.items, self.of_tensor = [], []
-        for t, (rows, _, kind, splits, _) in enumerate(tensors):
+        for t, (_, _, _, cuts) in enumerate(tensors):
             begin, mine = 0, []
-            for half, count in enumerate(splits):
+            for kind, count in cuts:
                 mine.append(len(self.items))
-                self.items.append((t, SEQUENCE[kind + "xy"[half]], begin, count))
+                self.items.append((t, SEQUENCE[kind], begin, count))
                 begin += count
             self.of_tensor.append(mine)
 
@@ -454,20 +454,12 @@
                 self.copy(i, phase, here, there, device, k).wait_send()
 
 
-def staged_order(tensors, lags):
-    order = []
-    for step in range(tensors + max(lags)):
-        for phase, lag in enumerate(lags):
-            if 0 <= step - lag < tensors:
-                order.append((step - lag, phase))
-    return order
-
-
 def got_shapes(plan):
     shapes = []
-    for rows, columns, kind, _, dtype in plan.tensors:
-        second, third = ((1, NZ), (3,)) if kind == "zf" else ((3, 2), (1,))
-        shapes.append([(d + (rows, columns), dtype) for d in ((NZ, 2), second, third)])
+    for t, seq, _, count in plan.items:
+        _, columns, dtype, _ = plan.tensors[t]
+        second, third = ((1, NZ), (3,)) if seq[0] == "z" else ((3, 2), (1,))
+        shapes.append([(d + (count, columns), dtype) for d in ((NZ, 2), second, third)])
     return shapes
 
 
@@ -478,18 +470,16 @@
 
     def moves(self, i, phase):
         t, seq, begin, count = self.plan.items[i]
-        me, total, got = self.me, self.total[t], self.got[t][phase]
+        me, total, got = self.me, self.total[t], self.got[i][phase]
         rows = pl.ds(begin, count)
         axis, done = seq[2 - phase], seq[3 - phase :]
         z = me.z if "z" in done else ALL_Z
         y = me.y if "y" in done else ALL_Y
         x = me.x if "x" in done else ALL_X
         if phase == 0:
-            lands = [got.at[ALL_Z, pl.ds(0, 2), rows, :]]
-        elif phase == 1:
-            lands = [got.at[k, pl.ds(0, got.shape[1]), rows, :] for k in range(got.shape[0])]
+            lands = [got]
         else:
-            lands = [got.at[k, rows, :] for k in range(got.shape[0])]
+            lands = [got.at[k] for k in range(got.shape[0])]
         if axis == "x":
             return [(total.at[z, y, 1 - me.x, rows, :], lands[0], me.to_x(), 0)]
         if axis == "y":
@@ -512,27 +502,27 @@
 
     def add(self, i, phase):
         t, seq, begin, count = self.plan.items[i]
-        me, total, got = self.me, self.total[t], self.got[t][phase]
+        me, total, got = self.me, self.total[t], self.got[i][phase]
         rows = pl.ds(begin, count)
         if phase == 0:
             for z in range(NZ):
                 for o in range(2):
                     at = (z, me.y, o) if seq[2] == "y" else (z, o, me.x)
-                    total[at + (rows,)] += got[z, o, rows]
+                    total[at + (rows,)] += got[z, o]
         elif phase == 1 and seq[1] != "z":
             for z in range(NZ):
-                total[z, me.y, me.x, rows] += got[0, z, rows]
+                total[z, me.y, me.x, rows] += got[0, z]
         elif phase == 1:
             for o in range(2):
                 at = (me.z, me.y, o) if seq[2] == "y" else (me.z, o, me.x)
                 part = total[at + (rows,)].astype(jnp.float32)
                 for k in range(3):
-                    part += got[k, o, rows].astype(jnp.float32)
+                    part += got[k, o].astype(jnp.float32)
                 total[at + (rows,)] = part.astype(total.dtype)
         else:
             part = total[me.z, me.y, me.x, rows].astype(jnp.float32)
             for k in range(got.shape[0]):
-                part += got[k, rows].astype(jnp.float32)
+                part += got[k].astype(jnp.float32)
             self.out[t][rows] = part
 
     def finish(self, i):
@@ -541,9 +531,34 @@
                 self.copy(i, phase, here, there, device, k).wait_send()
 
 
+FORWARD_SCRIPT = (
+    ("start", 12), ("start", 2), ("start", 0), ("start", 11), (0, 0), ("start", 1), (2, 0), ("start", 3),
+    ("start", 6), (1, 0), ("start", 5), (1, 1), (2, 1), ("start", 7), (6, 0), (5, 0), (0, 1), (3, 0),
+    ("start", 4), ("start", 16), (2, 2), ("start", 10), ("start", 17), (4, 0), (6, 1), (4, 1), (12, 0),
+    (1, 2), (3, 1), (5, 1), ("start", 8), (0, 2), (10, 0), ("start", 9), "norm", ("start", 15), "query",
+    (7, 0), (9, 0), (7, 1), (4, 2), ("start", 19), (5, 2), (17, 0), ("start", 14), (8, 0), (11, 0), (9, 1),
+    (14, 0), ("start", 13), (15, 0), (3, 2), (8, 1), ("start", 18), (6, 2), (12, 1), (14, 1), ("start", 20),
+    (7, 2), (11, 1), (10, 1), "key", (9, 2), (16, 0), "value", ("attend", 0), ("attend", 1), (18, 0), (13, 0),
+    (15, 1), (19, 0), (8, 2), (13, 1), (11, 2), (16, 1), ("attend", 2), (14, 2), (19, 1), ("attend", 3),
+    "out", (10, 2), (20, 0), (18, 1), (16, 2), (15, 2), (12, 2), (20, 1), (13, 2), (17, 1), ("mlp", 0),
+    (19, 2), ("mlp", 1), (18, 2), ("mlp", 2), (20, 2), (17, 2), ("mlp", 3), "down",
+)
+BACKWARD_SCRIPT = (
+    "down", ("hidden", 0), ("hidden", 1), "up", (3, 0), (1, 0), "gate", (0, 0), ("dh2", 0), ("dh2", 1),
+    (2, 0), "norm2", (0, 1), (1, 1), "heads", (3, 1), "out", (11, 0), (5, 0), (6, 0), (7, 0), ("attend", 0),
+    ("attend", 1), (4, 0), (10, 0), ("attend", 2), ("attend", 3), ("qkv", 0), (6, 1), (2, 1), (15, 0), (5, 1),
+    ("qkv", 1), (9, 0), (12, 0), (14, 0), (4, 1), (7, 1), (5, 2), (15, 1), ("qkv", 2), (1, 2), (2, 2),
+    (13, 0), (9, 1), "dh1", (14, 1), (16, 0), (12, 1), (6, 2), (19, 0), (17, 0), (16, 1), (10, 1), (8, 0),
+    (7, 2), "norm1", (13, 1), (9, 2), (19, 1), (16, 2), (12, 2), (18, 0), (8, 1), "gains", (18, 1), (17, 1),
+    (4, 2), (11, 1), (10, 2), (14, 2), (20, 0), (11, 2), (13, 2), (8, 2), (3, 2), (20, 1), (15, 2), (19, 2),
+    (0, 2), (18, 2), (17, 2), (20, 2),
+)
+
+
 EPS = 1e-05
 PAIR = 2 * HEAD_DIM
 SPAN = 2 * WINDOW
+GROUP = 8
 LOW = jnp.bfloat16
 F32 = jnp.float32
 
@@ -616,16 +631,15 @@
             copy.wait()
 
 
-FORWARD_ORDER = staged_order(8, (0, 2, 4))
-
-
 def forward_kernel(plan, *refs):
     n = len(plan.tensors)
     lens, x_in, dy_in, refs = refs[0], refs[1], refs[2], refs[3:]
-    shards, refs = refs[:n], refs[n:]
+    raw, refs = refs[:n], refs[n:]
     w_out, refs = refs[: n - 1], refs[n - 1 :]
     (mixed_o, q_o, k_o, v_o, p_o, x1_o, ha_o, ho_o, hm_o, hid_o, dact_o, act_o, dyh_o, gain_o), refs = refs[:14], refs[14:]
     bufs, refs = refs[:n], refs[n:]
+    gate_pad, up_pad, down_pad, refs = refs[0], refs[1], refs[2], refs[3:]
+    shards = list(raw[:5]) + [gate_pad, up_pad, down_pad]
     (gains, h1, q, kx, vx, probs, o, x1, h2, hid, act, dact, ha, ho, hm, hidt, mixed), refs = refs[:17], refs[17:]
     send, recv, own_sem, out_sem, rim_send, rim_recv, half_send, half_recv = refs
     rows, width = x_in.shape
@@ -648,10 +662,18 @@
         copies.start(mine, lanes(whole))
         to_partner(k, mine, lanes(whole))
 
-    for t in range(n):
+    for t in range(5):
         gather.own_copy(t).start()
-    for i in range(len(plan.items)):
-        gather.start(i, 0)
+    part, tile = raw[7].shape[0], down_pad.shape[0]
+    zero = jnp.zeros((raw[5].shape[0], tile - part), LOW)
+    for src, dst in ((raw[5], gate_pad), (raw[6], up_pad)):
+        value, pieces = src[...], []
+        for k in range(value.shape[1] // part):
+            pieces += [value[:, k * part : (k + 1) * part], zero]
+        dst[...] = jnp.concatenate(pieces, axis=1)
+    down_pad[...] = jnp.concatenate([raw[7][...], jnp.zeros((tile - part, down_pad.shape[1]), LOW)], axis=0)
+    for t in range(5, n):
+        gather.own_copy(t).start()
     for t in range(n):
         gather.own_copy(t).wait()
     half = dyh_o.shape[1]
@@ -739,15 +761,21 @@
         visible = (col >= row) & (col <= row + WINDOW) & (k_pos >= 0) & (doc(q_pos) == doc(k_pos))
         bias = jnp.where(visible, 0.0, -1e30)
         bias = jnp.concatenate([bias, bias], axis=0)
-        for p in range(HEADS // 2):
-            cols = slice(p * PAIR, (p + 1) * PAIR)
-            q2 = both_heads(q[at, cols])
-            s = mm_nt(q2, kx[over, cols]) * HEAD_DIM ** (-0.5) + bias
-            e = jnp.exp(s - jnp.max(s, axis=-1, keepdims=True))
-            prob = (e / jnp.sum(e, axis=-1, keepdims=True)).astype(LOW)
-            probs[at, 2 * p * SPAN : (2 * p + 1) * SPAN] = prob[:WINDOW]
-            probs[at, (2 * p + 1) * SPAN : (2 * p + 2) * SPAN] = prob[WINDOW:]
-            o[at, cols] = merge_heads(mm(prob, vx[over, cols])).astype(LOW)
+        for group in range(0, HEADS // 2, GROUP):
+            pairs = range(group, group + GROUP)
+            cols = [slice(p * PAIR, (p + 1) * PAIR) for p in pairs]
+            queries = [both_heads(q[at, c]) for c in cols]
+            keys, values = [kx[over, c] for c in cols], [vx[over, c] for c in cols]
+            scores = [mm_nt(q2, k) * HEAD_DIM ** (-0.5) + bias for q2, k in zip(queries, keys)]
+            tops = [jnp.max(s, axis=-1, keepdims=True) for s in scores]
+            exps = [jnp.exp(s - top) for s, top in zip(scores, tops)]
+            sums = [jnp.sum(e, axis=-1, keepdims=True) for e in exps]
+            weights = [(e * (1.0 / total)).astype(LOW) for e, total in zip(exps, sums)]
+            parts = [merge_heads(mm(w, v)).astype(LOW) for w, v in zip(weights, values)]
+            for p, c, w, part in zip(pairs, cols, weights, parts):
+                probs[at, 2 * p * SPAN : (2 * p + 1) * SPAN] = w[:WINDOW]
+                probs[at, (2 * p + 1) * SPAN : (2 * p + 2) * SPAN] = w[WINDOW:]
+                o[at, c] = part
 
     def attend_some(begin, count):
         def step(b, _):
@@ -818,43 +846,63 @@
             each_tile(columns, 256, body)
         copies.start(mixed, mixed_o)
 
-    blocks = rows // WINDOW
     whole = wide // 256
     rest = wide - whole * 256
-    work = [(0, first_norm), (1, do_query), (2, do_key), (3, do_value), (3, rims)]
-    work += [(3, functools.partial(attend_some, b, 2)) for b in range(0, blocks, 2)]
-    work += [(3, after_attention), (4, add_out)]
-    for side in range(2):
-        work += [(6, functools.partial(mlp_some, side, 0, 256, whole))]
-        work += [(6, functools.partial(mlp, side, whole * 256, rest))] if rest else []
-    work += [(6, after_mlp), (7, add_down)]
-    passed, done = set(), set()
-
-    def arrive(t):
-        if t in passed:
-            return
-        passed.add(t)
-        for i in plan.of_tensor[t]:
-            gather.wait(i, 3)
-        if t:
-            copies.start(bufs[t], w_out[t - 1])
-
-    for t, phase in FORWARD_ORDER:
-        for i in plan.of_tensor[t]:
+    quarter = rows // WINDOW // 4
+    passed = set()
+
+    def need(t):
+        for k in range(t + 1):
+            if k not in passed:
+                passed.add(k)
+                for i in plan.of_tensor[k]:
+                    gather.wait(i, 3)
+                if k:
+                    copies.start(bufs[k], w_out[k - 1])
+
+    def mlp_part(side, part):
+        need(6)
+        count = (whole + 1) // 2
+        if part == 0:
+            mlp_some(side, 0, 256, count)
+        else:
+            mlp_some(side, count * 256, 256, whole - count)
+            if rest:
+                mlp(side, whole * 256, rest)
+            if side == 1:
+                after_mlp()
+
+    def attend_part(k):
+        if k == 0:
+            rims()
+        attend_some(k * quarter, quarter)
+        if k == 3:
+            after_attention()
+
+    def with_weight(t, piece):
+        need(t)
+        piece()
+
+    work = {
+        "norm": lambda: with_weight(0, first_norm),
+        "query": lambda: with_weight(1, do_query),
+        "key": lambda: with_weight(2, do_key),
+        "value": lambda: with_weight(3, do_value),
+        "out": lambda: with_weight(4, add_out),
+        "down": lambda: with_weight(7, add_down),
+    }
+    for k in range(4):
+        work["attend", k] = functools.partial(attend_part, k)
+        work["mlp", k] = functools.partial(mlp_part, k // 2, k % 2)
+    for step in FORWARD_SCRIPT:
+        if step in work:
+            work[step]()
+        elif step[0] == "start":
+            gather.start(step[1], 0)
+        else:
+            i, phase = step
             gather.wait(i, phase)
             gather.start(i, phase + 1)
-        if phase == 2:
-            done.add(t)
-        for _ in range(2):
-            if work and all(k in done for k in range(work[0][0] + 1)) and not (phase == 2 and t == work[0][0]):
-                need, piece = work.pop(0)
-                for k in range(need + 1):
-                    arrive(k)
-                piece()
-    for need, piece in work:
-        for k in range(need + 1):
-            arrive(k)
-        piece()
     for i in range(len(plan.items)):
         gather.finish(i)
     for k, ref in ((0, kx), (1, vx)):
@@ -912,9 +960,10 @@
     outs = pl.pallas_call(
         functools.partial(forward_kernel, plan),
         out_shape=[shape(b, LOW) for b in bufs[1:]] + [shape(*s) for s in kept],
-        in_specs=[pl.BlockSpec(memory_space=pltpu.SMEM), inside, anywhere] + [anywhere] * n,
+        in_specs=[pl.BlockSpec(memory_space=pltpu.SMEM), inside, anywhere] + [anywhere] * (n - 3) + [inside] * 3,
         out_specs=[anywhere] * (n - 1 + len(kept)),
         scratch_shapes=[pltpu.VMEM(b, LOW) for b in bufs]
+        + [pltpu.VMEM(t[:2], LOW) for t in plan.tensors[5:]]
         + [pltpu.VMEM(*s) for s in scratch]
         + [dma((k, 4, 3)), dma((k, 4, 3)), dma((n,)), dma((24,)), dma((2,)), dma((2,)), dma((5,)), dma((5,))],
         compiler_params=pltpu.CompilerParams(
@@ -939,7 +988,7 @@
         for copy in self.copies(0, 0):
             copy.start()
 
-    def run(self, body):
+    def run(self, body, first=0, last=None):
         def step(j, _):
             slot = j % 2
 
@@ -953,21 +1002,7 @@
             body(j, slot)
             return 0
 
-        lax.fori_loop(0, self.count, step, 0)
-
-
-BACKWARD_EVENTS = {
-    "hidden": [],
-    "up": [(0, 0)],
-    "gate": [],
-    "dh2": [(0, 1), (1, 0)],
-    "norm2": [],
-    "out": [(0, 2), (2, 0)],
-    "attend": [(1, 1), (2, 1), (1, 2), (3, 0)],
-    "qkv": [(2, 2), (3, 1)],
-    "dh1": [(3, 2), (4, 0)],
-    "end": [(5, 0), (4, 1), (6, 0), (5, 1), (7, 0), (4, 2), (6, 1), (7, 1), (5, 2), (6, 2), (7, 2)],
-}
+        lax.fori_loop(first, self.count if last is None else last, step, 0)
 
 
 def backward_kernel(plan, *refs):
@@ -976,7 +1011,8 @@
     (x_h, dy_h, q_h, k_h, v_h, p_h, x1_h, ha_h, ho_h, hm_h, hid_h, dact_h, act_h, dyh_h, gains), refs = refs[:15], refs[15:]
     (gtok_o,), outs, refs = refs[:1], refs[1 : 1 + n], refs[1 + n :]
     total, refs = refs[:n], refs[n:]
-    got, refs = [refs[3 * t : 3 * t + 3] for t in range(n)], refs[3 * n :]
+    k = len(plan.items)
+    got, refs = [refs[3 * i : 3 * i + 3] for i in range(k)], refs[3 * k :]
     (da, db, kx, vx, dar, dbr, dxr_r, qr, kr, vr, dyh, turned, small, broad, dy, x1, dh, dxr, do), refs = refs[:19], refs[19:]
     (kc, vc, rim_k, rim_v, gain_sum, gain_other), refs = refs[:6], refs[6:]
     send, recv, load_sem, small_sem, broad_sem, turn_sem, half_send, half_recv, out_sem = refs
@@ -1033,14 +1069,6 @@
     get_x1 = load(x1_h, x1)
     get_k, get_v = load(k_h, kx), load(v_h, vx)
 
-    def events(name):
-        for t, phase in BACKWARD_EVENTS[name]:
-            for i in plan.of_tensor[t]:
-                scatter.wait(i, phase)
-                scatter.add(i, phase)
-                if phase < 2:
-                    scatter.start(i, phase + 1)
-
     def begin(t):
         for i in plan.of_tensor[t]:
             scatter.start(i, 0)
@@ -1049,19 +1077,14 @@
         row_count, column_count = plan.tensors[t][:2]
         total[t][z] = part.reshape(NY, NX, row_count, column_count).astype(total[t].dtype)
 
-    get_dyh.wait()
-
-    def down_body(z, slot):
-        put(0, z, mm(turned[slot, :tall], dyh[...]))
-
-    hid_tiles.run(down_body)
-    begin(0)
-    get_hm = load(hm_h, turned.at[0])
-    get_ho = load(ho_h, turned.at[1])
-    events("hidden")
-
-    for copy in (get_dy, get_dact, get_act):
-        copy.wait()
+    later = {}
+
+    def grad_down():
+        get_dyh.wait()
+        hid_tiles.run(lambda z, slot: put(0, z, mm(turned[slot, :tall], dyh[...])))
+        begin(0)
+        later["hm"] = load(hm_h, turned.at[0])
+        later["ho"] = load(ho_h, turned.at[1])
 
     def hidden_body(j, slot):
         part = mm_nt(dy[:, :columns], small[slot, 0, 0]) + mm_nt(dy[:, columns:], small[slot, 0, 1])
@@ -1069,11 +1092,17 @@
         da[:, at] = (part * da[:, at].astype(F32)).astype(LOW)
         db[:, at] = (part * db[:, at].astype(F32)).astype(LOW)
 
-    down_tiles.run(hidden_body)
-    out_tiles.prime()
-    got_db = to_partner(0, db.at[:, own(wide, 1)], dbr)
-    got_da = to_partner(1, da.at[:, own(wide, 1)], dar)
-    events("up")
+    def hidden(k):
+        middle = down_tiles.count // 2
+        if k == 0:
+            for copy in (get_dy, get_dact, get_act):
+                copy.wait()
+            down_tiles.run(hidden_body, 0, middle)
+            return
+        down_tiles.run(hidden_body, middle)
+        out_tiles.prime()
+        later["db"] = to_partner(0, db.at[:, own(wide, 1)], dbr)
+        later["da"] = to_partner(1, da.at[:, own(wide, 1)], dar)
 
     def weight_grad_to(t, slot, mine, theirs):
         row_count = plan.tensors[t][0] * NY * NX
@@ -1086,14 +1115,15 @@
         lax.fori_loop(0, NZ, step, 0)
         begin(t)
 
-    get_hm.wait()
-    got_db.wait_recv()
-    weight_grad_to(1, 0, lambda: db[:, own(wide)], dbr)
-    events("gate")
-    got_da.wait_recv()
-    weight_grad_to(2, 0, lambda: da[:, own(wide)], dar)
-    get_ha = load(ha_h, turned.at[0])
-    events("dh2")
+    def grad_up():
+        later["hm"].wait()
+        later["db"].wait_recv()
+        weight_grad_to(1, 0, lambda: db[:, own(wide)], dbr)
+
+    def grad_gate():
+        later["da"].wait_recv()
+        weight_grad_to(2, 0, lambda: da[:, own(wide)], dar)
+        later["ha"] = load(ha_h, turned.at[0])
 
     def dh2_body(j, slot):
         part = None
@@ -1103,13 +1133,17 @@
                 part = term if part is None else part + term
         dh[:, pl.ds(pl.multiple_of(j * tile, tile), tile)] = part
 
-    mlp_tiles.run(dh2_body)
-    for copy in halves[:2]:
-        copy.wait_send()
-    get_q = load(q_h, da.at[:, pl.ds(0, width)])
-    get_p = load(p_h, db.at[:, pl.ds(0, HEADS * SPAN)])
-    get_x = load(x_h, da.at[:, pl.ds(width, width)])
-    events("norm2")
+    def grad_norm2(k):
+        middle = mlp_tiles.count // 2
+        if k == 0:
+            mlp_tiles.run(dh2_body, 0, middle)
+            return
+        mlp_tiles.run(dh2_body, middle)
+        later["db"].wait_send()
+        later["da"].wait_send()
+        later["q"] = load(q_h, da.at[:, pl.ds(0, width)])
+        later["p"] = load(p_h, db.at[:, pl.ds(0, HEADS * SPAN)])
+        later["x"] = load(x_h, da.at[:, pl.ds(width, width)])
 
     def norm_grad(values, grad_norm, gain):
         inverse = lax.rsqrt(jnp.mean(values * values, axis=-1, keepdims=True) + EPS)
@@ -1118,9 +1152,6 @@
         back = inverse * scaled - values * (inverse * inverse * inverse) * mean_term
         return back, jnp.sum(values * inverse * grad_norm, axis=0, keepdims=True)
 
-    gain_sum[...] = jnp.zeros_like(gain_sum)
-    get_x1.wait()
-
     def norm2_body(at):
         back, gain_part = norm_grad(x1[at, :], dh[at, :], gains[1:2, :])
         gain_sum[1:2, :] += gain_part
@@ -1128,68 +1159,86 @@
         x1[at, :] = grad
         dxr[at, :] = grad.astype(LOW)
 
-    each_rows(rows, 64, norm2_body)
-    got_dxr = to_partner(2, dxr.at[:, own(columns, 1)], dxr_r)
-    events("out")
+    def norm2():
+        gain_sum[...] = jnp.zeros_like(gain_sum)
+        get_x1.wait()
+        each_rows(rows, 64, norm2_body)
+        later["dxr"] = to_partner(2, dxr.at[:, own(columns, 1)], dxr_r)
 
     def out_body(j, slot):
         part = mm_nt(dxr[:, :columns], small[slot, 0, 0]) + mm_nt(dxr[:, columns:], small[slot, 0, 1])
         do[:, pl.ds(pl.multiple_of(j * tile, tile), tile)] = part.astype(LOW)
 
-    out_tiles.run(out_body)
-    qkv_tiles.prime()
-    get_ho.wait()
-    got_dxr.wait_recv()
-    weight_grad_to(3, 1, lambda: dxr[:, own(columns)], dxr_r)
-    events("attend")
-
-    kc[...] = jnp.zeros_like(kc)
-    vc[...] = jnp.zeros_like(vc)
-    for copy in (get_q, get_p, get_k, get_v):
-        copy.wait()
+    def grad_heads():
+        out_tiles.run(out_body)
+        qkv_tiles.prime()
+
+    def grad_out():
+        later["ho"].wait()
+        later["dxr"].wait_recv()
+        weight_grad_to(3, 1, lambda: dxr[:, own(columns)], dxr_r)
+
     scale = HEAD_DIM ** (-0.5)
 
     def attend(b, _):
         at = pl.ds(pl.multiple_of(b * WINDOW, WINDOW), WINDOW)
         over = pl.ds(pl.multiple_of(b * WINDOW, WINDOW), SPAN)
-        for p in range(HEADS // 2):
-            cols = slice(p * PAIR, (p + 1) * PAIR)
-            q2, do2 = both_heads(da[at, cols]), both_heads(do[at, cols])
-            keys, values = kx[over, cols], vx[over, cols]
-            prob = jnp.concatenate(
-                [db[at, 2 * p * SPAN : (2 * p + 1) * SPAN], db[at, (2 * p + 1) * SPAN : (2 * p + 2) * SPAN]], axis=0
-            )
-            wide_prob = prob.astype(F32)
-            grad_prob = mm_nt(do2, values)
-            inner = jnp.sum(wide_prob * grad_prob, axis=-1, keepdims=True)
-            grad_score = (wide_prob * (grad_prob - inner)).astype(LOW)
-            da[at, cols] = (merge_heads(mm(grad_score, keys)) * scale).astype(LOW)
-            grad_keys = mm_tn(grad_score, q2) * scale
-            grad_values = mm_tn(prob, do2)
-            kx[at, cols] = (kc[:, cols] + grad_keys[:WINDOW]).astype(LOW)
-            vx[at, cols] = (vc[:, cols] + grad_values[:WINDOW]).astype(LOW)
-            kc[:, cols] = grad_keys[WINDOW:]
-            vc[:, cols] = grad_values[WINDOW:]
+        for group in range(0, HEADS // 2, GROUP):
+            pairs = range(group, group + GROUP)
+            cols = [slice(p * PAIR, (p + 1) * PAIR) for p in pairs]
+            queries, grads = [both_heads(da[at, c]) for c in cols], [both_heads(do[at, c]) for c in cols]
+            keys, values = [kx[over, c] for c in cols], [vx[over, c] for c in cols]
+            lows = [
+                jnp.concatenate([db[at, (2 * p + h) * SPAN : (2 * p + h + 1) * SPAN] for h in range(2)], axis=0)
+                for p in pairs
+            ]
+            carry_k, carry_v = [kc[:, c] for c in cols], [vc[:, c] for c in cols]
+            probs = [low.astype(F32) for low in lows]
+            grad_probs = [mm_nt(g, v) for g, v in zip(grads, values)]
+            grad_values = [mm_tn(low, g) for low, g in zip(lows, grads)]
+            inners = [jnp.sum(p * g, axis=-1, keepdims=True) for p, g in zip(probs, grad_probs)]
+            scores = [(p * (g - i)).astype(LOW) for p, g, i in zip(probs, grad_probs, inners)]
+            grad_queries = [(merge_heads(mm(s, k)) * scale).astype(LOW) for s, k in zip(scores, keys)]
+            grad_keys = [mm_tn(s, q2) * scale for s, q2 in zip(scores, queries)]
+            new_k = [(old + g[:WINDOW]).astype(LOW) for old, g in zip(carry_k, grad_keys)]
+            new_v = [(old + g[:WINDOW]).astype(LOW) for old, g in zip(carry_v, grad_values)]
+            for c, gq, gk, gv, nk, nv in zip(cols, grad_queries, grad_keys, grad_values, new_k, new_v):
+                da[at, c] = gq
+                kx[at, c] = nk
+                vx[at, c] = nv
+                kc[:, c] = gk[WINDOW:]
+                vc[:, c] = gv[WINDOW:]
         return 0
 
-    lax.fori_loop(0, rows // WINDOW, attend, 0)
-    rims = [to_partner(3, kx.at[pl.ds(0, WINDOW), :], rim_k), to_partner(4, vx.at[pl.ds(0, WINDOW), :], rim_v)]
-    got_q = to_partner(5, da.at[:, own(columns, 1)], qr)
-    events("qkv")
-    got_q.wait_recv()
-    get_ha.wait()
-    weight_grad_to(4, 0, lambda: da[:, own(columns)], qr)
-    for copy, ref, carry, rim in ((rims[0], kx, kc, rim_k), (rims[1], vx, vc, rim_v)):
-        copy.wait_recv()
-        ref[pl.ds(rows, WINDOW), :] = (carry[...] + rim[...].astype(F32)).astype(LOW)
-    later = pl.ds(WINDOW, rows)
-    got_k = to_partner(6, kx.at[later, own(columns, 1)], kr)
-    got_v = to_partner(7, vx.at[later, own(columns, 1)], vr)
-    got_k.wait_recv()
-    weight_grad_to(5, 0, lambda: kx[later, own(columns)], kr)
-    got_v.wait_recv()
-    weight_grad_to(6, 0, lambda: vx[later, own(columns)], vr)
-    events("dh1")
+    def attend_part(k):
+        quarter = rows // WINDOW // 4
+        if k == 0:
+            kc[...] = jnp.zeros_like(kc)
+            vc[...] = jnp.zeros_like(vc)
+            for copy in (later["q"], later["p"], get_k, get_v):
+                copy.wait()
+        lax.fori_loop(k * quarter, (k + 1) * quarter, attend, 0)
+        if k == 0:
+            later["rim"] = [
+                to_partner(3, kx.at[pl.ds(0, WINDOW), :], rim_k),
+                to_partner(4, vx.at[pl.ds(0, WINDOW), :], rim_v),
+            ]
+        if k == 3:
+            for copy, ref, carry, rim in ((later["rim"][0], kx, kc, rim_k), (later["rim"][1], vx, vc, rim_v)):
+                copy.wait_recv()
+                ref[pl.ds(rows, WINDOW), :] = (carry[...] + rim[...].astype(F32)).astype(LOW)
+            later["dq"] = to_partner(5, da.at[:, own(columns, 1)], qr)
+            later["dk"] = to_partner(6, kx.at[own_rows, own(columns, 1)], kr)
+            later["dv"] = to_partner(7, vx.at[own_rows, own(columns, 1)], vr)
+
+    own_rows = pl.ds(WINDOW, rows)
+
+    def grad_qkv(k):
+        if k == 0:
+            later["ha"].wait()
+        later[("dq", "dk", "dv")[k]].wait_recv()
+        mine = (lambda: da[:, own(columns)], lambda: kx[own_rows, own(columns)], lambda: vx[own_rows, own(columns)])[k]
+        weight_grad_to(4 + k, 0, mine, (qr, kr, vr)[k])
 
     def dh1_body(j, slot):
         part = None
@@ -1200,30 +1249,61 @@
                 part = term if part is None else part + term
         dh[:, pl.ds(pl.multiple_of(j * tile, tile), tile)] = part
 
-    qkv_tiles.run(dh1_body)
-    get_x.wait()
+    def grad_norm1():
+        qkv_tiles.run(dh1_body)
 
     def norm1_body(at):
         back, gain_part = norm_grad(da[at, pl.ds(width, width)].astype(F32), dh[at, :], gains[0:1, :])
         gain_sum[0:1, :] += gain_part
         x1[at, :] = x1[at, :] + back
 
-    each_rows(rows, 64, norm1_body)
     give = pltpu.make_async_copy(x1, gtok_o, out_sem)
-    give.start()
-    got_gain = to_partner(8, gain_sum, gain_other)
-    got_gain.wait_recv()
-    lanes = plan.tensors[7][1]
-    for c in range(NZ * NY * NX):
-        at = slice(c // 2 * lanes, (c // 2 + 1) * lanes)
-        total[7][c // 4, c // 2 % 2, c % 2] = gain_sum[:, at] + gain_other[:, at]
-    begin(7)
-    events("end")
+
+    def norm1():
+        later["x"].wait()
+        each_rows(rows, 64, norm1_body)
+        give.start()
+        later["gain"] = to_partner(8, gain_sum, gain_other)
+
+    def grad_gains():
+        later["gain"].wait_recv()
+        lanes = plan.tensors[7][1]
+        for c in range(NZ * NY * NX):
+            at = slice(c // 2 * lanes, (c // 2 + 1) * lanes)
+            total[7][c // 4, c // 2 % 2, c % 2] = gain_sum[:, at] + gain_other[:, at]
+        begin(7)
+
+    work = {
+        "down": grad_down,
+        "up": grad_up,
+        "gate": grad_gate,
+        "norm2": norm2,
+        "heads": grad_heads,
+        "out": grad_out,
+        "dh1": grad_norm1,
+        "norm1": norm1,
+        "gains": grad_gains,
+    }
+    for k in range(4):
+        work["attend", k] = functools.partial(attend_part, k)
+    for k in range(3):
+        work["qkv", k] = functools.partial(grad_qkv, k)
+    for k in range(2):
+        work["hidden", k] = functools.partial(hidden, k)
+        work["dh2", k] = functools.partial(grad_norm2, k)
+    for step in BACKWARD_SCRIPT:
+        if step in work:
+            work[step]()
+            continue
+        i, phase = step
+        scatter.wait(i, phase)
+        scatter.add(i, phase)
+        if phase < 2:
+            scatter.start(i, phase + 1)
     for i in range(len(plan.items)):
         scatter.finish(i)
-    for k, copy in enumerate(halves):
-        if k >= 2:
-            copy.wait_send()
+    for copy in halves[2:]:
+        copy.wait_send()
     give.wait()
 
 
@@ -1261,7 +1341,7 @@
         ((8, width), F32),
         ((8, width), F32),
     ]
-    totals = [((NZ, NY, NX) + t[:2], t[4]) for t in plan.tensors]
+    totals = [((NZ, NY, NX) + t[:2], t[2]) for t in plan.tensors]
     got = [shape for shapes in got_shapes(plan) for shape in shapes]
     dma = pltpu.SemaphoreType.DMA
     return pl.pallas_call(
@@ -1279,14 +1359,64 @@
     )(*ws, tokens, cotangent, *acts)
 
 
-def pad_columns(w, part, tile):
-    rows = w.shape[0]
-    return jnp.pad(w.reshape(rows, -1, part), ((0, 0), (0, 0), (0, tile - part))).reshape(rows, -1)
-
-
-def unpad_columns(w, part, tile):
-    rows = w.shape[0]
-    return w.reshape(rows, -1, tile)[:, :, :part].reshape(rows, -1)
+def finish_kernel(*refs):
+    n = 10
+    ins, outs, held, made = refs[:n], refs[n : 2 * n + 1], refs[2 * n + 1 : 3 * n + 1], refs[3 * n + 1 : 4 * n + 2]
+    sem_in, sem_out = refs[4 * n + 2 :]
+    gets = [pltpu.make_async_copy(src, dst, sem_in.at[k]) for k, (src, dst) in enumerate(zip(ins, held))]
+    for copy in gets:
+        copy.start()
+    puts = []
+
+    def put(k, src):
+        copy = pltpu.make_async_copy(src, outs[k], sem_out.at[k])
+        copy.start()
+        puts.append(copy)
+
+    down, up, gate, out, query, key, value, gain = held[2:]
+    for copy in gets[2:]:
+        copy.wait()
+    for k, src in ((2, query), (3, key), (4, value), (5, out)):
+        put(k, src)
+    rows, part, tile = query.shape[0], outs[8].shape[0], down.shape[0]
+    made[8][...] = down[...][:part]
+    put(8, made[8])
+    for k, src in ((6, gate), (7, up)):
+        values = src[...]
+        made[k][...] = jnp.concatenate(
+            [values[:, j * tile : j * tile + part] for j in range(values.shape[1] // tile)], axis=1
+        )
+        put(k, made[k])
+    both = gain[...]
+    own = jnp.where(lax.axis_index("dp") % 2 == 0, both[:, :rows], both[:, rows:])
+    made[9][...] = own[0:1]
+    made[10][...] = own[1:2]
+    put(9, made[9])
+    put(10, made[10])
+    for k in range(2):
+        gets[k].wait()
+        put(k, held[k])
+    for copy in puts:
+        copy.wait()
+
+
+def finish_all(mixed, tokens, sums, w_query, w_gate, w_down):
+    anywhere = pl.BlockSpec(memory_space=pl.ANY)
+    shape = jax.ShapeDtypeStruct
+    outs = [shape(mixed.shape, mixed.dtype), shape(tokens.shape, F32)]
+    outs += [shape(w_query.shape, F32)] * 4 + [shape(w_gate.shape, F32)] * 2 + [shape(w_down.shape, F32)]
+    outs += [shape((1, w_query.shape[0]), F32)] * 2
+    ins = [mixed, tokens, *sums]
+    return pl.pallas_call(
+        finish_kernel,
+        out_shape=outs,
+        in_specs=[anywhere] * len(ins),
+        out_specs=[anywhere] * len(outs),
+        scratch_shapes=[pltpu.VMEM(a.shape, a.dtype) for a in ins + outs]
+        + [pltpu.SemaphoreType.DMA((len(ins),)), pltpu.SemaphoreType.DMA((len(outs),))],
+        compiler_params=pltpu.CompilerParams(vmem_limit_bytes=62 * 2**20),
+        name="finish_all",
+    )(*ins)
 
 
 def kinds(w_query, w_gate, w_down):
@@ -1294,23 +1424,27 @@
     part = w_down.shape[0]
     tile = -(-part // 16) * 16
     wide = w_gate.shape[1] // part * tile
-    first = -(-tile // 32) * 16
-    halves = (rows // 2, rows // 2)
+    half, part16 = rows // 2, rows // 4
+    long, short = -(-tile // 64) * 16, tile - 3 * (-(-tile // 64) * 16)
+
+    def cuts(kinds, counts):
+        return tuple(zip(kinds, counts, strict=True))
+
     return {
-        "square": (rows, columns, "zf", halves, LOW),
-        "square_m": (rows, columns, "zm", halves, LOW),
-        "broad": (rows, wide, "zf", halves, LOW),
-        "tall": (tile, columns, "zm", (first, tile - first), LOW),
-        "gain": (16, 2 * rows, "zf", (16,), LOW),
-        "gain_grad": (8, 2 * rows, "zf", (8,), F32),
+        "square": (rows, columns, LOW, cuts(("zfx", "zfy"), (half, half))),
+        "broad": (rows, wide, LOW, cuts(("zfx", "zfy", "zmx", "zmy"), (part16,) * 4)),
+        "broad_f": (rows, wide, LOW, cuts(("zfx", "zfy", "zfx", "zfy"), (part16,) * 4)),
+        "tall": (tile, columns, LOW, cuts(("zfx", "zfy", "zmx", "zmy"), (long, long, long, short))),
+        "gain": (16, 2 * rows, LOW, cuts(("zfx",), (16,))),
+        "gain_grad": (8, 2 * rows, F32, cuts(("zfx",), (8,))),
     }
 
 
 def gather_plan(w_query, w_key, w_value, w_out, w_gate, w_up, w_down, gain_attn, gain_mlp):
     kind = kinds(w_query, w_gate, w_down)
-    names = ("gain", "square", "square", "square_m", "square", "broad", "broad", "tall")
+    names = ("gain", "square", "square", "square", "square", "broad", "broad", "tall")
     plan = Plan([kind[name] for name in names])
-    rows, part, tile = w_query.shape[0], w_down.shape[0], kind["tall"][0]
+    rows = w_query.shape[0]
     both = jnp.stack([gain_attn, gain_mlp])
     left = jnp.pad(both, ((0, 14), (0, rows)))
     right = jnp.pad(both, ((0, 14), (rows, 0)))
@@ -1321,9 +1455,9 @@
         w_key,
         w_value,
         w_out,
-        pad_columns(w_gate, part, tile),
-        pad_columns(w_up, part, tile),
-        jnp.pad(w_down, ((0, tile - part), (0, 0))),
+        w_gate,
+        w_up,
+        w_down,
     ]
     return plan, shards
 
@@ -1346,24 +1480,11 @@
     ws, acts = forward_all(plan, seq_lengths, tokens, cotangent, shards)
     ws = [w.reshape(2, -1, w.shape[-1]) for w in ws]
     kind = kinds(w_query, w_gate, w_down)
-    names = ("tall", "broad", "broad", "square", "square", "square", "square_m", "gain_grad")
+    names = ("tall", "broad_f", "broad", "square", "square", "square", "square", "gain_grad")
     back = Plan([kind[name] for name in names])
     grad_tokens, *sums = backward_all(back, ws, tokens, cotangent, acts[1:])
-    rows, part, tile = w_query.shape[0], w_down.shape[0], kind["tall"][0]
-    own = lax.dynamic_slice_in_dim(sums[7], (lax.axis_index("dp") % 2) * rows, rows, 1)
-    return (
-        acts[0],
-        grad_tokens,
-        sums[4],
-        sums[5],
-        sums[6],
-        sums[3],
-        unpad_columns(sums[2], part, tile),
-        unpad_columns(sums[1], part, tile),
-        sums[0][:part],
-        own[0],
-        own[1],
-    )
+    outs = finish_all(acts[0], grad_tokens, sums, w_query, w_gate, w_down)
+    return (*outs[:9], outs[9].reshape(-1), outs[10].reshape(-1))
 
 
 def solution(mesh):

time: 349 us -> 289 us (0.83)
  Pallas kernels: 327 us -> 286 us
  local copies, waits for them, and re-layouts: 19.2 us -> 0 us
    pallas_call x1, Pallas kernels: 176 us -> 147 us  [backward_all(): pl.pallas_call(functools.partial(backward_kernel, plan), out_shape=[jax.S...]
    pallas_call x1, Pallas kernels: 150 us -> 134 us  [forward_all(): pl.pallas_call(functools.partial(forward_kernel, plan), out_shape=[shape(...]
    reshape x8 -> x0, local copies, waits for them, and re-layouts: 9.29 us -> none  [the longest x4 4.78 us: unpad_columns(): return w.reshape(rows, -1, tile)[:, :, :part].reshape(rows, -1)]
    unnamed x19 -> x0, local copies, waits for them, and re-layouts: 6.96 us -> none
    pallas_call x0 -> x1, Pallas kernels: none -> 4.79 us  [finish_all(): pl.pallas_call(finish_kernel, out_shape=outs, in_specs=[anywhere] * len(i...]
where the time goes in v3:
time: 289 us; the launch traced here: 288 us
  Pallas kernels  286 us (99%)
    pallas_call x1, Pallas kernels, backward_all(): pl.pallas_call(functools.partial(backward_kernel, plan), out_shape=[jax.S...  147 us
    pallas_call x1, Pallas kernels, forward_all(): pl.pallas_call(functools.partial(forward_kernel, plan), out_shape=[shape(...  134 us

profile of v3, /device:TPU:0, one launch (start us, length us, event | category | flops | bytes accessed | tf_op | source)
XLA Modules:
  0.0 288.2 jit_solution(2579923901942108531)
XLA Ops:
  0.7 0.7 pad_maximum_fusion
  1.3 0.7 pad_select_fusion.refs_3_
  2.0 134.2 %forward_all.1 = (bf16[2,4,2,2,64,512]{5,4,3,2,1,0:T(8,128)(2,1)}, bf16[2,4,2,2,64,512]{5,4,3,2,1,0:T(8,128)(2,1)}, bf16[2,4,2,2,64,512]{5,4,3,2,1,0:T(8,128)(2,...) custom-call(s32[1,3]{1,0:T(1,128)} %refs_0_.1, ...), custom_call_target="tpu_custom_call" | custom-call | tf_op jit(solution)/shard_map/forward_all/pallas_call | solution.py:960
  136.2 147.0 %backward_all.1 = (f32[512,1024]{1,0:T(8,128)}, f32[176,512]{1,0:T(8,128)}, f32[64,1408]{1,0:T(8,128)}, f32[64,1408]{1,0:T(8,128)}, f32[64,512]{1,0:T(8,128)}, /...) custom-call(bf16[2,1024,512]{2,1,0:T(8,128)(2,1)} %bitcast.14, ...), custom_call_target="tpu_custom_call" | custom-call | tf_op jit(solution)/shard_map/backward_all/pallas_call | solution.py:1347
  283.2 4.8 %finish_all.1 = (bf16[512,1024]{1,0:T(8,128)(2,1)}, f32[512,1024]{1,0:T(8,128)}, f32[64,512]{1,0:T(8,128)}, f32[64,512]{1,0:T(8,128)}, f32[64,512]{1,0:T(8,128)}...) custom-call(bf16[512,1024]{1,0:T(8,128)(2,1)} %get-tuple-element.52., ...), custom_call_target="tpu_custom_call" | custom-call | tf_op jit(solution)/shard_map/finish_all/pallas_call | solution.py:1410

commit v4 on v0

--- a/solution.py
+++ b/solution.py
@@ -1,6 +1,10 @@
+import functools
+
 import jax
 import jax.numpy as jnp
 from jax import lax
+from jax.experimental import pallas as pl
+from jax.experimental.pallas import tpu as pltpu
 from jax.sharding import PartitionSpec as P
 
 HEADS = 16
@@ -54,7 +58,7 @@
     return jnp.einsum("td,tf->df", inputs, grad_rows, preferred_element_type=jnp.float32)
 
 
-def shards(
+def plain_block(
     tokens,
     seq_lengths,
     w_query,
@@ -344,7 +348,1085 @@
     )
 
 
+SCRIPT = (
+    ("start", 16), ("start", 19), ("start", 11), ("start", 0), ("start", 2), ("start", 12), ("start", 15),
+    ("start", 3), (0, 0, 0), ("start", 20), ("start", 13), (0, 3, 0), ("start", 4), (0, 2, 0), (0, 13, 0),
+    ("start", 1), ("start", 7), (0, 2, 1), (0, 3, 1), (0, 4, 0), ("start", 10), (0, 1, 0), ("start", 14),
+    ("start", 5), (0, 13, 1), (0, 0, 1), (0, 4, 1), (0, 7, 0), (0, 2, 2), (0, 10, 0), ("start", 6), (0, 5, 0),
+    ("start", 17), (0, 14, 0), (0, 10, 1), ("start", 9), (0, 4, 2), (0, 1, 1), (0, 15, 0), (0, 14, 1),
+    (0, 5, 1), (0, 6, 0), (0, 9, 0), (0, 12, 0), (0, 15, 1), (0, 6, 1), ("start", 8), (0, 0, 2), (0, 7, 1),
+    (0, 1, 2), (0, 3, 2), "norm", (0, 11, 0), (0, 12, 1), (0, 8, 0), (0, 13, 2), (0, 5, 2), "key", (0, 6, 2),
+    "query", (0, 17, 0), (0, 16, 0), (0, 11, 1), "value", (0, 8, 1), ("see", 0), (0, 7, 2), (0, 12, 2),
+    (0, 14, 2), (0, 9, 1), ("start", 18), (0, 16, 1), ("see", 1), (0, 8, 2), (0, 11, 2), (0, 20, 0),
+    ("see", 2), (0, 15, 2), (0, 18, 0), ("see", 3), (0, 19, 0), (0, 10, 2), (0, 17, 1), (0, 16, 2), (0, 9, 2),
+    "project", ("mlp", 0), (0, 18, 1), ("mlp", 1), ("mlp", 2), ("mlp", 3), (0, 19, 1), (0, 20, 1), (0, 17, 2),
+    ("mlp", 4), ("mlp", 5), "down", (0, 19, 2), (0, 20, 2), (0, 18, 2), "mix", ("hidden", 0), (1, 1, 0),
+    ("hidden", 1), (1, 2, 0), (1, 3, 0), "up", ("dh2", 0), "gate", (1, 2, 1), (1, 2, 2), (1, 1, 1),
+    ("dh2", 1), (1, 3, 1), "norm2", "heads", ("attend", 0), (1, 5, 0), ("attend", 1), (1, 4, 0),
+    ("attend", 2), ("attend", 3), (1, 8, 0), (1, 7, 0), (1, 4, 1), (1, 9, 0), (1, 11, 0), (1, 5, 1),
+    (1, 6, 0), "out", (1, 8, 1), (1, 6, 1), (1, 1, 2), ("qkv", 0), (1, 7, 1), "dh1", (1, 11, 1), (1, 9, 1),
+    (1, 10, 0), "norm1", (1, 15, 0), (1, 13, 0), (1, 12, 0), (1, 10, 1), (1, 0, 0), (1, 14, 0), ("qkv", 1),
+    "gains", (1, 12, 1), (1, 13, 1), (1, 15, 1), (1, 14, 1), ("qkv", 2), (1, 9, 2), (1, 16, 0), (1, 20, 0),
+    (1, 5, 2), (1, 0, 1), (1, 17, 0), (1, 20, 1), (1, 16, 1), (1, 18, 0), (1, 6, 2), (1, 4, 2), (1, 15, 2),
+    (1, 19, 0), (1, 17, 1), (1, 13, 2), (1, 8, 2), (1, 18, 1), (1, 16, 2), (1, 19, 1), (1, 7, 2), (1, 0, 2),
+    (1, 3, 2), (1, 14, 2), (1, 20, 2), (1, 10, 2), (1, 11, 2), (1, 12, 2), (1, 17, 2), (1, 18, 2), (1, 19, 2),
+)
+
+
+MESH = pl.DeviceIdType.MESH
+NZ, NY, NX = 4, 2, 2
+SEQUENCE = {"zfx": "zxy", "zfy": "zyx", "zmx": "xzy", "zmy": "yzx"}
+ALL_Z, ALL_Y, ALL_X = pl.ds(0, NZ), pl.ds(0, NY), pl.ds(0, NX)
+
+
+class Plan:
+    def __init__(self, tensors):
+        self.tensors = tensors
+        self.items, self.of_tensor = [], []
+        for t, (_, _, _, cuts) in enumerate(tensors):
+            begin, mine = 0, []
+            for kind, count in cuts:
+                mine.append(len(self.items))
+                self.items.append((t, SEQUENCE[kind], begin, count))
+                begin += count
+            self.of_tensor.append(mine)
+
+
+class Place:
+    def __init__(self):
+        self.c, self.s = lax.axis_index("dp"), lax.axis_index("seq")
+        self.z, self.y, self.x = self.c // 4, (self.c // 2) % 2, self.c % 2
+
+    def at(self, z, y, x):
+        return (z * 4 + y * 2 + x, self.s)
+
+    def to_x(self):
+        return self.at(self.z, self.y, 1 - self.x)
+
+    def to_y(self):
+        return self.at(self.z, 1 - self.y, self.x)
+
+    def to_z(self, step):
+        return self.at((self.z + step) % NZ, self.y, self.x)
+
+    def to_core(self):
+        return (self.c, 1 - self.s)
+
+    def greet(self):
+        barrier = pltpu.get_barrier_semaphore()
+        peers = [self.to_x(), self.to_y(), self.to_core()] + [self.to_z(k) for k in (1, 2, 3)]
+        for peer in peers:
+            pl.semaphore_signal(barrier, inc=1, device_id=peer, device_id_type=MESH)
+        pl.semaphore_wait(barrier, len(peers))
+
+
+def remote(src, dst, send, recv, device):
+    return pltpu.make_async_remote_copy(
+        src_ref=src, dst_ref=dst, send_sem=send, recv_sem=recv, device_id=device, device_id_type=MESH
+    )
+
+
+def slots(seq, count):
+    firsts, used = [], 0
+    for phase in range(count):
+        firsts.append(used)
+        used += 3 if phase < 3 and seq[phase] == "z" else 1
+    return firsts
+
+
+class Gather:
+    def __init__(self, plan, place, shards, bufs, send, recv, local):
+        self.plan, self.me, self.shards, self.bufs = plan, place, shards, bufs
+        self.send, self.recv, self.local = send, recv, local
+
+    def own_copy(self, t):
+        me = self.me
+        return pltpu.make_async_copy(
+            self.shards[t], self.bufs[t].at[me.s, me.z, me.y, me.x], self.local.at[t]
+        )
+
+    def moves(self, i, phase):
+        t, seq, begin, count = self.plan.items[i]
+        me, buf = self.me, self.bufs[t]
+        rows = pl.ds(begin, count)
+
+        def view(z, y, x, half=me.s):
+            return buf.at[half, z, y, x, rows, :]
+
+        if phase == 3:
+            whole = view(ALL_Z, ALL_Y, ALL_X)
+            return [(whole, whole, me.to_core(), view(ALL_Z, ALL_Y, ALL_X, 1 - me.s), 0)]
+        done, axis = seq[:phase], seq[phase]
+        z = ALL_Z if "z" in done else me.z
+        y = ALL_Y if "y" in done else me.y
+        x = ALL_X if "x" in done else me.x
+        there = view(z, y, x)
+        here = self.shards[t].at[rows, :] if phase == 0 else there
+        if axis == "x":
+            return [(here, there, me.to_x(), view(z, y, 1 - me.x), 0)]
+        if axis == "y":
+            return [(here, there, me.to_y(), view(z, 1 - me.y, x), 0)]
+        return [
+            (here, there, me.to_z(k), view((me.z + NZ - k) % NZ, y, x), k - 1) for k in (1, 2, 3)
+        ]
+
+    def copy(self, i, phase, src, dst, device, k):
+        at = 6 * i + slots(self.plan.items[i][1], 4)[phase] + k
+        return remote(src, dst, self.send.at[at], self.recv.at[at], device)
+
+    def start(self, i, phase):
+        for here, there, device, _, k in self.moves(i, phase):
+            self.copy(i, phase, here, there, device, k).start()
+
+    def wait(self, i, phase):
+        for _, _, device, arrived, k in self.moves(i, phase):
+            self.copy(i, phase, arrived, arrived, device, k).wait_recv()
+
+    def finish(self, i):
+        for phase in range(4):
+            for here, there, device, _, k in self.moves(i, phase):
+                self.copy(i, phase, here, there, device, k).wait_send()
+
+
+def got_shapes(plan):
+    shapes = []
+    for t, seq, _, count in plan.items:
+        _, columns, dtype, _ = plan.tensors[t]
+        second, third = ((1, NZ), (3,)) if seq[0] == "z" else ((3, 2), (1,))
+        shapes.append([(d + (count, columns), dtype) for d in ((NZ, 2), second, third)])
+    return shapes
+
+
+class Scatter:
+    def __init__(self, plan, place, total, got, out, send, recv):
+        self.plan, self.me, self.total, self.got, self.out = plan, place, total, got, out
+        self.send, self.recv = send, recv
+
+    def moves(self, i, phase):
+        t, seq, begin, count = self.plan.items[i]
+        me, total, got = self.me, self.total[t], self.got[i][phase]
+        rows = pl.ds(begin, count)
+        axis, done = seq[2 - phase], seq[3 - phase :]
+        z = me.z if "z" in done else ALL_Z
+        y = me.y if "y" in done else ALL_Y
+        x = me.x if "x" in done else ALL_X
+        if phase == 0:
+            lands = [got]
+        else:
+            lands = [got.at[k] for k in range(got.shape[0])]
+        if axis == "x":
+            return [(total.at[z, y, 1 - me.x, rows, :], lands[0], me.to_x(), 0)]
+        if axis == "y":
+            return [(total.at[z, 1 - me.y, x, rows, :], lands[0], me.to_y(), 0)]
+        return [
+            (total.at[(me.z + k) % NZ, y, x, rows, :], lands[k - 1], me.to_z(k), k - 1)
+            for k in (1, 2, 3)
+        ]
+
+    def copy(self, i, phase, src, dst, device, k):
+        at = 5 * i + slots(self.plan.items[i][1][::-1], 3)[phase] + k
+        return remote(src, dst, self.send.at[at], self.recv.at[at], device)
+
+    def start(self, i, phase):
+        for here, there, device, k in self.moves(i, phase):
+            self.copy(i, phase, here, there, device, k).start()
+
+    def wait(self, i, phase):
+        for here, there, device, k in self.moves(i, phase):
+            self.copy(i, phase, there, there, device, k).wait_recv()
+
+    def add(self, i, phase):
+        t, seq, begin, count = self.plan.items[i]
+        me, total, got = self.me, self.total[t], self.got[i][phase]
+        rows = pl.ds(begin, count)
+        if phase == 0:
+            for z in range(NZ):
+                for o in range(2):
+                    at = (z, me.y, o) if seq[2] == "y" else (z, o, me.x)
+                    total[at + (rows,)] += got[z, o]
+        elif phase == 1 and seq[1] != "z":
+            for z in range(NZ):
+                total[z, me.y, me.x, rows] += got[0, z]
+        elif phase == 1:
+            for o in range(2):
+                at = (me.z, me.y, o) if seq[2] == "y" else (me.z, o, me.x)
+                part = total[at + (rows,)].astype(jnp.float32)
+                for k in range(3):
+                    part += got[k, o].astype(jnp.float32)
+                total[at + (rows,)] = part.astype(total.dtype)
+        else:
+            part = total[me.z, me.y, me.x, rows].astype(jnp.float32)
+            for k in range(got.shape[0]):
+                part += got[k].astype(jnp.float32)
+            self.out[t][rows] = part
+
+    def finish(self, i):
+        for phase in range(3):
+            for here, there, device, k in self.moves(i, phase):
+                self.copy(i, phase, here, there, device, k).wait_send()
+
+
+EPS = 1e-05
+PAIR = 2 * HEAD_DIM
+SPAN = 2 * WINDOW
+LOW = jnp.bfloat16
+F32 = jnp.float32
+
+
+def mm(left, right):
+    return jnp.dot(left, right, preferred_element_type=F32)
+
+
+def mm_nt(left, right):
+    return lax.dot_general(left, right, (((1,), (1,)), ((), ())), preferred_element_type=F32)
+
+
+def mm_tn(left, right):
+    return lax.dot_general(left, right, (((0,), (0,)), ((), ())), preferred_element_type=F32)
+
+
+def column_tiles(columns, size):
+    full = columns // size
+    tiles = [(0, size, full)]
+    if columns % size:
+        tiles.append((full * size, columns % size, 1))
+    return tiles
+
+
+def each_tile(columns, size, body):
+    for begin, width, count in column_tiles(columns, size):
+        if count == 1:
+            body(begin, width)
+        else:
+
+            def step(j, _, begin=begin, width=width):
+                body(pl.multiple_of(begin + j * width, 128), width)
+                return 0
+
+            lax.fori_loop(0, count, step, 0)
+
+
+def each_rows(rows, size, body):
+    def step(j, _):
+        body(pl.ds(pl.multiple_of(j * size, size), size))
+        return 0
+
+    lax.fori_loop(0, rows // size, step, 0)
+
+
+def both_heads(block):
+    first = lax.broadcasted_iota(jnp.int32, block.shape, 1) < HEAD_DIM
+    zero = jnp.zeros_like(block)
+    return jnp.concatenate([jnp.where(first, block, zero), jnp.where(first, zero, block)], axis=0)
+
+
+def merge_heads(stacked):
+    rows = stacked.shape[0] // 2
+    first = lax.broadcasted_iota(jnp.int32, (rows, PAIR), 1) < HEAD_DIM
+    return jnp.where(first, stacked[:rows], stacked[rows:])
+
+
+VMEM_LIMIT = 64 * 2**20
+
+
+class Stream:
+    def __init__(self, count, sems, fetch):
+        self.count, self.sems, self.fetch = count, sems, fetch
+
+    def copies(self, j, slot):
+        return [
+            pltpu.make_async_copy(src, dst, self.sems.at[slot, k])
+            for k, (src, dst) in enumerate(self.fetch(j, slot))
+        ]
+
+    def prime(self):
+        for copy in self.copies(0, 0):
+            copy.start()
+
+    def run(self, body, first=0, last=None):
+        def step(j, _):
+            slot = j % 2
+
+            @pl.when(j + 1 < self.count)
+            def _():
+                for copy in self.copies(j + 1, 1 - slot):
+                    copy.start()
+
+            for copy in self.copies(j, slot):
+                copy.wait()
+            body(j, slot)
+            return 0
+
+        lax.fori_loop(first, self.count if last is None else last, step, 0)
+
+
+def block_kernel(ahead, back, *refs):
+    n = len(ahead.tensors)
+    (lens, x_h, dy_h), raw, refs = refs[:3], refs[3 : 3 + n], refs[3 + n :]
+    hbm_bufs, refs = refs[: n - 1], refs[n - 1 :]
+    (mixed_o, gtok_o, q_h, p_h, ha_h, ho_h, hm_h, hid_h), refs = refs[:8], refs[8:]
+    outs, refs = refs[:n], refs[n:]
+    total, refs = refs[:n], refs[n:]
+    count = len(back.items)
+    got, refs = [refs[3 * i : 3 * i + 3] for i in range(count)], refs[3 * count :]
+    (gate_pad, up_pad, down_pad, gain_buf, gains, xb, h1, da, db, kx, vx, o, x1, hid), refs = refs[:14], refs[14:]
+    (dy, dyr, dh, dxr_r, qr, kr, vr, turned, pool, broad), refs = refs[:10], refs[10:]
+    (kc, vc, rim_k, rim_v, gain_sum, gain_other), refs = refs[:6], refs[6:]
+    (a_send, a_recv, own_sem, b_send, b_recv, load_sem, pool_sem, broad_sem, turn_sem), refs = refs[:9], refs[9:]
+    half_send, half_recv, clear = refs
+    rows, width = xb.shape
+    wide, columns = ahead.tensors[5][1], ahead.tensors[1][1]
+    chips = NZ * NY * NX
+    me = Place()
+    halves, loads, later = {}, [0], {}
+
+    def load(src, dst):
+        copy = pltpu.make_async_copy(src, dst, load_sem.at[loads[0]])
+        loads[0] += 1
+        copy.start()
+        return copy
+
+    def to_partner(k, src, dst):
+        copy = remote(src, dst, half_send.at[k], half_recv.at[k], me.to_core())
+        copy.start()
+        halves[k] = copy
+        return copy
+
+    def own(size, side=0):
+        return pl.ds(pl.multiple_of((me.s if side == 0 else 1 - me.s) * size, 128), size)
+
+    get_x, get_dy = load(x_h, xb), load(dy_h, dy)
+    me.greet()
+    shards = list(raw[:5]) + [gate_pad, up_pad, down_pad]
+    bufs = [gain_buf] + list(hbm_bufs)
+    flat = [b.reshape(2, chips * b.shape[4], b.shape[5]) for b in bufs]
+    gather = Gather(ahead, me, shards, bufs, a_send, a_recv, own_sem)
+    scatter = Scatter(back, me, total, got, outs, b_send, b_recv)
+    ready = set()
+
+    def pad_shards():
+        part, tile = raw[7].shape[0], down_pad.shape[0]
+        zero = jnp.zeros((raw[5].shape[0], tile - part), LOW)
+        for src, dst in ((raw[5], gate_pad), (raw[6], up_pad)):
+            value, pieces = src[...], []
+            for k in range(value.shape[1] // part):
+                pieces += [value[:, k * part : (k + 1) * part], zero]
+            dst[...] = jnp.concatenate(pieces, axis=1)
+        down_pad[...] = jnp.concatenate([raw[7][...], jnp.zeros((tile - part, down_pad.shape[1]), LOW)], axis=0)
+
+    def prepare(t):
+        if t >= 5 and 5 not in ready:
+            pad_shards()
+            for k in range(5, n):
+                gather.own_copy(k).start()
+                ready.add(k)
+        elif t not in ready:
+            gather.own_copy(t).start()
+            ready.add(t)
+
+    landed, arrived = set(), set()
+
+    def land(t):
+        if t not in landed:
+            landed.add(t)
+            gather.own_copy(t).wait()
+
+    def need(t):
+        for k in range(t + 1):
+            if k not in arrived:
+                arrived.add(k)
+                for i in ahead.of_tensor[k]:
+                    gather.wait(i, 3)
+
+    def norm(values, gain):
+        inverse = lax.rsqrt(jnp.mean(values * values, axis=-1, keepdims=True) + EPS)
+        return (values * inverse * gain).astype(LOW)
+
+    def share(name, k, mine, whole):
+        to = whole.at[:, own(rows)]
+        later[name] = (load(mine, to), to_partner(k, mine, to))
+
+    def shared(name):
+        copy, sent = later[name]
+        copy.wait()
+        sent.wait()
+
+    def turn(src, dst, lane):
+        def body(j, _):
+            at = pl.ds(pl.multiple_of(j * 128, 128), 128)
+            dst[at, pl.ds(lane, rows)] = src[:, at].T
+            return 0
+
+        lax.fori_loop(0, src.shape[1] // 128, body, 0)
+        return dst.at[:, pl.ds(lane, rows)]
+
+    def first_norm():
+        need(0)
+        get_dy.wait()
+        later["dy"] = to_partner(0, dy.at[:, own(columns, 1)], dyr)
+        parts = []
+        for z in range(NZ):
+            for y in range(NY):
+                pair = [gain_buf[me.s, z, y, x].astype(F32) for x in range(NX)]
+                parts.append(pair[0] + pair[1])
+        gains[...] = jnp.concatenate(parts, axis=1)[0:8]
+        get_x.wait()
+
+        def body(at):
+            h1[at, :] = norm(xb[at, :].astype(F32), gains[0:1, :])
+
+        each_rows(rows, 64, body)
+        share("ha", 1, turn(h1, turned.at[0], 0), ha_h)
+
+    def project(t, src, store):
+        need(t)
+        tiles = Stream(2, pool_sem, lambda j, slot: [(flat[t].at[j], pool.at[slot, pl.ds(0, width), :])])
+        tiles.prime()
+
+        def body(side, slot):
+            for begin in range(0, columns, 256):
+                part = mm(src[...], pool[slot, :width, begin : begin + 256])
+                store(pl.ds(pl.multiple_of(side * columns + begin, 128), 256), part)
+
+        tiles.run(body)
+
+    def rim(k, ref):
+        to = ref.at[pl.ds(0, WINDOW), :]
+        return remote(ref.at[pl.ds(rows, WINDOW), :], to, half_send.at[2 + k], half_recv.at[2 + k], me.to_core())
+
+    def put_into(ref, skip):
+        def store(cols, part):
+            ref[pl.ds(skip, rows), cols] = part.astype(LOW)
+
+        return store
+
+    def do_query():
+        project(1, h1, put_into(da, 0))
+        later["q_out"] = load(da.at[:, pl.ds(0, width)], q_h)
+
+    def do_key():
+        project(2, h1, put_into(kx, WINDOW))
+        rim(0, kx).start()
+
+    def do_value():
+        project(3, h1, put_into(vx, WINDOW))
+        rim(1, vx).start()
+
+    first_end = lens[0, 0]
+    second_end = first_end + lens[0, 1]
+
+    def attend(b, _):
+        base = me.s * rows + b * WINDOW
+        at = pl.ds(pl.multiple_of(b * WINDOW, WINDOW), WINDOW)
+        over = pl.ds(pl.multiple_of(b * WINDOW, WINDOW), SPAN)
+        row = lax.broadcasted_iota(jnp.int32, (WINDOW, SPAN), 0)
+        col = lax.broadcasted_iota(jnp.int32, (WINDOW, SPAN), 1)
+        q_pos, k_pos = base + row, base - WINDOW + col
+
+        def doc(pos):
+            return (pos >= first_end).astype(jnp.int32) + (pos >= second_end).astype(jnp.int32)
+
+        visible = (col >= row) & (col <= row + WINDOW) & (k_pos >= 0) & (doc(q_pos) == doc(k_pos))
+        bias = jnp.where(visible, 0.0, -1e30)
+        bias = jnp.concatenate([bias, bias], axis=0)
+        pairs = range(HEADS // 2)
+        cols = [slice(p * PAIR, (p + 1) * PAIR) for p in pairs]
+        queries = [both_heads(da[at, c]) for c in cols]
+        keys, values = [kx[over, c] for c in cols], [vx[over, c] for c in cols]
+        scores = [mm_nt(q2, k) * HEAD_DIM ** (-0.5) + bias for q2, k in zip(queries, keys)]
+        tops = [jnp.max(s, axis=-1, keepdims=True) for s in scores]
+        exps = [jnp.exp(s - top) for s, top in zip(scores, tops)]
+        sums = [jnp.sum(e, axis=-1, keepdims=True) for e in exps]
+        weights = [(e * (1.0 / t)).astype(LOW) for e, t in zip(exps, sums)]
+        parts = [merge_heads(mm(w, v)).astype(LOW) for w, v in zip(weights, values)]
+        for p, c, w, part in zip(pairs, cols, weights, parts):
+            db[at, 2 * p * SPAN : (2 * p + 1) * SPAN] = w[:WINDOW]
+            db[at, (2 * p + 1) * SPAN : (2 * p + 2) * SPAN] = w[WINDOW:]
+            o[at, c] = part
+        return 0
+
+    quarter = rows // WINDOW // 4
+
+    def attend_part(k):
+        if k == 0:
+            for j, ref in ((0, kx), (1, vx)):
+                rim(j, ref).wait_recv()
+        lax.fori_loop(k * quarter, (k + 1) * quarter, attend, 0)
+        if k == 3:
+            later["p_out"] = load(db.at[:, pl.ds(0, HEADS * SPAN)], p_h)
+            share("ho", 4, turn(o, turned.at[0], rows), ho_h)
+
+    def add_out():
+        def store(cols, part):
+            x1[:, cols] = xb[:, cols].astype(F32) + part
+
+        project(4, o, store)
+
+        def body(at):
+            xb[at, :] = norm(x1[at, :], gains[1:2, :])
+
+        each_rows(rows, 64, body)
+        share("hm", 5, turn(xb, turned.at[1], rows), hm_h)
+
+    tiles = [(side, begin, min(512, wide - begin)) for side in range(2) for begin in range(0, wide, 512)]
+    stages = [(1, 0), (1, 1), (0, 0), (0, 1), (0, 2), (0, 3)]
+
+    def mlp_copies(j):
+        side, begin, size = tiles[j]
+        cols = pl.ds(begin, size)
+        return [
+            pltpu.make_async_copy(
+                flat[5 + k].at[side, :, cols], pool.at[j % 2, pl.ds(k * width, width), pl.ds(0, size)], pool_sem.at[j % 2, k]
+            )
+            for k in range(2)
+        ]
+
+    def mlp(j):
+        if j == 0:
+            need(6)
+            for copy in mlp_copies(0):
+                copy.start()
+            later["q_out"].wait()
+            later["p_out"].wait()
+            shared("ha")
+            shared("ho")
+        if j + 1 < len(tiles):
+            for copy in mlp_copies(j + 1):
+                copy.start()
+        for copy in mlp_copies(j):
+            copy.wait()
+        side, begin, size = tiles[j]
+        which, place = stages[j]
+        lane, first = (0, place * 512) if place < 2 else (rows, (place - 2) * 512)
+        for skip in range(0, size, 256):
+            w = min(256, size - skip)
+            cols = slice(skip, skip + w)
+            a = mm(xb[...], pool[j % 2, :width, cols])
+            b = mm(xb[...], pool[j % 2, width : 2 * width, cols])
+            sig = 1.0 / (1.0 + jnp.exp(-a))
+            silu = a * sig
+            at = side * wide + begin + skip
+            db[:, at : at + w] = silu.astype(LOW)
+            da[:, at : at + w] = (b * sig * (1.0 + a * (1.0 - sig))).astype(LOW)
+            hidden = (silu * b).astype(LOW)
+            hid[side, :, begin + skip : begin + skip + w] = hidden
+            turned[which, first + skip : first + skip + w, lane : lane + rows] = hidden.T
+        at = side * wide + begin
+        mine = turned.at[which, pl.ds(first, size), pl.ds(lane, rows)]
+        share(("hid", j), 6 + j, mine, hid_h.at[pl.ds(at, size), :])
+
+    tall = back.tensors[0][0] * NY * NX
+    hid_tiles = Stream(
+        NZ, turn_sem, lambda j, slot: [(hid_h.at[pl.ds(pl.multiple_of(j * tall, 16), tall), :], turned.at[slot, pl.ds(0, tall), :])]
+    )
+    tile, thin = 256, 128
+    small = pool.reshape(2, pool.shape[1] // tile, tile, columns)
+
+    def row_tiles(w, size, dst):
+        return lambda j, slot: (w.at[:, pl.ds(pl.multiple_of(j * size, size), size), :], dst(slot))
+
+    def small_at(k):
+        return lambda slot: small.at[slot, pl.ds(2 * k, 2)]
+
+    def broad_at(k):
+        return lambda slot: broad.at[slot, k]
+
+    def stream_of(fetchers, count, sems):
+        return Stream(count, sems, lambda j, slot: [f(j, slot) for f in fetchers])
+
+    def down_rows(j, slot):
+        side = jnp.where(j < wide // thin, 1 - me.s, me.s)
+        at = pl.ds(pl.multiple_of(side * wide + j % (wide // thin) * thin, thin), thin)
+        return [(flat[7].at[:, at, :], small.at[slot, pl.ds(0, 2), pl.ds(0, thin), :])]
+
+    down_tiles = Stream(2 * wide // thin, pool_sem, down_rows)
+    mlp_tiles = stream_of([row_tiles(flat[5 + k], thin, broad_at(k)) for k in range(2)], width // thin, broad_sem)
+    out_tiles = stream_of([row_tiles(flat[4], tile, small_at(0))], width // tile, pool_sem)
+    qkv_tiles = stream_of([row_tiles(flat[1 + k], tile, small_at(k)) for k in range(3)], width // tile, pool_sem)
+
+    def begin_scatter(t):
+        for i in back.of_tensor[t]:
+            scatter.start(i, 0)
+
+    def put(t, z, part):
+        row_count, column_count = back.tensors[t][:2]
+        total[t][z] = part.reshape(NY, NX, row_count, column_count).astype(total[t].dtype)
+
+    def grad_down():
+        for j in range(len(tiles)):
+            shared(("hid", j))
+        shared("hm")
+        later["dy"].wait_recv()
+        hid_tiles.prime()
+
+        def body(z, slot):
+            mine = mm(turned[slot, :tall, own(rows)], dy[:, own(columns)])
+            put(0, z, mine + mm(turned[slot, :tall, own(rows, 1)], dyr[...]))
+
+        hid_tiles.run(body)
+        begin_scatter(0)
+        later["hm"] = load(hm_h, turned.at[0])
+        later["ho"] = load(ho_h, turned.at[1])
+
+    def add_down():
+        need(7)
+        tiles2 = Stream(2, pool_sem, lambda j, slot: [(flat[7].at[j], pool.at[slot])])
+        tiles2.prime()
+
+        def body(side, slot):
+            for begin in range(0, columns, 256):
+                part = mm(hid[0], pool[slot, :wide, begin : begin + 256])
+                part += mm(hid[1], pool[slot, wide:, begin : begin + 256])
+                cols = pl.ds(pl.multiple_of(side * columns + begin, 128), 256)
+                xb[:, cols] = (x1[:, cols] + part).astype(LOW)
+
+        tiles2.run(body)
+        down_tiles.prime()
+        mlp_tiles.prime()
+        later["mixed"] = load(xb, mixed_o)
+        pl.semaphore_signal(clear, inc=1, device_id=me.to_core(), device_id_type=MESH)
+
+    def hidden_body(j, slot):
+        part = mm_nt(dy[:, :columns], small[slot, 0, :thin]) + mm_nt(dy[:, columns:], small[slot, 1, :thin])
+        side = jnp.where(j < wide // thin, 1 - me.s, me.s)
+        at = pl.ds(pl.multiple_of(side * wide + j % (wide // thin) * thin, thin), thin)
+        da[:, at] = (part * da[:, at].astype(F32)).astype(LOW)
+        db[:, at] = (part * db[:, at].astype(F32)).astype(LOW)
+
+    def hidden(k):
+        middle = down_tiles.count // 2
+        if k == 0:
+            down_tiles.run(hidden_body, 0, middle)
+            pl.semaphore_wait(clear, 1)
+            later["db"] = to_partner(12, db.at[:, own(wide, 1)], hid.at[1])
+            later["da"] = to_partner(13, da.at[:, own(wide, 1)], hid.at[0])
+            return
+        down_tiles.run(hidden_body, middle)
+        out_tiles.prime()
+
+    def weight_grad_to(t, slot, mine, theirs):
+        row_count = back.tensors[t][0] * NY * NX
+
+        def step(z, _):
+            at = pl.ds(pl.multiple_of(z * row_count, 16), row_count)
+            put(t, z, mm(turned[slot, at, own(rows)], mine()) + mm(turned[slot, at, own(rows, 1)], theirs[...]))
+            return 0
+
+        lax.fori_loop(0, NZ, step, 0)
+        begin_scatter(t)
+
+    def grad_up():
+        later["hm"].wait()
+        later["db"].wait_recv()
+        weight_grad_to(1, 0, lambda: db[:, own(wide)], hid.at[1])
+
+    def grad_gate():
+        later["da"].wait_recv()
+        weight_grad_to(2, 0, lambda: da[:, own(wide)], hid.at[0])
+        later["ha"] = load(ha_h, turned.at[0])
+
+    def dh2_body(j, slot):
+        part = None
+        for k, grad in ((0, da), (1, db)):
+            for side in range(2):
+                term = mm_nt(grad[:, side * wide : (side + 1) * wide], broad[slot, k, side])
+                part = term if part is None else part + term
+        dh[:, pl.ds(pl.multiple_of(j * thin, thin), thin)] = part
+
+    def grad_norm2(k):
+        middle = mlp_tiles.count // 2
+        if k == 0:
+            mlp_tiles.run(dh2_body, 0, middle)
+            return
+        mlp_tiles.run(dh2_body, middle)
+        later["db"].wait_send()
+        later["da"].wait_send()
+        later["q"] = load(q_h, da.at[:, pl.ds(0, width)])
+        later["p"] = load(p_h, db.at[:, pl.ds(0, HEADS * SPAN)])
+        later["mixed"].wait()
+        later["x"] = load(x_h, xb)
+
+    def norm_grad(values, grad_norm, gain):
+        inverse = lax.rsqrt(jnp.mean(values * values, axis=-1, keepdims=True) + EPS)
+        scaled = grad_norm * gain
+        mean_term = jnp.mean(values * scaled, axis=-1, keepdims=True)
+        back_part = inverse * scaled - values * (inverse * inverse * inverse) * mean_term
+        return back_part, jnp.sum(values * inverse * grad_norm, axis=0, keepdims=True)
+
+    def norm2_body(at):
+        back_part, gain_part = norm_grad(x1[at, :], dh[at, :], gains[1:2, :])
+        gain_sum[1:2, :] += gain_part
+        grad = dy[at, :].astype(F32) + back_part
+        x1[at, :] = grad
+        h1[at, :] = grad.astype(LOW)
+
+    def norm2():
+        gain_sum[...] = jnp.zeros_like(gain_sum)
+        each_rows(rows, 64, norm2_body)
+        later["dxr"] = to_partner(14, h1.at[:, own(columns, 1)], dxr_r)
+
+    def out_body(j, slot):
+        part = mm_nt(h1[:, :columns], small[slot, 0]) + mm_nt(h1[:, columns:], small[slot, 1])
+        o[:, pl.ds(pl.multiple_of(j * tile, tile), tile)] = part.astype(LOW)
+
+    def grad_heads():
+        out_tiles.run(out_body)
+        qkv_tiles.prime()
+
+    def grad_out():
+        later["ho"].wait()
+        later["dxr"].wait_recv()
+        weight_grad_to(3, 1, lambda: h1[:, own(columns)], dxr_r)
+
+    scale = HEAD_DIM ** (-0.5)
+
+    def attend_back(b, _):
+        at = pl.ds(pl.multiple_of(b * WINDOW, WINDOW), WINDOW)
+        over = pl.ds(pl.multiple_of(b * WINDOW, WINDOW), SPAN)
+        pairs = range(HEADS // 2)
+        cols = [slice(p * PAIR, (p + 1) * PAIR) for p in pairs]
+        queries, grads = [both_heads(da[at, c]) for c in cols], [both_heads(o[at, c]) for c in cols]
+        keys, values = [kx[over, c] for c in cols], [vx[over, c] for c in cols]
+        lows = [
+            jnp.concatenate([db[at, (2 * p + h) * SPAN : (2 * p + h + 1) * SPAN] for h in range(2)], axis=0)
+            for p in pairs
+        ]
+        carry_k, carry_v = [kc[:, c] for c in cols], [vc[:, c] for c in cols]
+        probs = [low.astype(F32) for low in lows]
+        grad_probs = [mm_nt(g, v) for g, v in zip(grads, values)]
+        grad_values = [mm_tn(low, g) for low, g in zip(lows, grads)]
+        inners = [jnp.sum(p * g, axis=-1, keepdims=True) for p, g in zip(probs, grad_probs)]
+        scores = [(p * (g - i)).astype(LOW) for p, g, i in zip(probs, grad_probs, inners)]
+        grad_queries = [(merge_heads(mm(s, k)) * scale).astype(LOW) for s, k in zip(scores, keys)]
+        grad_keys = [mm_tn(s, q2) * scale for s, q2 in zip(scores, queries)]
+        new_k = [(old + g[:WINDOW]).astype(LOW) for old, g in zip(carry_k, grad_keys)]
+        new_v = [(old + g[:WINDOW]).astype(LOW) for old, g in zip(carry_v, grad_values)]
+        for c, gq, gk, gv, nk, nv in zip(cols, grad_queries, grad_keys, grad_values, new_k, new_v):
+            da[at, c] = gq
+            kx[at, c] = nk
+            vx[at, c] = nv
+            kc[:, c] = gk[WINDOW:]
+            vc[:, c] = gv[WINDOW:]
+        return 0
+
+    own_rows = pl.ds(WINDOW, rows)
+
+    def attend_back_part(k):
+        if k == 0:
+            kc[...] = jnp.zeros_like(kc)
+            vc[...] = jnp.zeros_like(vc)
+            for j, ref in ((0, kx), (1, vx)):
+                rim(j, ref).wait_send()
+            later["q"].wait()
+            later["p"].wait()
+        lax.fori_loop(k * quarter, (k + 1) * quarter, attend_back, 0)
+        if k == 0:
+            later["rim"] = [
+                to_partner(15, kx.at[pl.ds(0, WINDOW), :], rim_k),
+                to_partner(16, vx.at[pl.ds(0, WINDOW), :], rim_v),
+            ]
+        if k == 3:
+            for copy, ref, carry, rim_in in ((later["rim"][0], kx, kc, rim_k), (later["rim"][1], vx, vc, rim_v)):
+                copy.wait_recv()
+                ref[pl.ds(rows, WINDOW), :] = (carry[...] + rim_in[...].astype(F32)).astype(LOW)
+            later["dq"] = to_partner(17, da.at[:, own(columns, 1)], qr)
+            later["dk"] = to_partner(18, kx.at[own_rows, own(columns, 1)], kr)
+            later["dv"] = to_partner(19, vx.at[own_rows, own(columns, 1)], vr)
+
+    def grad_qkv(k):
+        if k == 0:
+            later["ha"].wait()
+        later[("dq", "dk", "dv")[k]].wait_recv()
+        mine = (lambda: da[:, own(columns)], lambda: kx[own_rows, own(columns)], lambda: vx[own_rows, own(columns)])[k]
+        weight_grad_to(4 + k, 0, mine, (qr, kr, vr)[k])
+
+    def dh1_body(j, slot):
+        part = None
+        for k, (grad, skip) in enumerate(((da, 0), (kx, WINDOW), (vx, WINDOW))):
+            for side in range(2):
+                left = grad[pl.ds(skip, rows), side * columns : (side + 1) * columns]
+                term = mm_nt(left, small[slot, 2 * k + side])
+                part = term if part is None else part + term
+        dh[:, pl.ds(pl.multiple_of(j * tile, tile), tile)] = part
+
+    def grad_norm1():
+        qkv_tiles.run(dh1_body)
+
+    def norm1_body(at):
+        back_part, gain_part = norm_grad(xb[at, :].astype(F32), dh[at, :], gains[0:1, :])
+        gain_sum[0:1, :] += gain_part
+        x1[at, :] = x1[at, :] + back_part
+
+    def norm1():
+        later["x"].wait()
+        each_rows(rows, 64, norm1_body)
+        later["gtok"] = load(x1, gtok_o)
+        later["gain"] = to_partner(20, gain_sum, gain_other)
+
+    def grad_gains():
+        later["gain"].wait_recv()
+        lanes = back.tensors[7][1]
+        for c in range(chips):
+            at = slice(c // 2 * lanes, (c // 2 + 1) * lanes)
+            total[7][c // 4, c // 2 % 2, c % 2] = gain_sum[:, at] + gain_other[:, at]
+        begin_scatter(7)
+
+    work = {
+        "norm": first_norm,
+        "query": do_query,
+        "key": do_key,
+        "value": do_value,
+        "project": add_out,
+        "mix": add_down,
+        "down": grad_down,
+        "up": grad_up,
+        "gate": grad_gate,
+        "norm2": norm2,
+        "heads": grad_heads,
+        "out": grad_out,
+        "dh1": grad_norm1,
+        "norm1": norm1,
+        "gains": grad_gains,
+    }
+    for k in range(4):
+        work["see", k] = functools.partial(attend_part, k)
+        work["attend", k] = functools.partial(attend_back_part, k)
+    for k in range(len(tiles)):
+        work["mlp", k] = functools.partial(mlp, k)
+    for k in range(3):
+        work["qkv", k] = functools.partial(grad_qkv, k)
+    for k in range(2):
+        work["hidden", k] = functools.partial(hidden, k)
+        work["dh2", k] = functools.partial(grad_norm2, k)
+    for step in SCRIPT:
+        if step in work:
+            work[step]()
+        elif step[0] == "start":
+            prepare(ahead.items[step[1]][0])
+            gather.start(step[1], 0)
+        elif step[0] == 0:
+            _, i, phase = step
+            land(ahead.items[i][0])
+            gather.wait(i, phase)
+            gather.start(i, phase + 1)
+        else:
+            _, i, phase = step
+            scatter.wait(i, phase)
+            scatter.add(i, phase)
+            if phase < 2:
+                scatter.start(i, phase + 1)
+    for i in range(len(ahead.items)):
+        gather.finish(i)
+    for i in range(len(back.items)):
+        scatter.finish(i)
+    for k in (0, 14, 15, 16, 17, 18, 19, 20):
+        halves[k].wait_send()
+    later["gtok"].wait()
+
+
+def block_all(ahead, back, lens, tokens, cotangent, shards):
+    n, na, nb = len(ahead.tensors), len(ahead.items), len(back.items)
+    rows, width = tokens.shape
+    columns, wide = ahead.tensors[1][1], ahead.tensors[5][1]
+    anywhere = pl.BlockSpec(memory_space=pl.ANY)
+    inside = pl.BlockSpec(memory_space=pltpu.VMEM)
+    shape = jax.ShapeDtypeStruct
+    over = WINDOW + rows
+    bufs = [(2, NZ, NY, NX) + t[:2] for t in ahead.tensors]
+    kept = [
+        ((rows, width), LOW),
+        ((rows, width), F32),
+        ((rows, width), LOW),
+        ((rows, HEADS * SPAN), LOW),
+        ((width, 2 * rows), LOW),
+        ((width, 2 * rows), LOW),
+        ((width, 2 * rows), LOW),
+        ((2 * wide, 2 * rows), LOW),
+    ]
+    scratch = [
+        (ahead.tensors[5][:2], LOW),
+        (ahead.tensors[6][:2], LOW),
+        (ahead.tensors[7][:2], LOW),
+        (bufs[0], LOW),
+        ((8, width), F32),
+        ((rows, width), LOW),
+        ((rows, width), LOW),
+        ((rows, 2 * wide), LOW),
+        ((rows, 2 * wide), LOW),
+        ((over, width), LOW),
+        ((over, width), LOW),
+        ((rows, width), LOW),
+        ((rows, width), F32),
+        ((2, rows, wide), LOW),
+        ((rows, width), LOW),
+        ((rows, columns), LOW),
+        ((rows, width), F32),
+        ((rows, columns), LOW),
+        ((rows, columns), LOW),
+        ((rows, columns), LOW),
+        ((rows, columns), LOW),
+        ((2, width, 2 * rows), LOW),
+        ((2, 2 * wide, columns), LOW),
+        ((2, 2, 2, 128, wide), LOW),
+        ((WINDOW, width), F32),
+        ((WINDOW, width), F32),
+        ((WINDOW, width), LOW),
+        ((WINDOW, width), LOW),
+        ((8, width), F32),
+        ((8, width), F32),
+    ]
+    totals = [((NZ, NY, NX) + t[:2], t[2]) for t in back.tensors]
+    got = [part for parts in got_shapes(back) for part in parts]
+    dma = pltpu.SemaphoreType.DMA
+    outs = pl.pallas_call(
+        functools.partial(block_kernel, ahead, back),
+        out_shape=[shape(b, LOW) for b in bufs[1:]]
+        + [shape(*s) for s in kept]
+        + [shape(t[:2], F32) for t in back.tensors],
+        in_specs=[pl.BlockSpec(memory_space=pltpu.SMEM), anywhere, anywhere] + [inside] * n,
+        out_specs=[anywhere] * (n - 1 + len(kept)) + [inside] * n,
+        scratch_shapes=[pltpu.VMEM(*s) for s in totals + got + scratch]
+        + [dma((6 * na,)), dma((6 * na,)), dma((n,)), dma((5 * nb,)), dma((5 * nb,)), dma((24,))]
+        + [dma((2, 3)), dma((2, 2)), dma((2, 1)), dma((21,)), dma((21,)), pltpu.SemaphoreType.REGULAR],
+        compiler_params=pltpu.CompilerParams(
+            collective_id=0, has_side_effects=True, vmem_limit_bytes=VMEM_LIMIT
+        ),
+        name="block_all",
+    )(lens, tokens, cotangent, *shards)
+    return outs[n - 1 : n + 1], outs[n - 1 + len(kept) :]
+
+
+def finish_kernel(*refs):
+    n = 10
+    ins, outs, held, made = refs[:n], refs[n : 2 * n + 1], refs[2 * n + 1 : 3 * n + 1], refs[3 * n + 1 : 4 * n + 2]
+    sem_in, sem_out = refs[4 * n + 2 :]
+    gets = [pltpu.make_async_copy(src, dst, sem_in.at[k]) for k, (src, dst) in enumerate(zip(ins, held))]
+    for copy in gets:
+        copy.start()
+    puts = []
+
+    def put(k, src):
+        copy = pltpu.make_async_copy(src, outs[k], sem_out.at[k])
+        copy.start()
+        puts.append(copy)
+
+    down, up, gate, out, query, key, value, gain = held[2:]
+    for copy in gets[2:]:
+        copy.wait()
+    for k, src in ((2, query), (3, key), (4, value), (5, out)):
+        put(k, src)
+    rows, part, tile = query.shape[0], outs[8].shape[0], down.shape[0]
+    made[8][...] = down[...][:part]
+    put(8, made[8])
+    for k, src in ((6, gate), (7, up)):
+        values = src[...]
+        made[k][...] = jnp.concatenate(
+            [values[:, j * tile : j * tile + part] for j in range(values.shape[1] // tile)], axis=1
+        )
+        put(k, made[k])
+    both = gain[...]
+    own = jnp.where(lax.axis_index("dp") % 2 == 0, both[:, :rows], both[:, rows:])
+    made[9][...] = own[0:1]
+    made[10][...] = own[1:2]
+    put(9, made[9])
+    put(10, made[10])
+    for k in range(2):
+        gets[k].wait()
+        put(k, held[k])
+    for copy in puts:
+        copy.wait()
+
+
+def finish_all(mixed, tokens, sums, w_query, w_gate, w_down):
+    anywhere = pl.BlockSpec(memory_space=pl.ANY)
+    shape = jax.ShapeDtypeStruct
+    outs = [shape(mixed.shape, mixed.dtype), shape(tokens.shape, F32)]
+    outs += [shape(w_query.shape, F32)] * 4 + [shape(w_gate.shape, F32)] * 2 + [shape(w_down.shape, F32)]
+    outs += [shape((1, w_query.shape[0]), F32)] * 2
+    ins = [mixed, tokens, *sums]
+    return pl.pallas_call(
+        finish_kernel,
+        out_shape=outs,
+        in_specs=[anywhere] * len(ins),
+        out_specs=[anywhere] * len(outs),
+        scratch_shapes=[pltpu.VMEM(a.shape, a.dtype) for a in ins + outs]
+        + [pltpu.SemaphoreType.DMA((len(ins),)), pltpu.SemaphoreType.DMA((len(outs),))],
+        compiler_params=pltpu.CompilerParams(vmem_limit_bytes=62 * 2**20),
+        name="finish_all",
+    )(*ins)
+
+
+def kinds(w_query, w_gate, w_down):
+    rows, columns = w_query.shape
+    part = w_down.shape[0]
+    tile = -(-part // 16) * 16
+    wide = w_gate.shape[1] // part * tile
+    half, part16 = rows // 2, rows // 4
+    long, short = -(-tile // 64) * 16, tile - 3 * (-(-tile // 64) * 16)
+
+    def cuts(kinds, counts):
+        return tuple(zip(kinds, counts, strict=True))
+
+    return {
+        "square": (rows, columns, LOW, cuts(("zfx", "zfy"), (half, half))),
+        "broad": (rows, wide, LOW, cuts(("zfx", "zfy", "zmx", "zmy"), (part16,) * 4)),
+        "broad_f": (rows, wide, LOW, cuts(("zfx", "zfy", "zfx", "zfy"), (part16,) * 4)),
+        "tall": (tile, columns, LOW, cuts(("zfx", "zfy", "zmx", "zmy"), (long, long, long, short))),
+        "square_m": (rows, columns, LOW, cuts(("zmx", "zmy"), (half, half))),
+        "tall_f": (tile, columns, LOW, cuts(("zfx", "zfy", "zfx", "zfy"), (long, long, long, short))),
+        "gain": (16, 2 * rows, LOW, cuts(("zfx",), (16,))),
+        "gain_grad": (8, 2 * rows, F32, cuts(("zfx",), (8,))),
+    }
+
+
+def gather_plan(w_query, w_key, w_value, w_out, w_gate, w_up, w_down, gain_attn, gain_mlp):
+    kind = kinds(w_query, w_gate, w_down)
+    names = ("gain", "square", "square", "square", "square", "broad", "broad", "tall")
+    plan = Plan([kind[name] for name in names])
+    rows = w_query.shape[0]
+    both = jnp.stack([gain_attn, gain_mlp])
+    left = jnp.pad(both, ((0, 14), (0, rows)))
+    right = jnp.pad(both, ((0, 14), (rows, 0)))
+    pair = jnp.where(lax.axis_index("dp") % 2 == 0, left, right)
+    shards = [
+        pair,
+        w_query,
+        w_key,
+        w_value,
+        w_out,
+        w_gate,
+        w_up,
+        w_down,
+    ]
+    return plan, shards
+
+
+def swift_block(
+    tokens,
+    seq_lengths,
+    w_query,
+    w_key,
+    w_value,
+    w_out,
+    w_gate,
+    w_up,
+    w_down,
+    gain_attn,
+    gain_mlp,
+    cotangent,
+):
+    plan, shards = gather_plan(w_query, w_key, w_value, w_out, w_gate, w_up, w_down, gain_attn, gain_mlp)
+    kind = kinds(w_query, w_gate, w_down)
+    names = ("tall_f", "broad_f", "broad_f", "square", "square", "square", "square", "gain_grad")
+    back = Plan([kind[name] for name in names])
+    results, sums = block_all(plan, back, seq_lengths, tokens, cotangent, shards)
+    outs = finish_all(results[0], results[1], sums, w_query, w_gate, w_down)
+    return (*outs[:9], outs[9].reshape(-1), outs[10].reshape(-1))
+
+
 def solution(mesh):
+    fast = (mesh.shape["dp"], mesh.shape["seq"]) == (NZ * NY * NX, 2)
+    shards = swift_block if fast else plain_block
     in_specs = (
         P(("dp", "seq"), None),
         P("dp", None),

time: 1340 us -> 261 us (0.19)
  waiting for transfers between devices: 731 us -> 0 us
  blocking collectives: 300 us -> 0 us
  Pallas kernels: 0 us -> 258 us
  matrix products: 168 us -> 0 us
  local copies, waits for them, and re-layouts: 54.9 us -> 0 us
  other arithmetic: 45.3 us -> 1.35 us
  between operations: 18.8 us -> 0.85 us
    all_gather x14 -> x0, waiting for transfers between devices: 406 us -> none  [the longest x1 67.3 us: shards(): lax.all_gather(w_gate, 'dp', axis=0, tiled=True)]
    unnamed x3 -> x0, blocking collectives: 297 us -> none
    reduce_scatter x11 -> x0, waiting for transfers between devices: 294 us -> none  [the longest x1 122 us: shards(): lax.psum_scatter(d_gate.astype(jnp.bfloat16), 'dp', scatter_dimension=0,...]
    pallas_call x0 -> x2, Pallas kernels: none -> 258 us  [the longest x1 253 us: block_all(): pl.pallas_call(functools.partial(block_kernel, ahead, back), out_shape=[s...]
    dot_general x33 -> x0, matrix products: 168 us -> none  [the longest x7 38.7 us: weight_grad(): jnp.einsum('td,tf->df', inputs, grad_rows, preferred_element_type=jnp.flo...]
    unnamed x87 -> x0, local copies, waits for them, and re-layouts: 31.1 us -> none
    unnamed x30 -> x0, waiting for transfers between devices: 28.7 us -> none
    convert_element_type x13 -> x0, other arithmetic: 24.7 us -> none  [the longest x1 14.1 us: shards(): grad_score = (prob_full * (grad_prob - inner)).astype(jnp.bfloat16)]
  transfers between devices with their start and end apart: 32 -> 0, of which waited for: 23 -> 0; matrix products, arithmetic and copies ran while one was open for 30% -> 0% of each run, Pallas kernels for 0% -> 0%
where the time goes in v4:
time: 261 us; the launch traced here: 260 us
  Pallas kernels  258 us (99%)
    pallas_call x1, Pallas kernels, block_all(): pl.pallas_call(functools.partial(block_kernel, ahead, back), out_shape=[s...  253 us

profile of v4, /device:TPU:0, one launch (start us, length us, event | category | flops | bytes accessed | tf_op | source)
XLA Modules:
  0.0 259.8 jit_solution(1664109981867604300)
XLA Ops:
  0.7 0.7 pad_maximum_fusion
  1.3 0.7 pad_select_fusion.refs_3_
  2.0 252.8 %block_all.1 = (bf16[2,4,2,2,64,512]{5,4,3,2,1,0:T(8,128)(2,1)}, bf16[2,4,2,2,64,512]{5,4,3,2,1,0:T(8,128)(2,1)}, bf16[2,4,2,2,64,512]{5,4,3,2,1,0:T(8,128)(2,1)...) custom-call(s32[1,3]{1,0:T(1,128)} %refs_0_.1, ...), custom_call_target="tpu_custom_call" | custom-call | tf_op jit(solution)/shard_map/block_all/pallas_call | solution.py:1281
  254.8 4.8 %finish_all.1 = (bf16[512,1024]{1,0:T(8,128)(2,1)}, f32[512,1024]{1,0:T(8,128)}, f32[64,512]{1,0:T(8,128)}, f32[64,512]{1,0:T(8,128)}, f32[64,512]{1,0:T(8,128)}...) custom-call(bf16[512,1024]{1,0:T(8,128)(2,1)} %get-tuple-element.32., ...), custom_call_target="tpu_custom_call" | custom-call | tf_op jit(solution)/shard_map/finish_all/pallas_call | solution.py:1347

commit v5 on v4

--- a/solution.py
+++ b/solution.py
@@ -349,27 +349,35 @@
 
 
 SCRIPT = (
-    ("start", 16), ("start", 19), ("start", 11), ("start", 0), ("start", 2), ("start", 12), ("start", 15),
-    ("start", 3), (0, 0, 0), ("start", 20), ("start", 13), (0, 3, 0), ("start", 4), (0, 2, 0), (0, 13, 0),
-    ("start", 1), ("start", 7), (0, 2, 1), (0, 3, 1), (0, 4, 0), ("start", 10), (0, 1, 0), ("start", 14),
-    ("start", 5), (0, 13, 1), (0, 0, 1), (0, 4, 1), (0, 7, 0), (0, 2, 2), (0, 10, 0), ("start", 6), (0, 5, 0),
-    ("start", 17), (0, 14, 0), (0, 10, 1), ("start", 9), (0, 4, 2), (0, 1, 1), (0, 15, 0), (0, 14, 1),
-    (0, 5, 1), (0, 6, 0), (0, 9, 0), (0, 12, 0), (0, 15, 1), (0, 6, 1), ("start", 8), (0, 0, 2), (0, 7, 1),
-    (0, 1, 2), (0, 3, 2), "norm", (0, 11, 0), (0, 12, 1), (0, 8, 0), (0, 13, 2), (0, 5, 2), "key", (0, 6, 2),
-    "query", (0, 17, 0), (0, 16, 0), (0, 11, 1), "value", (0, 8, 1), ("see", 0), (0, 7, 2), (0, 12, 2),
-    (0, 14, 2), (0, 9, 1), ("start", 18), (0, 16, 1), ("see", 1), (0, 8, 2), (0, 11, 2), (0, 20, 0),
-    ("see", 2), (0, 15, 2), (0, 18, 0), ("see", 3), (0, 19, 0), (0, 10, 2), (0, 17, 1), (0, 16, 2), (0, 9, 2),
-    "project", ("mlp", 0), (0, 18, 1), ("mlp", 1), ("mlp", 2), ("mlp", 3), (0, 19, 1), (0, 20, 1), (0, 17, 2),
-    ("mlp", 4), ("mlp", 5), "down", (0, 19, 2), (0, 20, 2), (0, 18, 2), "mix", ("hidden", 0), (1, 1, 0),
-    ("hidden", 1), (1, 2, 0), (1, 3, 0), "up", ("dh2", 0), "gate", (1, 2, 1), (1, 2, 2), (1, 1, 1),
-    ("dh2", 1), (1, 3, 1), "norm2", "heads", ("attend", 0), (1, 5, 0), ("attend", 1), (1, 4, 0),
-    ("attend", 2), ("attend", 3), (1, 8, 0), (1, 7, 0), (1, 4, 1), (1, 9, 0), (1, 11, 0), (1, 5, 1),
-    (1, 6, 0), "out", (1, 8, 1), (1, 6, 1), (1, 1, 2), ("qkv", 0), (1, 7, 1), "dh1", (1, 11, 1), (1, 9, 1),
-    (1, 10, 0), "norm1", (1, 15, 0), (1, 13, 0), (1, 12, 0), (1, 10, 1), (1, 0, 0), (1, 14, 0), ("qkv", 1),
-    "gains", (1, 12, 1), (1, 13, 1), (1, 15, 1), (1, 14, 1), ("qkv", 2), (1, 9, 2), (1, 16, 0), (1, 20, 0),
-    (1, 5, 2), (1, 0, 1), (1, 17, 0), (1, 20, 1), (1, 16, 1), (1, 18, 0), (1, 6, 2), (1, 4, 2), (1, 15, 2),
-    (1, 19, 0), (1, 17, 1), (1, 13, 2), (1, 8, 2), (1, 18, 1), (1, 16, 2), (1, 19, 1), (1, 7, 2), (1, 0, 2),
-    (1, 3, 2), (1, 14, 2), (1, 20, 2), (1, 10, 2), (1, 11, 2), (1, 12, 2), (1, 17, 2), (1, 18, 2), (1, 19, 2),
+    ("start", 7), ("start", 14), ("start", 4), ("start", 1), ("start", 20), ("start", 0), ("start", 18),
+    ("start", 16), ("start", 6), ("start", 3), ("start", 5), ("start", 9), ("start", 10), (0, 0, 0, 1),
+    (0, 5, 0), (0, 4, 0, 1), (0, 3, 0, 1), (0, 9, 0, 1), ("start", 11), (0, 1, 0, 1), (0, 5, 1, 1),
+    (0, 3, 0, 2), (0, 0, 0, 2), (0, 4, 0, 2), ("start", 19), (0, 20, 0), (0, 5, 1, 2), ("start", 2),
+    (0, 4, 0, 3), (0, 0, 0, 3), ("start", 12), (0, 3, 0, 3), (0, 19, 0), ("start", 17), (0, 0, 1),
+    (0, 14, 0, 1), ("start", 15), (0, 2, 0, 1), (0, 6, 0), ("start", 13), (0, 5, 1, 3), (0, 20, 1, 1),
+    (0, 9, 0, 2), (0, 4, 1), (0, 9, 0, 3), (0, 2, 0, 2), (0, 3, 1), (0, 18, 0), (0, 19, 1, 1), (0, 20, 1, 2),
+    ("start", 8), (0, 2, 0, 3), (0, 0, 2), (0, 1, 0, 2), (0, 18, 1, 1), (0, 9, 1), (0, 6, 1, 1), (0, 1, 0, 3),
+    (0, 19, 1, 2), (0, 5, 2), (0, 2, 1), (0, 14, 0, 2), (0, 3, 2), (0, 8, 0), (0, 6, 1, 2), (0, 12, 0),
+    (0, 19, 1, 3), (0, 17, 0), (0, 16, 0), (0, 20, 1, 3), (0, 13, 0, 1), "norm", (0, 6, 1, 3), (0, 8, 1, 1),
+    (0, 18, 1, 2), (0, 7, 0), (0, 14, 0, 3), (0, 18, 1, 3), (0, 2, 2), (0, 17, 1, 1), (0, 17, 1, 2),
+    (0, 7, 1, 1), (0, 1, 1), (0, 4, 2), (0, 17, 1, 3), (0, 6, 2), (0, 14, 1), (0, 19, 2), (0, 11, 0),
+    (0, 10, 0, 1), (0, 10, 0, 2), (0, 15, 0), (0, 7, 1, 2), "value", (0, 9, 2), (0, 10, 0, 3), (0, 18, 2),
+    (0, 1, 2), (0, 8, 1, 2), (0, 7, 1, 3), (0, 13, 0, 2), (0, 13, 0, 3), (0, 11, 1, 1), "key", (0, 8, 1, 3),
+    (0, 14, 2), "query", ("see", 0), (0, 20, 2), (0, 13, 1), ("see", 1), (0, 16, 1, 1), (0, 10, 1),
+    (0, 12, 1, 1), (0, 17, 2), (0, 15, 1, 1), ("see", 2), (0, 7, 2), (0, 8, 2), ("see", 3), (0, 11, 1, 2),
+    ("hidden", 0), (0, 15, 1, 2), (0, 11, 1, 3), (0, 12, 1, 2), ("hidden", 1), (0, 16, 1, 2), (0, 13, 2),
+    "project", (0, 15, 1, 3), (0, 16, 1, 3), (0, 10, 2), ("mlp", 0), (0, 12, 1, 3), (0, 11, 2), ("mlp", 1),
+    ("up", 0), ("gate", 0), (0, 15, 2), ("gate", 1), ("up", 1), (0, 12, 2), (0, 16, 2), ("mlp", 2),
+    ("mlp", 3), ("gate", 2), (1, 8, 0), ("dh2", 0), ("up", 2), ("up", 3), (1, 5, 0), (1, 4, 0), ("gate", 3),
+    (1, 8, 1), (1, 9, 0), (1, 10, 0), "mix", "down", (1, 5, 1), ("dh2", 1), (1, 9, 1), "norm2", (1, 11, 0),
+    "heads", "out", ("attend", 0), (1, 3, 0), ("attend", 1), (1, 6, 0), (1, 4, 1), ("attend", 2), (1, 1, 0),
+    ("attend", 3), (1, 2, 0), (1, 7, 0), (1, 0, 0), (1, 6, 1), ("qkv", 0), "dh1", (1, 8, 2), (1, 7, 1),
+    ("qkv", 1), (1, 3, 1), (1, 9, 2), (1, 13, 0), (1, 15, 0), (1, 1, 1), (1, 14, 0), (1, 0, 1), "norm1",
+    (1, 5, 2), (1, 3, 2), ("qkv", 2), (1, 12, 0), (1, 14, 1), "gains", (1, 2, 1), (1, 17, 0), (1, 15, 1),
+    (1, 13, 1), (1, 16, 0), (1, 1, 2), (1, 12, 1), (1, 6, 2), (1, 19, 0), (1, 2, 2), (1, 10, 1), (1, 17, 1),
+    (1, 18, 0), (1, 0, 2), (1, 15, 2), (1, 16, 1), (1, 20, 0), (1, 12, 2), (1, 19, 1), (1, 13, 2), (1, 11, 1),
+    (1, 7, 2), (1, 14, 2), (1, 10, 2), (1, 20, 1), (1, 17, 2), (1, 18, 1), (1, 16, 2), (1, 20, 2), (1, 19, 2),
+    (1, 4, 2), (1, 11, 2), (1, 18, 2),
 )
 
 
@@ -385,9 +393,11 @@
         self.items, self.of_tensor = [], []
         for t, (_, _, _, cuts) in enumerate(tensors):
             begin, mine = 0, []
-            for kind, count in cuts:
+            for kind, along, count in cuts:
                 mine.append(len(self.items))
-                self.items.append((t, SEQUENCE[kind], begin, count))
+                whole = [(0, tensors[t][0]), (0, tensors[t][1])]
+                whole[along] = (begin, count)
+                self.items.append((t, SEQUENCE[kind], *whole))
                 begin += count
             self.of_tensor.append(mine)
 
@@ -426,11 +436,11 @@
     )
 
 
-def slots(seq, count):
+def slots(seq, count, along_z):
     firsts, used = [], 0
     for phase in range(count):
         firsts.append(used)
-        used += 3 if phase < 3 and seq[phase] == "z" else 1
+        used += along_z if phase < 3 and seq[phase] == "z" else 1
     return firsts
 
 
@@ -446,12 +456,12 @@
         )
 
     def moves(self, i, phase):
-        t, seq, begin, count = self.plan.items[i]
+        t, seq, rows, cols = self.plan.items[i]
         me, buf = self.me, self.bufs[t]
-        rows = pl.ds(begin, count)
+        rows, cols = pl.ds(*rows), pl.ds(*cols)
 
         def view(z, y, x, half=me.s):
-            return buf.at[half, z, y, x, rows, :]
+            return buf.at[half, z, y, x, rows, cols]
 
         if phase == 3:
             whole = view(ALL_Z, ALL_Y, ALL_X)
@@ -461,20 +471,58 @@
         y = ALL_Y if "y" in done else me.y
         x = ALL_X if "x" in done else me.x
         there = view(z, y, x)
-        here = self.shards[t].at[rows, :] if phase == 0 else there
+        here = self.shards[t].at[rows, cols] if phase == 0 else there
         if axis == "x":
             return [(here, there, me.to_x(), view(z, y, 1 - me.x), 0)]
-        if axis == "y":
-            return [(here, there, me.to_y(), view(z, 1 - me.y, x), 0)]
-        return [
-            (here, there, me.to_z(k), view((me.z + NZ - k) % NZ, y, x), k - 1) for k in (1, 2, 3)
-        ]
+        return [(here, there, me.to_y(), view(z, 1 - me.y, x), 0)]
+
+    def hops(self, i, phase, hop):
+        t, seq, rows, cols = self.plan.items[i]
+        me, buf = self.me, self.bufs[t]
+        rows, cols = pl.ds(*rows), pl.ds(*cols)
+        done = seq[:phase]
+        y = ALL_Y if "y" in done else me.y
+        x = ALL_X if "x" in done else me.x
+        moves = []
+        for k, way in enumerate((1, -1)):
+            first, last = (me.z, NZ - 1 - me.z) if way == 1 else (NZ - 1 - me.z, me.z)
+            sends = (first >= hop - 1) & (last >= 1)
+            takes = first >= hop
+            z = me.z - way * (hop - 1)
+            there = buf.at[me.s, z, y, x, rows, cols]
+            here = self.shards[t].at[rows, cols] if phase == 0 and hop == 1 else there
+            arrived = buf.at[me.s, me.z - way * hop, y, x, rows, cols]
+            moves.append((sends, takes, here, there, me.at(me.z + way, me.y, me.x), arrived, 3 * k + hop - 1))
+        return moves
+
+    def along_z(self, i, phase):
+        return phase < 3 and self.plan.items[i][1][phase] == "z"
 
     def copy(self, i, phase, src, dst, device, k):
-        at = 6 * i + slots(self.plan.items[i][1], 4)[phase] + k
+        at = 9 * i + slots(self.plan.items[i][1], 4, 6)[phase] + k
         return remote(src, dst, self.send.at[at], self.recv.at[at], device)
 
+    def send_hop(self, i, phase, hop):
+        for sends, _, here, there, device, _, k in self.hops(i, phase, hop):
+
+            @pl.when(sends)
+            def _(here=here, there=there, device=device, k=k):
+                self.copy(i, phase, here, there, device, k).start()
+
+    def take_hop(self, i, phase, hop):
+        for _, takes, _, _, device, arrived, k in self.hops(i, phase, hop):
+
+            @pl.when(takes)
+            def _(device=device, arrived=arrived, k=k):
+                self.copy(i, phase, arrived, arrived, device, k).wait_recv()
+
+        if hop < NZ - 1:
+            self.send_hop(i, phase, hop + 1)
+
     def start(self, i, phase):
+        if self.along_z(i, phase):
+            self.send_hop(i, phase, 1)
+            return
         for here, there, device, _, k in self.moves(i, phase):
             self.copy(i, phase, here, there, device, k).start()
 
@@ -484,16 +532,25 @@
 
     def finish(self, i):
         for phase in range(4):
+            if self.along_z(i, phase):
+                for hop in range(1, NZ):
+                    for sends, _, here, there, device, _, k in self.hops(i, phase, hop):
+
+                        @pl.when(sends)
+                        def _(here=here, there=there, device=device, k=k):
+                            self.copy(i, phase, here, there, device, k).wait_send()
+
+                continue
             for here, there, device, _, k in self.moves(i, phase):
                 self.copy(i, phase, here, there, device, k).wait_send()
 
 
 def got_shapes(plan):
     shapes = []
-    for t, seq, _, count in plan.items:
-        _, columns, dtype, _ = plan.tensors[t]
+    for t, seq, (_, rows), (_, columns) in plan.items:
+        dtype = plan.tensors[t][2]
         second, third = ((1, NZ), (3,)) if seq[0] == "z" else ((3, 2), (1,))
-        shapes.append([(d + (count, columns), dtype) for d in ((NZ, 2), second, third)])
+        shapes.append([(d + (rows, columns), dtype) for d in ((NZ, 2), second, third)])
     return shapes
 
 
@@ -503,9 +560,9 @@
         self.send, self.recv = send, recv
 
     def moves(self, i, phase):
-        t, seq, begin, count = self.plan.items[i]
+        t, seq, rows, cols = self.plan.items[i]
         me, total, got = self.me, self.total[t], self.got[i][phase]
-        rows = pl.ds(begin, count)
+        rows, cols = pl.ds(*rows), pl.ds(*cols)
         axis, done = seq[2 - phase], seq[3 - phase :]
         z = me.z if "z" in done else ALL_Z
         y = me.y if "y" in done else ALL_Y
@@ -515,16 +572,16 @@
         else:
             lands = [got.at[k] for k in range(got.shape[0])]
         if axis == "x":
-            return [(total.at[z, y, 1 - me.x, rows, :], lands[0], me.to_x(), 0)]
+            return [(total.at[z, y, 1 - me.x, rows, cols], lands[0], me.to_x(), 0)]
         if axis == "y":
-            return [(total.at[z, 1 - me.y, x, rows, :], lands[0], me.to_y(), 0)]
+            return [(total.at[z, 1 - me.y, x, rows, cols], lands[0], me.to_y(), 0)]
         return [
-            (total.at[(me.z + k) % NZ, y, x, rows, :], lands[k - 1], me.to_z(k), k - 1)
+            (total.at[(me.z + k) % NZ, y, x, rows, cols], lands[k - 1], me.to_z(k), k - 1)
             for k in (1, 2, 3)
         ]
 
     def copy(self, i, phase, src, dst, device, k):
-        at = 5 * i + slots(self.plan.items[i][1][::-1], 3)[phase] + k
+        at = 5 * i + slots(self.plan.items[i][1][::-1], 3, 3)[phase] + k
         return remote(src, dst, self.send.at[at], self.recv.at[at], device)
 
     def start(self, i, phase):
@@ -536,29 +593,29 @@
             self.copy(i, phase, there, there, device, k).wait_recv()
 
     def add(self, i, phase):
-        t, seq, begin, count = self.plan.items[i]
+        t, seq, rows, cols = self.plan.items[i]
         me, total, got = self.me, self.total[t], self.got[i][phase]
-        rows = pl.ds(begin, count)
+        rows, cols = pl.ds(*rows), pl.ds(*cols)
         if phase == 0:
             for z in range(NZ):
                 for o in range(2):
                     at = (z, me.y, o) if seq[2] == "y" else (z, o, me.x)
-                    total[at + (rows,)] += got[z, o]
+                    total[at + (rows, cols)] += got[z, o]
         elif phase == 1 and seq[1] != "z":
             for z in range(NZ):
-                total[z, me.y, me.x, rows] += got[0, z]
+                total[z, me.y, me.x, rows, cols] += got[0, z]
         elif phase == 1:
             for o in range(2):
                 at = (me.z, me.y, o) if seq[2] == "y" else (me.z, o, me.x)
-                part = total[at + (rows,)].astype(jnp.float32)
+                part = total[at + (rows, cols)].astype(jnp.float32)
                 for k in range(3):
                     part += got[k, o].astype(jnp.float32)
-                total[at + (rows,)] = part.astype(total.dtype)
+                total[at + (rows, cols)] = part.astype(total.dtype)
         else:
-            part = total[me.z, me.y, me.x, rows].astype(jnp.float32)
+            part = total[me.z, me.y, me.x, rows, cols].astype(jnp.float32)
             for k in range(got.shape[0]):
                 part += got[k].astype(jnp.float32)
-            self.out[t][rows] = part
+            self.out[t][rows, cols] = part
 
     def finish(self, i):
         for phase in range(3):
@@ -670,10 +727,11 @@
     count = len(back.items)
     got, refs = [refs[3 * i : 3 * i + 3] for i in range(count)], refs[3 * count :]
     (gate_pad, up_pad, down_pad, gain_buf, gains, xb, h1, da, db, kx, vx, o, x1, hid), refs = refs[:14], refs[14:]
-    (dy, dyr, dh, dxr_r, qr, kr, vr, turned, pool, broad), refs = refs[:10], refs[10:]
+    (dar, dbr), refs = refs[:2], refs[2:]
+    (dy, dyr, dh, dxr_r, turned, pool, broad), refs = refs[:7], refs[7:]
     (kc, vc, rim_k, rim_v, gain_sum, gain_other), refs = refs[:6], refs[6:]
     (a_send, a_recv, own_sem, b_send, b_recv, load_sem, pool_sem, broad_sem, turn_sem), refs = refs[:9], refs[9:]
-    half_send, half_recv, clear = refs
+    half_send, half_recv = refs
     rows, width = xb.shape
     wide, columns = ahead.tensors[5][1], ahead.tensors[1][1]
     chips = NZ * NY * NX
@@ -731,11 +789,12 @@
             landed.add(t)
             gather.own_copy(t).wait()
 
-    def need(t):
-        for k in range(t + 1):
-            if k not in arrived:
-                arrived.add(k)
-                for i in ahead.of_tensor[k]:
+    def need(*tensors, part=None):
+        for t in tensors:
+            mine = ahead.of_tensor[t]
+            for i in mine if part is None else mine[part : part + 1]:
+                if i not in arrived:
+                    arrived.add(i)
                     gather.wait(i, 3)
 
     def norm(values, gain):
@@ -868,52 +927,60 @@
         each_rows(rows, 64, body)
         share("hm", 5, turn(xb, turned.at[1], rows), hm_h)
 
-    tiles = [(side, begin, min(512, wide - begin)) for side in range(2) for begin in range(0, wide, 512)]
-    stages = [(1, 0), (1, 1), (0, 0), (0, 1), (0, 2), (0, 3)]
-
-    def mlp_copies(j):
-        side, begin, size = tiles[j]
-        cols = pl.ds(begin, size)
+    strips = [ahead.items[i][3] for i in ahead.of_tensor[5]]
+
+    def strip_copies(p, side):
+        begin, size = strips[p]
         return [
             pltpu.make_async_copy(
-                flat[5 + k].at[side, :, cols], pool.at[j % 2, pl.ds(k * width, width), pl.ds(0, size)], pool_sem.at[j % 2, k]
+                flat[5 + k].at[side, :, pl.ds(begin, size)],
+                pool.at[side, pl.ds(k * width, width), pl.ds(0, size)],
+                pool_sem.at[side, k],
             )
             for k in range(2)
         ]
 
-    def mlp(j):
-        if j == 0:
-            need(6)
-            for copy in mlp_copies(0):
+    def mlp(p):
+        need(5, 6, part=p)
+        for side in range(2):
+            for copy in strip_copies(p, side):
                 copy.start()
-            later["q_out"].wait()
+        if p == 0:
             later["p_out"].wait()
-            shared("ha")
-            shared("ho")
-        if j + 1 < len(tiles):
-            for copy in mlp_copies(j + 1):
-                copy.start()
-        for copy in mlp_copies(j):
-            copy.wait()
-        side, begin, size = tiles[j]
-        which, place = stages[j]
-        lane, first = (0, place * 512) if place < 2 else (rows, (place - 2) * 512)
-        for skip in range(0, size, 256):
-            w = min(256, size - skip)
-            cols = slice(skip, skip + w)
-            a = mm(xb[...], pool[j % 2, :width, cols])
-            b = mm(xb[...], pool[j % 2, width : 2 * width, cols])
-            sig = 1.0 / (1.0 + jnp.exp(-a))
-            silu = a * sig
-            at = side * wide + begin + skip
-            db[:, at : at + w] = silu.astype(LOW)
-            da[:, at : at + w] = (b * sig * (1.0 + a * (1.0 - sig))).astype(LOW)
-            hidden = (silu * b).astype(LOW)
-            hid[side, :, begin + skip : begin + skip + w] = hidden
-            turned[which, first + skip : first + skip + w, lane : lane + rows] = hidden.T
-        at = side * wide + begin
-        mine = turned.at[which, pl.ds(first, size), pl.ds(lane, rows)]
-        share(("hid", j), 6 + j, mine, hid_h.at[pl.ds(at, size), :])
+            for name in ("ha", "ho", "hm"):
+                shared(name)
+            later["hm"] = load(hm_h, turned.at[0])
+        if p >= 2:
+            for side in range(2):
+                shared(("hid", p - 2, side))
+        begin, size = strips[p]
+        for side in range(2):
+            for copy in strip_copies(p, side):
+                copy.wait()
+            for skip in range(0, size, 256):
+                w = min(256, size - skip)
+                cols = slice(skip, skip + w)
+                a = mm(xb[...], pool[side, :width, cols])
+                b = mm(xb[...], pool[side, width : 2 * width, cols])
+                sig = 1.0 / (1.0 + jnp.exp(-a))
+                silu = a * sig
+                at = slice(side * wide + begin + skip, side * wide + begin + skip + w)
+                grad = da[:, at].astype(F32)
+                db[:, at] = (grad * silu).astype(LOW)
+                da[:, at] = (grad * b * sig * (1.0 + a * (1.0 - sig))).astype(LOW)
+                hidden_low = (silu * b).astype(LOW)
+                hid[side, :, begin + skip : begin + skip + w] = hidden_low
+                first = p % 2 * 512 + skip
+                turned[1, first : first + w, side * rows : (side + 1) * rows] = hidden_low.T
+        across = pl.ds(pl.multiple_of((1 - me.s) * wide + begin, 128), size)
+        here = pl.ds(begin, size)
+        later["db", p] = to_partner(6 + 4 * p, db.at[:, across], dbr.at[:, here])
+        later["da", p] = to_partner(7 + 4 * p, da.at[:, across], dar.at[:, here])
+        for side in range(2):
+            mine = turned.at[1, pl.ds(p % 2 * 512, size), pl.ds(side * rows, rows)]
+            share(("hid", p, side), 8 + 4 * p + side, mine, hid_h.at[pl.ds(side * wide + begin, size), :])
+        if p == len(strips) - 1:
+            mlp_tiles.prime()
 
     tall = back.tensors[0][0] * NY * NX
     hid_tiles = Stream(
@@ -934,12 +1001,7 @@
     def stream_of(fetchers, count, sems):
         return Stream(count, sems, lambda j, slot: [f(j, slot) for f in fetchers])
 
-    def down_rows(j, slot):
-        side = jnp.where(j < wide // thin, 1 - me.s, me.s)
-        at = pl.ds(pl.multiple_of(side * wide + j % (wide // thin) * thin, thin), thin)
-        return [(flat[7].at[:, at, :], small.at[slot, pl.ds(0, 2), pl.ds(0, thin), :])]
-
-    down_tiles = Stream(2 * wide // thin, pool_sem, down_rows)
+    down_tiles = stream_of([row_tiles(flat[7], tile, small_at(0))], flat[7].shape[1] // tile, pool_sem)
     mlp_tiles = stream_of([row_tiles(flat[5 + k], thin, broad_at(k)) for k in range(2)], width // thin, broad_sem)
     out_tiles = stream_of([row_tiles(flat[4], tile, small_at(0))], width // tile, pool_sem)
     qkv_tiles = stream_of([row_tiles(flat[1 + k], tile, small_at(k)) for k in range(3)], width // tile, pool_sem)
@@ -948,14 +1010,15 @@
         for i in back.of_tensor[t]:
             scatter.start(i, 0)
 
-    def put(t, z, part):
-        row_count, column_count = back.tensors[t][:2]
-        total[t][z] = part.reshape(NY, NX, row_count, column_count).astype(total[t].dtype)
+    def put(t, z, part, cols=slice(None)):
+        low = part.reshape(NY, NX, back.tensors[t][0], part.shape[1]).astype(total[t].dtype)
+        total[t][z, :, :, :, cols] = low
 
     def grad_down():
-        for j in range(len(tiles)):
-            shared(("hid", j))
-        shared("hm")
+        for p in range(len(strips)):
+            for side in range(2):
+                if p + 2 >= len(strips):
+                    shared(("hid", p, side))
         later["dy"].wait_recv()
         hid_tiles.prime()
 
@@ -965,11 +1028,10 @@
 
         hid_tiles.run(body)
         begin_scatter(0)
-        later["hm"] = load(hm_h, turned.at[0])
+        later["ha"] = load(ha_h, turned.at[0])
         later["ho"] = load(ho_h, turned.at[1])
 
     def add_down():
-        need(7)
         tiles2 = Stream(2, pool_sem, lambda j, slot: [(flat[7].at[j], pool.at[slot])])
         tiles2.prime()
 
@@ -981,49 +1043,41 @@
                 xb[:, cols] = (x1[:, cols] + part).astype(LOW)
 
         tiles2.run(body)
-        down_tiles.prime()
-        mlp_tiles.prime()
         later["mixed"] = load(xb, mixed_o)
-        pl.semaphore_signal(clear, inc=1, device_id=me.to_core(), device_id_type=MESH)
 
     def hidden_body(j, slot):
-        part = mm_nt(dy[:, :columns], small[slot, 0, :thin]) + mm_nt(dy[:, columns:], small[slot, 1, :thin])
-        side = jnp.where(j < wide // thin, 1 - me.s, me.s)
-        at = pl.ds(pl.multiple_of(side * wide + j % (wide // thin) * thin, thin), thin)
-        da[:, at] = (part * da[:, at].astype(F32)).astype(LOW)
-        db[:, at] = (part * db[:, at].astype(F32)).astype(LOW)
+        part = mm_nt(dy[:, :columns], small[slot, 0]) + mm_nt(dy[:, columns:], small[slot, 1])
+        da[:, pl.ds(pl.multiple_of(j * tile, tile), tile)] = part.astype(LOW)
 
     def hidden(k):
         middle = down_tiles.count // 2
         if k == 0:
+            need(7)
+            down_tiles.prime()
+            later["q_out"].wait()
             down_tiles.run(hidden_body, 0, middle)
-            pl.semaphore_wait(clear, 1)
-            later["db"] = to_partner(12, db.at[:, own(wide, 1)], hid.at[1])
-            later["da"] = to_partner(13, da.at[:, own(wide, 1)], hid.at[0])
             return
         down_tiles.run(hidden_body, middle)
-        out_tiles.prime()
-
-    def weight_grad_to(t, slot, mine, theirs):
+
+    def weight_grad_to(t, slot, mine, theirs, cols=slice(None)):
         row_count = back.tensors[t][0] * NY * NX
 
         def step(z, _):
             at = pl.ds(pl.multiple_of(z * row_count, 16), row_count)
-            put(t, z, mm(turned[slot, at, own(rows)], mine()) + mm(turned[slot, at, own(rows, 1)], theirs[...]))
+            put(t, z, mm(turned[slot, at, own(rows)], mine()) + mm(turned[slot, at, own(rows, 1)], theirs()), cols)
             return 0
 
         lax.fori_loop(0, NZ, step, 0)
-        begin_scatter(t)
-
-    def grad_up():
-        later["hm"].wait()
-        later["db"].wait_recv()
-        weight_grad_to(1, 0, lambda: db[:, own(wide)], hid.at[1])
-
-    def grad_gate():
-        later["da"].wait_recv()
-        weight_grad_to(2, 0, lambda: da[:, own(wide)], hid.at[0])
-        later["ha"] = load(ha_h, turned.at[0])
+
+    def grad_strip(t, name, grad, other, p):
+        begin, size = strips[p]
+        if p == 0 and t == 1:
+            later["hm"].wait()
+        later[name, p].wait_recv()
+        cols = slice(begin, begin + size)
+        mine = pl.ds(pl.multiple_of(me.s * wide + begin, 128), size)
+        weight_grad_to(t, 0, lambda: grad[:, mine], lambda: other[:, cols], cols)
+        scatter.start(back.of_tensor[t][p], 0)
 
     def dh2_body(j, slot):
         part = None
@@ -1039,8 +1093,10 @@
             mlp_tiles.run(dh2_body, 0, middle)
             return
         mlp_tiles.run(dh2_body, middle)
-        later["db"].wait_send()
-        later["da"].wait_send()
+        for p in range(len(strips)):
+            later["db", p].wait_send()
+            later["da", p].wait_send()
+        out_tiles.prime()
         later["q"] = load(q_h, da.at[:, pl.ds(0, width)])
         later["p"] = load(p_h, db.at[:, pl.ds(0, HEADS * SPAN)])
         later["mixed"].wait()
@@ -1063,7 +1119,7 @@
     def norm2():
         gain_sum[...] = jnp.zeros_like(gain_sum)
         each_rows(rows, 64, norm2_body)
-        later["dxr"] = to_partner(14, h1.at[:, own(columns, 1)], dxr_r)
+        later["dxr"] = to_partner(22, h1.at[:, own(columns, 1)], dxr_r)
 
     def out_body(j, slot):
         part = mm_nt(h1[:, :columns], small[slot, 0]) + mm_nt(h1[:, columns:], small[slot, 1])
@@ -1076,7 +1132,8 @@
     def grad_out():
         later["ho"].wait()
         later["dxr"].wait_recv()
-        weight_grad_to(3, 1, lambda: h1[:, own(columns)], dxr_r)
+        weight_grad_to(3, 1, lambda: h1[:, own(columns)], lambda: dxr_r[...])
+        begin_scatter(3)
 
     scale = HEAD_DIM ** (-0.5)
 
@@ -1110,6 +1167,7 @@
         return 0
 
     own_rows = pl.ds(WINDOW, rows)
+    qr, kr, vr = dar.at[:, pl.ds(0, columns)], dar.at[:, pl.ds(columns, columns)], dbr.at[:, pl.ds(0, columns)]
 
     def attend_back_part(k):
         if k == 0:
@@ -1122,23 +1180,25 @@
         lax.fori_loop(k * quarter, (k + 1) * quarter, attend_back, 0)
         if k == 0:
             later["rim"] = [
-                to_partner(15, kx.at[pl.ds(0, WINDOW), :], rim_k),
-                to_partner(16, vx.at[pl.ds(0, WINDOW), :], rim_v),
+                to_partner(23, kx.at[pl.ds(0, WINDOW), :], rim_k),
+                to_partner(24, vx.at[pl.ds(0, WINDOW), :], rim_v),
             ]
         if k == 3:
             for copy, ref, carry, rim_in in ((later["rim"][0], kx, kc, rim_k), (later["rim"][1], vx, vc, rim_v)):
                 copy.wait_recv()
                 ref[pl.ds(rows, WINDOW), :] = (carry[...] + rim_in[...].astype(F32)).astype(LOW)
-            later["dq"] = to_partner(17, da.at[:, own(columns, 1)], qr)
-            later["dk"] = to_partner(18, kx.at[own_rows, own(columns, 1)], kr)
-            later["dv"] = to_partner(19, vx.at[own_rows, own(columns, 1)], vr)
+            later["dq"] = to_partner(25, da.at[:, own(columns, 1)], qr)
+            later["dk"] = to_partner(26, kx.at[own_rows, own(columns, 1)], kr)
+            later["dv"] = to_partner(27, vx.at[own_rows, own(columns, 1)], vr)
 
     def grad_qkv(k):
         if k == 0:
             later["ha"].wait()
         later[("dq", "dk", "dv")[k]].wait_recv()
         mine = (lambda: da[:, own(columns)], lambda: kx[own_rows, own(columns)], lambda: vx[own_rows, own(columns)])[k]
-        weight_grad_to(4 + k, 0, mine, (qr, kr, vr)[k])
+        theirs = (qr, kr, vr)[k]
+        weight_grad_to(4 + k, 0, mine, lambda: theirs[...])
+        begin_scatter(4 + k)
 
     def dh1_body(j, slot):
         part = None
@@ -1161,7 +1221,7 @@
         later["x"].wait()
         each_rows(rows, 64, norm1_body)
         later["gtok"] = load(x1, gtok_o)
-        later["gain"] = to_partner(20, gain_sum, gain_other)
+        later["gain"] = to_partner(28, gain_sum, gain_other)
 
     def grad_gains():
         later["gain"].wait_recv()
@@ -1179,8 +1239,6 @@
         "project": add_out,
         "mix": add_down,
         "down": grad_down,
-        "up": grad_up,
-        "gate": grad_gate,
         "norm2": norm2,
         "heads": grad_heads,
         "out": grad_out,
@@ -1191,8 +1249,10 @@
     for k in range(4):
         work["see", k] = functools.partial(attend_part, k)
         work["attend", k] = functools.partial(attend_back_part, k)
-    for k in range(len(tiles)):
+    for k in range(len(strips)):
         work["mlp", k] = functools.partial(mlp, k)
+        work["up", k] = functools.partial(grad_strip, 1, "db", db, dbr, k)
+        work["gate", k] = functools.partial(grad_strip, 2, "da", da, dar, k)
     for k in range(3):
         work["qkv", k] = functools.partial(grad_qkv, k)
     for k in range(2):
@@ -1205,10 +1265,14 @@
             prepare(ahead.items[step[1]][0])
             gather.start(step[1], 0)
         elif step[0] == 0:
-            _, i, phase = step
+            _, i, phase, *hop = step
             land(ahead.items[i][0])
-            gather.wait(i, phase)
-            gather.start(i, phase + 1)
+            if hop:
+                gather.take_hop(i, phase, hop[0])
+            else:
+                gather.wait(i, phase)
+            if hop in ([], [NZ - 1]):
+                gather.start(i, phase + 1)
         else:
             _, i, phase = step
             scatter.wait(i, phase)
@@ -1219,7 +1283,7 @@
         gather.finish(i)
     for i in range(len(back.items)):
         scatter.finish(i)
-    for k in (0, 14, 15, 16, 17, 18, 19, 20):
+    for k in (0, 22, 23, 24, 25, 26, 27, 28):
         halves[k].wait_send()
     later["gtok"].wait()
 
@@ -1258,12 +1322,11 @@
         ((rows, width), LOW),
         ((rows, width), F32),
         ((2, rows, wide), LOW),
+        ((rows, wide), LOW),
+        ((rows, wide), LOW),
         ((rows, width), LOW),
         ((rows, columns), LOW),
         ((rows, width), F32),
-        ((rows, columns), LOW),
-        ((rows, columns), LOW),
-        ((rows, columns), LOW),
         ((rows, columns), LOW),
         ((2, width, 2 * rows), LOW),
         ((2, 2 * wide, columns), LOW),
@@ -1286,8 +1349,8 @@
         in_specs=[pl.BlockSpec(memory_space=pltpu.SMEM), anywhere, anywhere] + [inside] * n,
         out_specs=[anywhere] * (n - 1 + len(kept)) + [inside] * n,
         scratch_shapes=[pltpu.VMEM(*s) for s in totals + got + scratch]
-        + [dma((6 * na,)), dma((6 * na,)), dma((n,)), dma((5 * nb,)), dma((5 * nb,)), dma((24,))]
-        + [dma((2, 3)), dma((2, 2)), dma((2, 1)), dma((21,)), dma((21,)), pltpu.SemaphoreType.REGULAR],
+        + [dma((9 * na,)), dma((9 * na,)), dma((n,)), dma((5 * nb,)), dma((5 * nb,)), dma((28,))]
+        + [dma((2, 3)), dma((2, 2)), dma((2, 1)), dma((29,)), dma((29,))],
         compiler_params=pltpu.CompilerParams(
             collective_id=0, has_side_effects=True, vmem_limit_bytes=VMEM_LIMIT
         ),
@@ -1361,19 +1424,24 @@
     part = w_down.shape[0]
     tile = -(-part // 16) * 16
     wide = w_gate.shape[1] // part * tile
-    half, part16 = rows // 2, rows // 4
+    half, strip = rows // 2, -(-wide // 512) * 128
     long, short = -(-tile // 64) * 16, tile - 3 * (-(-tile // 64) * 16)
 
     def cuts(kinds, counts):
-        return tuple(zip(kinds, counts, strict=True))
+        return tuple((kind, 0, count) for kind, count in zip(kinds, counts, strict=True))
+
+    def strips(kinds):
+        return tuple((kind, 1, min(strip, wide - k * strip)) for k, kind in enumerate(kinds))
 
     return {
         "square": (rows, columns, LOW, cuts(("zfx", "zfy"), (half, half))),
-        "broad": (rows, wide, LOW, cuts(("zfx", "zfy", "zmx", "zmy"), (part16,) * 4)),
-        "broad_f": (rows, wide, LOW, cuts(("zfx", "zfy", "zfx", "zfy"), (part16,) * 4)),
+        "broad": (rows, wide, LOW, strips(("zfx", "zfy", "zmx", "zmy"))),
+        "broad_f": (rows, wide, LOW, strips(("zfx", "zfy", "zfx", "zfy"))),
+        "broad_m": (rows, wide, LOW, strips(("zmx", "zmy", "zmx", "zmy"))),
         "tall": (tile, columns, LOW, cuts(("zfx", "zfy", "zmx", "zmy"), (long, long, long, short))),
         "square_m": (rows, columns, LOW, cuts(("zmx", "zmy"), (half, half))),
         "tall_f": (tile, columns, LOW, cuts(("zfx", "zfy", "zfx", "zfy"), (long, long, long, short))),
+        "tall_m": (tile, columns, LOW, cuts(("zmx", "zmy", "zmx", "zmy"), (long, long, long, short))),
         "gain": (16, 2 * rows, LOW, cuts(("zfx",), (16,))),
         "gain_grad": (8, 2 * rows, F32, cuts(("zfx",), (8,))),
     }
@@ -1381,7 +1449,7 @@
 
 def gather_plan(w_query, w_key, w_value, w_out, w_gate, w_up, w_down, gain_attn, gain_mlp):
     kind = kinds(w_query, w_gate, w_down)
-    names = ("gain", "square", "square", "square", "square", "broad", "broad", "tall")
+    names = ("gain", "square", "square", "square_m", "square_m", "broad", "broad", "tall_m")
     plan = Plan([kind[name] for name in names])
     rows = w_query.shape[0]
     both = jnp.stack([gain_attn, gain_mlp])
@@ -1417,7 +1485,7 @@
 ):
     plan, shards = gather_plan(w_query, w_key, w_value, w_out, w_gate, w_up, w_down, gain_attn, gain_mlp)
     kind = kinds(w_query, w_gate, w_down)
-    names = ("tall_f", "broad_f", "broad_f", "square", "square", "square", "square", "gain_grad")
+    names = ("tall", "broad_f", "broad", "square", "square", "square", "square", "gain_grad")
     back = Plan([kind[name] for name in names])
     results, sums = block_all(plan, back, seq_lengths, tokens, cotangent, shards)
     outs = finish_all(results[0], results[1], sums, w_query, w_gate, w_down)

time: 261 us -> 250 us (0.958)
  Pallas kernels: 258 us -> 247 us
    pallas_call x1, Pallas kernels: 253 us -> 243 us  [block_all(): pl.pallas_call(functools.partial(block_kernel, ahead, back), out_shape=[s...]
where the time goes in v5:
time: 250 us
  Pallas kernels  247 us (99%)
    pallas_call x1, Pallas kernels, block_all(): pl.pallas_call(functools.partial(block_kernel, ahead, back), out_shape=[s...  243 us

profile of v5, /device:TPU:0, one launch (start us, length us, event | category | flops | bytes accessed | tf_op | source)
XLA Modules:
  0.0 249.6 jit_solution(4042189704748368983)
XLA Ops:
  0.7 0.7 pad_maximum_fusion
  1.3 0.7 pad_select_fusion.refs_3_
  2.0 242.6 %block_all.1 = (bf16[2,4,2,2,64,512]{5,4,3,2,1,0:T(8,128)(2,1)}, bf16[2,4,2,2,64,512]{5,4,3,2,1,0:T(8,128)(2,1)}, bf16[2,4,2,2,64,512]{5,4,3,2,1,0:T(8,128)(2,1)...) custom-call(s32[1,3]{1,0:T(1,128)} %refs_0_.1, ...), custom_call_target="tpu_custom_call" | custom-call | tf_op jit(solution)/shard_map/block_all/pallas_call | solution.py:1344
  244.6 4.8 %finish_all.1 = (bf16[512,1024]{1,0:T(8,128)(2,1)}, f32[512,1024]{1,0:T(8,128)}, f32[64,512]{1,0:T(8,128)}, f32[64,512]{1,0:T(8,128)}, f32[64,512]{1,0:T(8,128)}...) custom-call(bf16[512,1024]{1,0:T(8,128)(2,1)} %get-tuple-element.32., ...), custom_call_target="tpu_custom_call" | custom-call | tf_op jit(solution)/shard_map/finish_all/pallas_call | solution.py:1410

commit v6 on v5

--- a/solution.py
+++ b/solution.py
@@ -349,35 +349,35 @@
 
 
 SCRIPT = (
-    ("start", 7), ("start", 14), ("start", 4), ("start", 1), ("start", 20), ("start", 0), ("start", 18),
-    ("start", 16), ("start", 6), ("start", 3), ("start", 5), ("start", 9), ("start", 10), (0, 0, 0, 1),
-    (0, 5, 0), (0, 4, 0, 1), (0, 3, 0, 1), (0, 9, 0, 1), ("start", 11), (0, 1, 0, 1), (0, 5, 1, 1),
-    (0, 3, 0, 2), (0, 0, 0, 2), (0, 4, 0, 2), ("start", 19), (0, 20, 0), (0, 5, 1, 2), ("start", 2),
-    (0, 4, 0, 3), (0, 0, 0, 3), ("start", 12), (0, 3, 0, 3), (0, 19, 0), ("start", 17), (0, 0, 1),
-    (0, 14, 0, 1), ("start", 15), (0, 2, 0, 1), (0, 6, 0), ("start", 13), (0, 5, 1, 3), (0, 20, 1, 1),
-    (0, 9, 0, 2), (0, 4, 1), (0, 9, 0, 3), (0, 2, 0, 2), (0, 3, 1), (0, 18, 0), (0, 19, 1, 1), (0, 20, 1, 2),
-    ("start", 8), (0, 2, 0, 3), (0, 0, 2), (0, 1, 0, 2), (0, 18, 1, 1), (0, 9, 1), (0, 6, 1, 1), (0, 1, 0, 3),
-    (0, 19, 1, 2), (0, 5, 2), (0, 2, 1), (0, 14, 0, 2), (0, 3, 2), (0, 8, 0), (0, 6, 1, 2), (0, 12, 0),
-    (0, 19, 1, 3), (0, 17, 0), (0, 16, 0), (0, 20, 1, 3), (0, 13, 0, 1), "norm", (0, 6, 1, 3), (0, 8, 1, 1),
-    (0, 18, 1, 2), (0, 7, 0), (0, 14, 0, 3), (0, 18, 1, 3), (0, 2, 2), (0, 17, 1, 1), (0, 17, 1, 2),
-    (0, 7, 1, 1), (0, 1, 1), (0, 4, 2), (0, 17, 1, 3), (0, 6, 2), (0, 14, 1), (0, 19, 2), (0, 11, 0),
-    (0, 10, 0, 1), (0, 10, 0, 2), (0, 15, 0), (0, 7, 1, 2), "value", (0, 9, 2), (0, 10, 0, 3), (0, 18, 2),
-    (0, 1, 2), (0, 8, 1, 2), (0, 7, 1, 3), (0, 13, 0, 2), (0, 13, 0, 3), (0, 11, 1, 1), "key", (0, 8, 1, 3),
-    (0, 14, 2), "query", ("see", 0), (0, 20, 2), (0, 13, 1), ("see", 1), (0, 16, 1, 1), (0, 10, 1),
-    (0, 12, 1, 1), (0, 17, 2), (0, 15, 1, 1), ("see", 2), (0, 7, 2), (0, 8, 2), ("see", 3), (0, 11, 1, 2),
-    ("hidden", 0), (0, 15, 1, 2), (0, 11, 1, 3), (0, 12, 1, 2), ("hidden", 1), (0, 16, 1, 2), (0, 13, 2),
-    "project", (0, 15, 1, 3), (0, 16, 1, 3), (0, 10, 2), ("mlp", 0), (0, 12, 1, 3), (0, 11, 2), ("mlp", 1),
-    ("up", 0), ("gate", 0), (0, 15, 2), ("gate", 1), ("up", 1), (0, 12, 2), (0, 16, 2), ("mlp", 2),
-    ("mlp", 3), ("gate", 2), (1, 8, 0), ("dh2", 0), ("up", 2), ("up", 3), (1, 5, 0), (1, 4, 0), ("gate", 3),
-    (1, 8, 1), (1, 9, 0), (1, 10, 0), "mix", "down", (1, 5, 1), ("dh2", 1), (1, 9, 1), "norm2", (1, 11, 0),
-    "heads", "out", ("attend", 0), (1, 3, 0), ("attend", 1), (1, 6, 0), (1, 4, 1), ("attend", 2), (1, 1, 0),
-    ("attend", 3), (1, 2, 0), (1, 7, 0), (1, 0, 0), (1, 6, 1), ("qkv", 0), "dh1", (1, 8, 2), (1, 7, 1),
-    ("qkv", 1), (1, 3, 1), (1, 9, 2), (1, 13, 0), (1, 15, 0), (1, 1, 1), (1, 14, 0), (1, 0, 1), "norm1",
-    (1, 5, 2), (1, 3, 2), ("qkv", 2), (1, 12, 0), (1, 14, 1), "gains", (1, 2, 1), (1, 17, 0), (1, 15, 1),
-    (1, 13, 1), (1, 16, 0), (1, 1, 2), (1, 12, 1), (1, 6, 2), (1, 19, 0), (1, 2, 2), (1, 10, 1), (1, 17, 1),
-    (1, 18, 0), (1, 0, 2), (1, 15, 2), (1, 16, 1), (1, 20, 0), (1, 12, 2), (1, 19, 1), (1, 13, 2), (1, 11, 1),
-    (1, 7, 2), (1, 14, 2), (1, 10, 2), (1, 20, 1), (1, 17, 2), (1, 18, 1), (1, 16, 2), (1, 20, 2), (1, 19, 2),
-    (1, 4, 2), (1, 11, 2), (1, 18, 2),
+    ("start", 7), ("start", 6), ("start", 8), ("start", 2), ("start", 5), ("start", 9), ("start", 3),
+    ("start", 0), ("start", 10), ("start", 17), ("start", 4), (0, 4, 0), ("start", 13), ("start", 1),
+    ("start", 19), (0, 7, 0, 1), ("start", 18), ("start", 12), (0, 9, 0, 1), ("start", 15), ("start", 16),
+    (0, 8, 0, 1), ("start", 14), (0, 1, 0, 1), (0, 17, 0), (0, 8, 0, 2), (0, 0, 0, 1), (0, 2, 0, 1),
+    (0, 14, 0), (0, 1, 0, 2), (0, 7, 0, 2), (0, 0, 0, 2), (0, 4, 1, 1), (0, 0, 0, 3), ("start", 20),
+    (0, 5, 0), (0, 2, 0, 2), (0, 9, 0, 2), (0, 8, 0, 3), (0, 1, 0, 3), (0, 6, 0), (0, 1, 1), (0, 0, 1),
+    (0, 3, 0), (0, 4, 1, 2), (0, 18, 0), (0, 2, 0, 3), (0, 9, 0, 3), (0, 0, 2), (0, 4, 1, 3), (0, 7, 0, 3),
+    (0, 19, 0), (0, 9, 1), (0, 17, 1, 1), (0, 5, 1, 1), (0, 2, 1), (0, 6, 1, 1), (0, 15, 0), (0, 19, 1, 1),
+    (0, 7, 1), (0, 5, 1, 2), (0, 8, 1), (0, 3, 1, 1), (0, 20, 0), (0, 6, 1, 2), (0, 3, 1, 2), (0, 5, 1, 3),
+    (0, 17, 1, 2), (0, 20, 1, 1), (0, 6, 1, 3), "norm", (0, 16, 0), (0, 1, 2), (0, 3, 1, 3), (0, 20, 1, 2),
+    (0, 18, 1, 1), (0, 20, 1, 3), (0, 2, 2), (0, 5, 2), (0, 13, 0), (0, 19, 1, 2), (0, 17, 1, 3), (0, 6, 2),
+    (0, 18, 1, 2), (0, 10, 0, 1), ("start", 11), (0, 7, 2), (0, 3, 2), (0, 10, 0, 2), (0, 15, 1, 1), "query",
+    (0, 10, 0, 3), (0, 18, 1, 3), (0, 4, 2), (0, 13, 1, 1), "value", (0, 11, 0), (0, 17, 2), (0, 12, 0),
+    (0, 19, 1, 3), (0, 14, 1, 1), "key", (0, 13, 1, 2), (0, 10, 1), (0, 8, 2), ("see", 0), ("see", 1),
+    (0, 16, 1, 1), (0, 9, 2), (0, 13, 1, 3), ("see", 2), (0, 14, 1, 2), ("see", 3), (0, 15, 1, 2), (0, 19, 2),
+    (0, 20, 2), (0, 14, 1, 3), (0, 16, 1, 2), (0, 12, 1, 1), (0, 18, 2), (0, 11, 1, 1), "project",
+    (0, 15, 1, 3), (0, 12, 1, 2), (0, 10, 2), (0, 13, 2), ("hidden", 0), (0, 16, 1, 3), (0, 11, 1, 2),
+    ("hidden", 1), (0, 11, 1, 3), (0, 12, 1, 3), (0, 14, 2), ("mlp", 0), ("mlp", 1), ("up", 0), ("gate", 0),
+    (0, 15, 2), (0, 11, 2), ("up", 1), ("gate", 1), (0, 12, 2), (0, 16, 2), ("mlp", 2), ("mlp", 3),
+    ("gate", 2), (1, 4, 0), "mix", ("gate", 3), (1, 5, 0), ("up", 2), (1, 4, 1), ("up", 3), (1, 8, 0),
+    (1, 10, 0), "down", (1, 5, 1), ("dh2", 0), (1, 11, 0), ("dh2", 1), (1, 8, 1), "norm2", "heads",
+    ("attend", 0), (1, 10, 1), "out", (1, 3, 0), ("attend", 1), ("attend", 2), (1, 2, 0), (1, 7, 0),
+    (1, 9, 0), ("attend", 3), (1, 6, 0), (1, 8, 2), (1, 13, 0), (1, 1, 0), (1, 0, 0), "dh1", ("qkv", 0),
+    (1, 6, 1), (1, 7, 1), (1, 12, 0), (1, 0, 1), (1, 13, 1), ("qkv", 1), "norm1", (1, 2, 1), (1, 10, 2),
+    (1, 9, 1), (1, 1, 1), (1, 5, 2), (1, 14, 0), (1, 12, 1), (1, 15, 0), "gains", ("qkv", 2), (1, 17, 0),
+    (1, 2, 2), (1, 20, 0), (1, 13, 2), (1, 14, 1), (1, 20, 1), (1, 16, 0), (1, 0, 2), (1, 15, 1), (1, 17, 1),
+    (1, 19, 0), (1, 18, 0), (1, 16, 1), (1, 14, 2), (1, 4, 2), (1, 19, 1), (1, 15, 2), (1, 1, 2), (1, 20, 2),
+    (1, 12, 2), (1, 11, 1), (1, 3, 1), (1, 18, 1), (1, 16, 2), (1, 6, 2), (1, 7, 2), (1, 9, 2), (1, 17, 2),
+    (1, 19, 2), (1, 3, 2), (1, 11, 2), (1, 18, 2),
 )
 
 
@@ -722,12 +722,13 @@
     (lens, x_h, dy_h), raw, refs = refs[:3], refs[3 : 3 + n], refs[3 + n :]
     hbm_bufs, refs = refs[: n - 1], refs[n - 1 :]
     (mixed_o, gtok_o, q_h, p_h, ha_h, ho_h, hm_h, hid_h), refs = refs[:8], refs[8:]
+    outs_h, refs = refs[:n], refs[n:]
     outs, refs = refs[:n], refs[n:]
     total, refs = refs[:n], refs[n:]
     count = len(back.items)
     got, refs = [refs[3 * i : 3 * i + 3] for i in range(count)], refs[3 * count :]
     (gate_pad, up_pad, down_pad, gain_buf, gains, xb, h1, da, db, kx, vx, o, x1, hid), refs = refs[:14], refs[14:]
-    (dar, dbr), refs = refs[:2], refs[2:]
+    (dar, dbr, pair_of, pair_low), refs = refs[:4], refs[4:]
     (dy, dyr, dh, dxr_r, turned, pool, broad), refs = refs[:7], refs[7:]
     (kc, vc, rim_k, rim_v, gain_sum, gain_other), refs = refs[:6], refs[6:]
     (a_send, a_recv, own_sem, b_send, b_recv, load_sem, pool_sem, broad_sem, turn_sem), refs = refs[:9], refs[9:]
@@ -755,7 +756,14 @@
 
     get_x, get_dy = load(x_h, xb), load(dy_h, dy)
     me.greet()
-    shards = list(raw[:5]) + [gate_pad, up_pad, down_pad]
+    pair_of[...] = jnp.zeros_like(pair_of)
+    blank = jnp.zeros((1, raw[0].shape[1]), F32)
+    for k in range(2):
+        gain = raw[0][k : k + 1, :].astype(F32)
+        left, right = jnp.concatenate([gain, blank], axis=1), jnp.concatenate([blank, gain], axis=1)
+        pair_of[k : k + 1, :] = jnp.where(me.x == 0, left, right)
+    pair_low[...] = pair_of[...].astype(LOW)
+    shards = [pair_low] + list(raw[1:5]) + [gate_pad, up_pad, down_pad]
     bufs = [gain_buf] + list(hbm_bufs)
     flat = [b.reshape(2, chips * b.shape[4], b.shape[5]) for b in bufs]
     gather = Gather(ahead, me, shards, bufs, a_send, a_recv, own_sem)
@@ -1258,6 +1266,7 @@
     for k in range(2):
         work["hidden", k] = functools.partial(hidden, k)
         work["dh2", k] = functools.partial(grad_norm2, k)
+    summed = []
     for step in SCRIPT:
         if step in work:
             work[step]()
@@ -1279,6 +1288,11 @@
             scatter.add(i, phase)
             if phase < 2:
                 scatter.start(i, phase + 1)
+                continue
+            t = back.items[i][0]
+            summed.append(i)
+            if all(k in summed for k in back.of_tensor[t]):
+                later["sum", t] = load(outs[t], outs_h[t])
     for i in range(len(ahead.items)):
         gather.finish(i)
     for i in range(len(back.items)):
@@ -1286,6 +1300,8 @@
     for k in (0, 22, 23, 24, 25, 26, 27, 28):
         halves[k].wait_send()
     later["gtok"].wait()
+    for t in range(n):
+        later["sum", t].wait()
 
 
 def block_all(ahead, back, lens, tokens, cotangent, shards):
@@ -1324,6 +1340,8 @@
         ((2, rows, wide), LOW),
         ((rows, wide), LOW),
         ((rows, wide), LOW),
+        (ahead.tensors[0][:2], F32),
+        (ahead.tensors[0][:2], LOW),
         ((rows, width), LOW),
         ((rows, columns), LOW),
         ((rows, width), F32),
@@ -1338,6 +1356,7 @@
         ((8, width), F32),
         ((8, width), F32),
     ]
+    results = [(t[:2], F32) for t in back.tensors]
     totals = [((NZ, NY, NX) + t[:2], t[2]) for t in back.tensors]
     got = [part for parts in got_shapes(back) for part in parts]
     dma = pltpu.SemaphoreType.DMA
@@ -1347,9 +1366,9 @@
         + [shape(*s) for s in kept]
         + [shape(t[:2], F32) for t in back.tensors],
         in_specs=[pl.BlockSpec(memory_space=pltpu.SMEM), anywhere, anywhere] + [inside] * n,
-        out_specs=[anywhere] * (n - 1 + len(kept)) + [inside] * n,
-        scratch_shapes=[pltpu.VMEM(*s) for s in totals + got + scratch]
-        + [dma((9 * na,)), dma((9 * na,)), dma((n,)), dma((5 * nb,)), dma((5 * nb,)), dma((28,))]
+        out_specs=[anywhere] * (n - 1 + len(kept) + n),
+        scratch_shapes=[pltpu.VMEM(*s) for s in results + totals + got + scratch]
+        + [dma((9 * na,)), dma((9 * na,)), dma((n,)), dma((5 * nb,)), dma((5 * nb,)), dma((36,))]
         + [dma((2, 3)), dma((2, 2)), dma((2, 1)), dma((29,)), dma((29,))],
         compiler_params=pltpu.CompilerParams(
             collective_id=0, has_side_effects=True, vmem_limit_bytes=VMEM_LIMIT
@@ -1449,15 +1468,11 @@
 
 def gather_plan(w_query, w_key, w_value, w_out, w_gate, w_up, w_down, gain_attn, gain_mlp):
     kind = kinds(w_query, w_gate, w_down)
-    names = ("gain", "square", "square", "square_m", "square_m", "broad", "broad", "tall_m")
+    names = ("gain", "square", "square_m", "square_m", "square", "broad", "broad_m", "tall_m")
     plan = Plan([kind[name] for name in names])
-    rows = w_query.shape[0]
-    both = jnp.stack([gain_attn, gain_mlp])
-    left = jnp.pad(both, ((0, 14), (0, rows)))
-    right = jnp.pad(both, ((0, 14), (rows, 0)))
-    pair = jnp.where(lax.axis_index("dp") % 2 == 0, left, right)
+    both = jnp.concatenate([gain_attn[None], gain_mlp[None]], axis=0)
     shards = [
-        pair,
+        both,
         w_query,
         w_key,
         w_value,

time: 250 us -> 241 us (0.964)
  Pallas kernels: 247 us -> 238 us
    pallas_call x1, Pallas kernels: 243 us -> 233 us  [block_all(): pl.pallas_call(functools.partial(block_kernel, ahead, back), out_shape=[s...]
where the time goes in v6:
time: 241 us; the launch traced here: 240 us
  Pallas kernels  238 us (99%)
    pallas_call x1, Pallas kernels, block_all(): pl.pallas_call(functools.partial(block_kernel, ahead, back), out_shape=[s...  233 us

profile of v6, /device:TPU:0, one launch (start us, length us, event | category | flops | bytes accessed | tf_op | source)
XLA Modules:
  0.0 240.0 jit_solution(16690227026997561497)
XLA Ops:
  0.6 1.2 pad_maximum_fusion.refs_3_
  1.8 233.2 %block_all.1 = (bf16[2,4,2,2,64,512]{5,4,3,2,1,0:T(8,128)(2,1)}, bf16[2,4,2,2,64,512]{5,4,3,2,1,0:T(8,128)(2,1)}, bf16[2,4,2,2,64,512]{5,4,3,2,1,0:T(8,128)(2,1)...) custom-call(s32[1,3]{1,0:T(1,128)} %refs_0_.1, ...), custom_call_target="tpu_custom_call" | custom-call | tf_op jit(solution)/shard_map/block_all/pallas_call | solution.py:1363
  235.1 4.8 %finish_all.1 = (bf16[512,1024]{1,0:T(8,128)(2,1)}, f32[512,1024]{1,0:T(8,128)}, f32[64,512]{1,0:T(8,128)}, f32[64,512]{1,0:T(8,128)}, f32[64,512]{1,0:T(8,128)}...) custom-call(bf16[512,1024]{1,0:T(8,128)(2,1)} %get-tuple-element.32., ...), custom_call_target="tpu_custom_call" | custom-call | tf_op jit(solution)/shard_map/finish_all/pallas_call | solution.py:1429

commit v7 on v6

--- a/solution.py
+++ b/solution.py
@@ -349,41 +349,43 @@
 
 
 SCRIPT = (
-    ("start", 7), ("start", 6), ("start", 8), ("start", 2), ("start", 5), ("start", 9), ("start", 3),
-    ("start", 0), ("start", 10), ("start", 17), ("start", 4), (0, 4, 0), ("start", 13), ("start", 1),
-    ("start", 19), (0, 7, 0, 1), ("start", 18), ("start", 12), (0, 9, 0, 1), ("start", 15), ("start", 16),
-    (0, 8, 0, 1), ("start", 14), (0, 1, 0, 1), (0, 17, 0), (0, 8, 0, 2), (0, 0, 0, 1), (0, 2, 0, 1),
-    (0, 14, 0), (0, 1, 0, 2), (0, 7, 0, 2), (0, 0, 0, 2), (0, 4, 1, 1), (0, 0, 0, 3), ("start", 20),
-    (0, 5, 0), (0, 2, 0, 2), (0, 9, 0, 2), (0, 8, 0, 3), (0, 1, 0, 3), (0, 6, 0), (0, 1, 1), (0, 0, 1),
-    (0, 3, 0), (0, 4, 1, 2), (0, 18, 0), (0, 2, 0, 3), (0, 9, 0, 3), (0, 0, 2), (0, 4, 1, 3), (0, 7, 0, 3),
-    (0, 19, 0), (0, 9, 1), (0, 17, 1, 1), (0, 5, 1, 1), (0, 2, 1), (0, 6, 1, 1), (0, 15, 0), (0, 19, 1, 1),
-    (0, 7, 1), (0, 5, 1, 2), (0, 8, 1), (0, 3, 1, 1), (0, 20, 0), (0, 6, 1, 2), (0, 3, 1, 2), (0, 5, 1, 3),
-    (0, 17, 1, 2), (0, 20, 1, 1), (0, 6, 1, 3), "norm", (0, 16, 0), (0, 1, 2), (0, 3, 1, 3), (0, 20, 1, 2),
-    (0, 18, 1, 1), (0, 20, 1, 3), (0, 2, 2), (0, 5, 2), (0, 13, 0), (0, 19, 1, 2), (0, 17, 1, 3), (0, 6, 2),
-    (0, 18, 1, 2), (0, 10, 0, 1), ("start", 11), (0, 7, 2), (0, 3, 2), (0, 10, 0, 2), (0, 15, 1, 1), "query",
-    (0, 10, 0, 3), (0, 18, 1, 3), (0, 4, 2), (0, 13, 1, 1), "value", (0, 11, 0), (0, 17, 2), (0, 12, 0),
-    (0, 19, 1, 3), (0, 14, 1, 1), "key", (0, 13, 1, 2), (0, 10, 1), (0, 8, 2), ("see", 0), ("see", 1),
-    (0, 16, 1, 1), (0, 9, 2), (0, 13, 1, 3), ("see", 2), (0, 14, 1, 2), ("see", 3), (0, 15, 1, 2), (0, 19, 2),
-    (0, 20, 2), (0, 14, 1, 3), (0, 16, 1, 2), (0, 12, 1, 1), (0, 18, 2), (0, 11, 1, 1), "project",
-    (0, 15, 1, 3), (0, 12, 1, 2), (0, 10, 2), (0, 13, 2), ("hidden", 0), (0, 16, 1, 3), (0, 11, 1, 2),
-    ("hidden", 1), (0, 11, 1, 3), (0, 12, 1, 3), (0, 14, 2), ("mlp", 0), ("mlp", 1), ("up", 0), ("gate", 0),
-    (0, 15, 2), (0, 11, 2), ("up", 1), ("gate", 1), (0, 12, 2), (0, 16, 2), ("mlp", 2), ("mlp", 3),
-    ("gate", 2), (1, 4, 0), "mix", ("gate", 3), (1, 5, 0), ("up", 2), (1, 4, 1), ("up", 3), (1, 8, 0),
-    (1, 10, 0), "down", (1, 5, 1), ("dh2", 0), (1, 11, 0), ("dh2", 1), (1, 8, 1), "norm2", "heads",
-    ("attend", 0), (1, 10, 1), "out", (1, 3, 0), ("attend", 1), ("attend", 2), (1, 2, 0), (1, 7, 0),
-    (1, 9, 0), ("attend", 3), (1, 6, 0), (1, 8, 2), (1, 13, 0), (1, 1, 0), (1, 0, 0), "dh1", ("qkv", 0),
-    (1, 6, 1), (1, 7, 1), (1, 12, 0), (1, 0, 1), (1, 13, 1), ("qkv", 1), "norm1", (1, 2, 1), (1, 10, 2),
-    (1, 9, 1), (1, 1, 1), (1, 5, 2), (1, 14, 0), (1, 12, 1), (1, 15, 0), "gains", ("qkv", 2), (1, 17, 0),
-    (1, 2, 2), (1, 20, 0), (1, 13, 2), (1, 14, 1), (1, 20, 1), (1, 16, 0), (1, 0, 2), (1, 15, 1), (1, 17, 1),
-    (1, 19, 0), (1, 18, 0), (1, 16, 1), (1, 14, 2), (1, 4, 2), (1, 19, 1), (1, 15, 2), (1, 1, 2), (1, 20, 2),
-    (1, 12, 2), (1, 11, 1), (1, 3, 1), (1, 18, 1), (1, 16, 2), (1, 6, 2), (1, 7, 2), (1, 9, 2), (1, 17, 2),
-    (1, 19, 2), (1, 3, 2), (1, 11, 2), (1, 18, 2),
+    ("start", 4), ("start", 7), ("start", 9), ("start", 0), ("start", 13), ("start", 2), ("start", 11),
+    ("start", 5), ("start", 10), (0, 4, 0), ("start", 18), ("start", 15), ("start", 19), ("start", 20),
+    (0, 0, 0, 1), ("start", 6), ("start", 3), (0, 5, 0), (0, 10, 0, 1), ("start", 1), (0, 9, 0, 1), (0, 6, 0),
+    (0, 5, 1, 1), (0, 2, 0, 1), ("start", 16), (0, 9, 0, 2), (0, 0, 0, 2), (0, 1, 0, 1), (0, 10, 0, 2),
+    ("start", 17), ("start", 12), (0, 18, 0), (0, 0, 0, 3), ("start", 14), (0, 3, 0), (0, 1, 0, 2),
+    (0, 2, 0, 2), (0, 0, 1), (0, 9, 0, 3), (0, 10, 0, 3), (0, 2, 0, 3), (0, 20, 0), (0, 18, 1, 1), (0, 0, 2),
+    (0, 3, 1, 1), (0, 4, 1, 1), (0, 9, 1), (0, 7, 0, 1), (0, 1, 0, 3), (0, 12, 0), (0, 17, 0), (0, 19, 0),
+    (0, 2, 1), (0, 5, 1, 2), (0, 6, 1, 1), (0, 4, 1, 2), ("start", 8), (0, 1, 1), (0, 10, 1), (0, 3, 1, 2),
+    "norm", (0, 8, 0, 1), (0, 2, 2), (0, 5, 1, 3), (0, 7, 0, 2), (0, 8, 0, 2), (0, 7, 0, 3), (0, 20, 1, 1),
+    (0, 19, 1, 1), (0, 9, 2), (0, 1, 2), (0, 13, 0), (0, 17, 1, 1), (0, 6, 1, 2), (0, 4, 1, 3), (0, 3, 1, 3),
+    (0, 5, 2), (0, 8, 0, 3), (0, 6, 1, 3), (0, 20, 1, 2), (0, 17, 1, 2), (0, 18, 1, 2), (0, 7, 1), (0, 10, 2),
+    (0, 3, 2), (0, 4, 2), (0, 11, 0), "query", (0, 8, 1), (0, 18, 1, 3), (0, 14, 0), (0, 17, 1, 3),
+    (0, 13, 1, 1), (0, 16, 0), (0, 6, 2), "key", (0, 19, 1, 2), "value", (0, 19, 1, 3), (0, 16, 1, 1),
+    (0, 14, 1, 1), (0, 13, 1, 2), (0, 20, 1, 3), (0, 15, 0), ("see", 0), (0, 7, 2), (0, 8, 2), (0, 11, 1, 1),
+    ("see", 1), (0, 17, 2), (0, 13, 1, 3), ("see", 2), (0, 14, 1, 2), ("see", 3), (0, 12, 1, 1), (0, 18, 2),
+    (0, 14, 1, 3), (0, 19, 2), (0, 11, 1, 2), (0, 20, 2), (0, 15, 1, 1), "project", (0, 16, 1, 2), (0, 13, 2),
+    (0, 11, 1, 3), (0, 15, 1, 2), (0, 12, 1, 2), ("hidden", 0), ("hidden", 1), (0, 15, 1, 3), (0, 16, 1, 3),
+    (0, 14, 2), (0, 12, 1, 3), ("mlp", 0), ("mlp", 1), ("up", 0), (0, 11, 2), ("gate", 0), (0, 15, 2),
+    ("gate", 1), ("up", 1), (0, 12, 2), (0, 16, 2), ("mlp", 2), ("mlp", 3), (1, 9, 0), ("up", 2), (1, 8, 0),
+    ("dh2", 0), ("gate", 2), ("gate", 3), ("up", 3), "mix", (1, 9, 1), (1, 8, 1), "down", (1, 11, 0),
+    ("dh2", 1), "norm2", (1, 10, 0), "heads", (1, 6, 0), (1, 7, 0), ("attend", 0), ("attend", 1),
+    ("attend", 2), ("attend", 3), (1, 3, 0), "out", (1, 6, 1), (1, 0, 0), ("qkv", 0), (1, 2, 0), "dh1",
+    (1, 1, 0), (1, 7, 1), ("qkv", 1), (1, 14, 0), (1, 9, 2), (1, 0, 1), (1, 13, 0), "norm1", (1, 1, 1),
+    (1, 15, 0), (1, 12, 0), ("qkv", 2), (1, 14, 1), (1, 7, 2), "gains", (1, 13, 1), (1, 6, 2), (1, 12, 1),
+    (1, 16, 0), (1, 15, 1), (1, 17, 0), (1, 20, 0), (1, 5, 0), (1, 19, 0), (1, 18, 0), (1, 20, 1), (1, 0, 2),
+    (1, 10, 1), (1, 17, 1), (1, 4, 0), (1, 16, 1), (1, 2, 1), (1, 19, 1), (1, 11, 1), (1, 13, 2), (1, 20, 2),
+    (1, 14, 2), (1, 3, 1), (1, 8, 2), (1, 5, 1), (1, 18, 1), (1, 1, 2), (1, 4, 1), (1, 11, 2), (1, 15, 2),
+    (1, 12, 2), (1, 10, 2), (1, 2, 2), (1, 17, 2), (1, 16, 2), (1, 5, 2), (1, 3, 2), (1, 4, 2), (1, 19, 2),
+    (1, 18, 2),
 )
+GATHER_KINDS = (("gain", "f"), ("square", "f"), ("square", "m"), ("square", "m"), ("square", "f"), ("broad", "fm"), ("broad", "mm"), ("tall", "mm"))
+SCATTER_KINDS = (("tall", "fm"), ("broad", "lf"), ("broad", "fm"), ("square", "f"), ("square", "f"), ("square", "f"), ("square", "f"), ("gain_grad", "f"))
 
 
 MESH = pl.DeviceIdType.MESH
 NZ, NY, NX = 4, 2, 2
-SEQUENCE = {"zfx": "zxy", "zfy": "zyx", "zmx": "xzy", "zmy": "yzx"}
+SEQUENCE = {"zfx": "zxy", "zfy": "zyx", "zmx": "xzy", "zmy": "yzx", "zlx": "xyz", "zly": "yxz"}
 ALL_Z, ALL_Y, ALL_X = pl.ds(0, NZ), pl.ds(0, NY), pl.ds(0, NX)
 
 
@@ -549,8 +551,9 @@
     shapes = []
     for t, seq, (_, rows), (_, columns) in plan.items:
         dtype = plan.tensors[t][2]
-        second, third = ((1, NZ), (3,)) if seq[0] == "z" else ((3, 2), (1,))
-        shapes.append([(d + (rows, columns), dtype) for d in ((NZ, 2), second, third)])
+        leads = {"z": ((NZ, 2), (1, NZ), (3,)), "m": ((NZ, 2), (3, 2), (1,)), "l": ((3, 2, 2), (1, 2), (1,))}
+        lead = leads["zml"[seq.index("z")]]
+        shapes.append([(d + (rows, columns), dtype) for d in lead])
     return shapes
 
 
@@ -567,7 +570,7 @@
         z = me.z if "z" in done else ALL_Z
         y = me.y if "y" in done else ALL_Y
         x = me.x if "x" in done else ALL_X
-        if phase == 0:
+        if phase == 0 and axis != "z":
             lands = [got]
         else:
             lands = [got.at[k] for k in range(got.shape[0])]
@@ -596,7 +599,18 @@
         t, seq, rows, cols = self.plan.items[i]
         me, total, got = self.me, self.total[t], self.got[i][phase]
         rows, cols = pl.ds(*rows), pl.ds(*cols)
-        if phase == 0:
+        if phase == 0 and seq[2] == "z":
+            for y in range(NY):
+                for x in range(NX):
+                    part = total[me.z, y, x, rows, cols].astype(jnp.float32)
+                    for k in range(3):
+                        part += got[k, y, x].astype(jnp.float32)
+                    total[me.z, y, x, rows, cols] = part.astype(total.dtype)
+        elif phase == 1 and seq[2] == "z":
+            for o in range(2):
+                at = (me.z, me.y, o) if seq[1] == "y" else (me.z, o, me.x)
+                total[at + (rows, cols)] += got[0, o]
+        elif phase == 0:
             for z in range(NZ):
                 for o in range(2):
                     at = (z, me.y, o) if seq[2] == "y" else (z, o, me.x)
@@ -1452,24 +1466,27 @@
     def strips(kinds):
         return tuple((kind, 1, min(strip, wide - k * strip)) for k, kind in enumerate(kinds))
 
-    return {
-        "square": (rows, columns, LOW, cuts(("zfx", "zfy"), (half, half))),
-        "broad": (rows, wide, LOW, strips(("zfx", "zfy", "zmx", "zmy"))),
-        "broad_f": (rows, wide, LOW, strips(("zfx", "zfy", "zfx", "zfy"))),
-        "broad_m": (rows, wide, LOW, strips(("zmx", "zmy", "zmx", "zmy"))),
-        "tall": (tile, columns, LOW, cuts(("zfx", "zfy", "zmx", "zmy"), (long, long, long, short))),
-        "square_m": (rows, columns, LOW, cuts(("zmx", "zmy"), (half, half))),
-        "tall_f": (tile, columns, LOW, cuts(("zfx", "zfy", "zfx", "zfy"), (long, long, long, short))),
-        "tall_m": (tile, columns, LOW, cuts(("zmx", "zmy", "zmx", "zmy"), (long, long, long, short))),
-        "gain": (16, 2 * rows, LOW, cuts(("zfx",), (16,))),
-        "gain_grad": (8, 2 * rows, F32, cuts(("zfx",), (8,))),
-    }
+    def pairs(letters):
+        return tuple("z" + letter + axis for letter in letters for axis in "xy")
+
+    def of(kind, letters):
+        if kind == "square":
+            return (rows, columns, LOW, cuts(pairs(letters), (half, half)))
+        if kind == "broad":
+            return (rows, wide, LOW, strips(pairs(letters)))
+        if kind == "tall":
+            return (tile, columns, LOW, cuts(pairs(letters), (long, long, long, short)))
+        if kind == "gain":
+            return (16, 2 * rows, LOW, cuts(("zfx",), (16,)))
+        return (8, 2 * rows, F32, cuts(("zfx",), (8,)))
+
+    return of
 
 
 def gather_plan(w_query, w_key, w_value, w_out, w_gate, w_up, w_down, gain_attn, gain_mlp):
     kind = kinds(w_query, w_gate, w_down)
-    names = ("gain", "square", "square_m", "square_m", "square", "broad", "broad_m", "tall_m")
-    plan = Plan([kind[name] for name in names])
+    names = GATHER_KINDS
+    plan = Plan([kind(*name) for name in names])
     both = jnp.concatenate([gain_attn[None], gain_mlp[None]], axis=0)
     shards = [
         both,
@@ -1500,8 +1517,8 @@
 ):
     plan, shards = gather_plan(w_query, w_key, w_value, w_out, w_gate, w_up, w_down, gain_attn, gain_mlp)
     kind = kinds(w_query, w_gate, w_down)
-    names = ("tall", "broad_f", "broad", "square", "square", "square", "square", "gain_grad")
-    back = Plan([kind[name] for name in names])
+    names = SCATTER_KINDS
+    back = Plan([kind(*name) for name in names])
     results, sums = block_all(plan, back, seq_lengths, tokens, cotangent, shards)
     outs = finish_all(results[0], results[1], sums, w_query, w_gate, w_down)
     return (*outs[:9], outs[9].reshape(-1), outs[10].reshape(-1))

time: 241 us -> 235 us (0.975)
  Pallas kernels: 238 us -> 233 us
    pallas_call x1, Pallas kernels: 233 us -> 228 us  [block_all(): pl.pallas_call(functools.partial(block_kernel, ahead, back), out_shape=[s...]
where the time goes in v7:
time: 235 us
  Pallas kernels  233 us (99%)
    pallas_call x1, Pallas kernels, block_all(): pl.pallas_call(functools.partial(block_kernel, ahead, back), out_shape=[s...  228 us
    pallas_call x1, Pallas kernels, finish_all(): pl.pallas_call(finish_kernel, out_shape=outs, in_specs=[anywhere] * len(i...  4.79 us

profile of v7, /device:TPU:0, one launch (start us, length us, event | category | flops | bytes accessed | tf_op | source)
XLA Modules:
  0.0 234.7 jit_solution(2706898148081228739)
XLA Ops:
  0.6 1.2 pad_maximum_fusion.refs_3_
  1.8 227.9 %block_all.1 = (bf16[2,4,2,2,64,512]{5,4,3,2,1,0:T(8,128)(2,1)}, bf16[2,4,2,2,64,512]{5,4,3,2,1,0:T(8,128)(2,1)}, bf16[2,4,2,2,64,512]{5,4,3,2,1,0:T(8,128)(2,1)...) custom-call(s32[1,3]{1,0:T(1,128)} %refs_0_.1, ...), custom_call_target="tpu_custom_call" | custom-call | tf_op jit(solution)/shard_map/block_all/pallas_call | solution.py:1377
  229.7 4.8 %finish_all.1 = (bf16[512,1024]{1,0:T(8,128)(2,1)}, f32[512,1024]{1,0:T(8,128)}, f32[64,512]{1,0:T(8,128)}, f32[64,512]{1,0:T(8,128)}, f32[64,512]{1,0:T(8,128)}...) custom-call(bf16[512,1024]{1,0:T(8,128)(2,1)} %get-tuple-element.32., ...), custom_call_target="tpu_custom_call" | custom-call | tf_op jit(solution)/shard_map/finish_all/pallas_call | solution.py:1443

commit v8 on v7

--- a/solution.py
+++ b/solution.py
@@ -349,35 +349,35 @@
 
 
 SCRIPT = (
-    ("start", 4), ("start", 7), ("start", 9), ("start", 0), ("start", 13), ("start", 2), ("start", 11),
-    ("start", 5), ("start", 10), (0, 4, 0), ("start", 18), ("start", 15), ("start", 19), ("start", 20),
-    (0, 0, 0, 1), ("start", 6), ("start", 3), (0, 5, 0), (0, 10, 0, 1), ("start", 1), (0, 9, 0, 1), (0, 6, 0),
-    (0, 5, 1, 1), (0, 2, 0, 1), ("start", 16), (0, 9, 0, 2), (0, 0, 0, 2), (0, 1, 0, 1), (0, 10, 0, 2),
-    ("start", 17), ("start", 12), (0, 18, 0), (0, 0, 0, 3), ("start", 14), (0, 3, 0), (0, 1, 0, 2),
-    (0, 2, 0, 2), (0, 0, 1), (0, 9, 0, 3), (0, 10, 0, 3), (0, 2, 0, 3), (0, 20, 0), (0, 18, 1, 1), (0, 0, 2),
-    (0, 3, 1, 1), (0, 4, 1, 1), (0, 9, 1), (0, 7, 0, 1), (0, 1, 0, 3), (0, 12, 0), (0, 17, 0), (0, 19, 0),
-    (0, 2, 1), (0, 5, 1, 2), (0, 6, 1, 1), (0, 4, 1, 2), ("start", 8), (0, 1, 1), (0, 10, 1), (0, 3, 1, 2),
-    "norm", (0, 8, 0, 1), (0, 2, 2), (0, 5, 1, 3), (0, 7, 0, 2), (0, 8, 0, 2), (0, 7, 0, 3), (0, 20, 1, 1),
-    (0, 19, 1, 1), (0, 9, 2), (0, 1, 2), (0, 13, 0), (0, 17, 1, 1), (0, 6, 1, 2), (0, 4, 1, 3), (0, 3, 1, 3),
-    (0, 5, 2), (0, 8, 0, 3), (0, 6, 1, 3), (0, 20, 1, 2), (0, 17, 1, 2), (0, 18, 1, 2), (0, 7, 1), (0, 10, 2),
-    (0, 3, 2), (0, 4, 2), (0, 11, 0), "query", (0, 8, 1), (0, 18, 1, 3), (0, 14, 0), (0, 17, 1, 3),
-    (0, 13, 1, 1), (0, 16, 0), (0, 6, 2), "key", (0, 19, 1, 2), "value", (0, 19, 1, 3), (0, 16, 1, 1),
-    (0, 14, 1, 1), (0, 13, 1, 2), (0, 20, 1, 3), (0, 15, 0), ("see", 0), (0, 7, 2), (0, 8, 2), (0, 11, 1, 1),
-    ("see", 1), (0, 17, 2), (0, 13, 1, 3), ("see", 2), (0, 14, 1, 2), ("see", 3), (0, 12, 1, 1), (0, 18, 2),
-    (0, 14, 1, 3), (0, 19, 2), (0, 11, 1, 2), (0, 20, 2), (0, 15, 1, 1), "project", (0, 16, 1, 2), (0, 13, 2),
-    (0, 11, 1, 3), (0, 15, 1, 2), (0, 12, 1, 2), ("hidden", 0), ("hidden", 1), (0, 15, 1, 3), (0, 16, 1, 3),
-    (0, 14, 2), (0, 12, 1, 3), ("mlp", 0), ("mlp", 1), ("up", 0), (0, 11, 2), ("gate", 0), (0, 15, 2),
-    ("gate", 1), ("up", 1), (0, 12, 2), (0, 16, 2), ("mlp", 2), ("mlp", 3), (1, 9, 0), ("up", 2), (1, 8, 0),
-    ("dh2", 0), ("gate", 2), ("gate", 3), ("up", 3), "mix", (1, 9, 1), (1, 8, 1), "down", (1, 11, 0),
-    ("dh2", 1), "norm2", (1, 10, 0), "heads", (1, 6, 0), (1, 7, 0), ("attend", 0), ("attend", 1),
-    ("attend", 2), ("attend", 3), (1, 3, 0), "out", (1, 6, 1), (1, 0, 0), ("qkv", 0), (1, 2, 0), "dh1",
-    (1, 1, 0), (1, 7, 1), ("qkv", 1), (1, 14, 0), (1, 9, 2), (1, 0, 1), (1, 13, 0), "norm1", (1, 1, 1),
-    (1, 15, 0), (1, 12, 0), ("qkv", 2), (1, 14, 1), (1, 7, 2), "gains", (1, 13, 1), (1, 6, 2), (1, 12, 1),
-    (1, 16, 0), (1, 15, 1), (1, 17, 0), (1, 20, 0), (1, 5, 0), (1, 19, 0), (1, 18, 0), (1, 20, 1), (1, 0, 2),
-    (1, 10, 1), (1, 17, 1), (1, 4, 0), (1, 16, 1), (1, 2, 1), (1, 19, 1), (1, 11, 1), (1, 13, 2), (1, 20, 2),
-    (1, 14, 2), (1, 3, 1), (1, 8, 2), (1, 5, 1), (1, 18, 1), (1, 1, 2), (1, 4, 1), (1, 11, 2), (1, 15, 2),
-    (1, 12, 2), (1, 10, 2), (1, 2, 2), (1, 17, 2), (1, 16, 2), (1, 5, 2), (1, 3, 2), (1, 4, 2), (1, 19, 2),
-    (1, 18, 2),
+    ("start", 7), ("start", 6), ("start", 3), ("start", 10), ("start", 2), ("start", 19), ("start", 0),
+    ("start", 9), (0, 3, 0), (0, 0, 0, 1), (0, 2, 0, 1), ("start", 17), ("start", 5), ("start", 18),
+    ("start", 14), ("start", 1), ("start", 20), (0, 0, 0, 2), (0, 9, 0, 1), ("start", 15), (0, 3, 1, 1),
+    (0, 10, 0, 1), (0, 2, 0, 2), (0, 9, 0, 2), (0, 5, 0), (0, 2, 0, 3), ("start", 16), ("start", 13),
+    (0, 0, 0, 3), (0, 10, 0, 2), (0, 1, 0, 1), (0, 9, 0, 3), ("start", 4), (0, 0, 1), (0, 10, 0, 3),
+    (0, 5, 1, 1), (0, 1, 0, 2), (0, 1, 0, 3), (0, 6, 0), ("start", 8), (0, 0, 2), (0, 20, 0), (0, 5, 1, 2),
+    (0, 3, 1, 2), (0, 9, 1), (0, 18, 0), (0, 2, 1), (0, 17, 0), (0, 7, 0, 1), (0, 1, 1), (0, 8, 0, 1),
+    ("start", 12), (0, 10, 1), (0, 6, 1, 1), (0, 4, 0), (0, 3, 1, 3), (0, 7, 0, 2), (0, 7, 0, 3), (0, 19, 0),
+    (0, 4, 1, 1), (0, 6, 1, 2), (0, 6, 1, 3), (0, 4, 1, 2), (0, 19, 1, 1), (0, 5, 1, 3), (0, 4, 1, 3),
+    (0, 8, 0, 2), (0, 2, 2), (0, 17, 1, 1), (0, 1, 2), (0, 18, 1, 1), (0, 16, 0), (0, 8, 0, 3), "norm",
+    (0, 20, 1, 1), (0, 14, 0), (0, 3, 2), (0, 17, 1, 2), ("start", 11), (0, 20, 1, 2), (0, 7, 1), (0, 8, 1),
+    (0, 4, 2), "query", (0, 5, 2), (0, 17, 1, 3), (0, 20, 1, 3), (0, 6, 2), (0, 13, 0), (0, 19, 1, 2),
+    (0, 18, 1, 2), "key", (0, 14, 1, 1), "value", (0, 19, 1, 3), (0, 18, 1, 3), (0, 14, 1, 2), (0, 13, 1, 1),
+    (0, 11, 0), (0, 20, 2), ("see", 0), (0, 7, 2), (0, 8, 2), (0, 15, 0), ("see", 1), (0, 13, 1, 2),
+    (0, 9, 2), (0, 14, 1, 3), (0, 17, 2), ("see", 2), (0, 16, 1, 1), ("see", 3), (0, 13, 1, 3), (0, 18, 2),
+    (0, 10, 2), (0, 15, 1, 1), (0, 19, 2), (0, 12, 0), (0, 11, 1, 1), "project", (0, 15, 1, 2), ("hidden", 0),
+    (0, 11, 1, 2), (0, 15, 1, 3), (0, 16, 1, 2), (0, 13, 2), ("hidden", 1), (0, 14, 2), (0, 16, 1, 3),
+    (0, 11, 1, 3), (0, 12, 1, 1), ("mlp", 0), (0, 12, 1, 2), ("mlp", 1), (0, 12, 1, 3), ("up", 0), (0, 15, 2),
+    (0, 11, 2), ("gate", 0), ("gate", 1), ("up", 1), (0, 12, 2), (0, 16, 2), ("mlp", 2), ("mlp", 3),
+    (1, 9, 0), (1, 8, 0), ("up", 2), ("gate", 2), ("gate", 3), "mix", (1, 8, 1), ("up", 3), ("dh2", 0),
+    (1, 11, 0), "down", (1, 7, 0), (1, 9, 1), (1, 10, 0), ("dh2", 1), "norm2", (1, 6, 0), "heads", (1, 7, 1),
+    ("attend", 0), (1, 3, 0), "out", ("attend", 1), ("attend", 2), ("attend", 3), (1, 0, 0), (1, 1, 0),
+    (1, 6, 1), (1, 2, 0), (1, 12, 0), (1, 10, 1), (1, 13, 0), ("qkv", 0), "dh1", (1, 0, 1), ("qkv", 1),
+    (1, 7, 2), (1, 12, 1), (1, 1, 1), (1, 14, 0), (1, 15, 0), ("qkv", 2), "norm1", (1, 8, 2), (1, 13, 1),
+    (1, 11, 1), "gains", (1, 14, 1), (1, 16, 0), (1, 15, 1), (1, 9, 2), (1, 17, 0), (1, 11, 2), (1, 10, 2),
+    (1, 6, 2), (1, 20, 0), (1, 5, 0), (1, 19, 0), (1, 16, 1), (1, 20, 1), (1, 18, 0), (1, 17, 1), (1, 4, 0),
+    (1, 14, 2), (1, 2, 1), (1, 19, 1), (1, 3, 1), (1, 20, 2), (1, 5, 1), (1, 18, 1), (1, 12, 2), (1, 0, 2),
+    (1, 4, 1), (1, 15, 2), (1, 16, 2), (1, 17, 2), (1, 3, 2), (1, 5, 2), (1, 2, 2), (1, 1, 2), (1, 13, 2),
+    (1, 4, 2), (1, 19, 2), (1, 18, 2),
 )
 GATHER_KINDS = (("gain", "f"), ("square", "f"), ("square", "m"), ("square", "m"), ("square", "f"), ("broad", "fm"), ("broad", "mm"), ("tall", "mm"))
 SCATTER_KINDS = (("tall", "fm"), ("broad", "lf"), ("broad", "fm"), ("square", "f"), ("square", "f"), ("square", "f"), ("square", "f"), ("gain_grad", "f"))
@@ -733,7 +733,7 @@
 
 def block_kernel(ahead, back, *refs):
     n = len(ahead.tensors)
-    (lens, x_h, dy_h), raw, refs = refs[:3], refs[3 : 3 + n], refs[3 + n :]
+    (lens, x_h, dy_h), raw_h, refs = refs[:3], refs[3 : 3 + n], refs[3 + n :]
     hbm_bufs, refs = refs[: n - 1], refs[n - 1 :]
     (mixed_o, gtok_o, q_h, p_h, ha_h, ho_h, hm_h, hid_h), refs = refs[:8], refs[8:]
     outs_h, refs = refs[:n], refs[n:]
@@ -743,6 +743,7 @@
     got, refs = [refs[3 * i : 3 * i + 3] for i in range(count)], refs[3 * count :]
     (gate_pad, up_pad, down_pad, gain_buf, gains, xb, h1, da, db, kx, vx, o, x1, hid), refs = refs[:14], refs[14:]
     (dar, dbr, pair_of, pair_low), refs = refs[:4], refs[4:]
+    raw, refs = list(refs[:7]) + [raw_h[7]], refs[7:]
     (dy, dyr, dh, dxr_r, turned, pool, broad), refs = refs[:7], refs[7:]
     (kc, vc, rim_k, rim_v, gain_sum, gain_other), refs = refs[:6], refs[6:]
     (a_send, a_recv, own_sem, b_send, b_recv, load_sem, pool_sem, broad_sem, turn_sem), refs = refs[:9], refs[9:]
@@ -768,9 +769,11 @@
     def own(size, side=0):
         return pl.ds(pl.multiple_of((me.s if side == 0 else 1 - me.s) * size, 128), size)
 
+    get_raw = [load(raw_h[t], raw[t]) for t in range(7)]
     get_x, get_dy = load(x_h, xb), load(dy_h, dy)
     me.greet()
     pair_of[...] = jnp.zeros_like(pair_of)
+    get_raw[0].wait()
     blank = jnp.zeros((1, raw[0].shape[1]), F32)
     for k in range(2):
         gain = raw[0][k : k + 1, :].astype(F32)
@@ -795,7 +798,11 @@
         down_pad[...] = jnp.concatenate([raw[7][...], jnp.zeros((tile - part, down_pad.shape[1]), LOW)], axis=0)
 
     def prepare(t):
+        if t not in ready and 0 < t < 5:
+            get_raw[t].wait()
         if t >= 5 and 5 not in ready:
+            get_raw[5].wait()
+            get_raw[6].wait()
             pad_shards()
             for k in range(5, n):
                 gather.own_copy(k).start()
@@ -893,8 +900,8 @@
         project(3, h1, put_into(vx, WINDOW))
         rim(1, vx).start()
 
-    first_end = lens[0, 0]
-    second_end = first_end + lens[0, 1]
+    first_end = lens[0:1, 0:1]
+    second_end = first_end + lens[0:1, 1:2]
 
     def attend(b, _):
         base = me.s * rows + b * WINDOW
@@ -1356,6 +1363,7 @@
         ((rows, wide), LOW),
         (ahead.tensors[0][:2], F32),
         (ahead.tensors[0][:2], LOW),
+        *((shard.shape, LOW) for shard in shards[:7]),
         ((rows, width), LOW),
         ((rows, columns), LOW),
         ((rows, width), F32),
@@ -1379,10 +1387,10 @@
         out_shape=[shape(b, LOW) for b in bufs[1:]]
         + [shape(*s) for s in kept]
         + [shape(t[:2], F32) for t in back.tensors],
-        in_specs=[pl.BlockSpec(memory_space=pltpu.SMEM), anywhere, anywhere] + [inside] * n,
+        in_specs=[inside, anywhere, anywhere] + [anywhere] * (n - 1) + [inside],
         out_specs=[anywhere] * (n - 1 + len(kept) + n),
         scratch_shapes=[pltpu.VMEM(*s) for s in results + totals + got + scratch]
-        + [dma((9 * na,)), dma((9 * na,)), dma((n,)), dma((5 * nb,)), dma((5 * nb,)), dma((36,))]
+        + [dma((9 * na,)), dma((9 * na,)), dma((n,)), dma((5 * nb,)), dma((5 * nb,)), dma((44,))]
         + [dma((2, 3)), dma((2, 2)), dma((2, 1)), dma((29,)), dma((29,))],
         compiler_params=pltpu.CompilerParams(
             collective_id=0, has_side_effects=True, vmem_limit_bytes=VMEM_LIMIT
@@ -1396,10 +1404,22 @@
     n = 10
     ins, outs, held, made = refs[:n], refs[n : 2 * n + 1], refs[2 * n + 1 : 3 * n + 1], refs[3 * n + 1 : 4 * n + 2]
     sem_in, sem_out = refs[4 * n + 2 :]
-    gets = [pltpu.make_async_copy(src, dst, sem_in.at[k]) for k, (src, dst) in enumerate(zip(ins, held))]
-    for copy in gets:
+    chunks = [(k, pl.ds(j * (held[k].shape[0] // 4), held[k].shape[0] // 4)) for k in (1, 0) for j in range(4)]
+    large = [
+        pltpu.make_async_copy(ins[k].at[at, :], held[k].at[at, :], sem_in.at[n + j]) for j, (k, at) in enumerate(chunks)
+    ]
+    gets = [pltpu.make_async_copy(ins[k], held[k], sem_in.at[k]) for k in range(2, n)]
+    for copy in large[:2] + gets + large[2:]:
         copy.start()
     puts = []
+
+    def pass_on(some):
+        for j in some:
+            k, at = chunks[j]
+            large[j].wait()
+            copy = pltpu.make_async_copy(held[k].at[at, :], outs[k].at[at, :], sem_out.at[n + 1 + j])
+            copy.start()
+            puts.append(copy)
 
     def put(k, src):
         copy = pltpu.make_async_copy(src, outs[k], sem_out.at[k])
@@ -1407,10 +1427,12 @@
         puts.append(copy)
 
     down, up, gate, out, query, key, value, gain = held[2:]
-    for copy in gets[2:]:
+    pass_on(range(2))
+    for copy in gets:
         copy.wait()
     for k, src in ((2, query), (3, key), (4, value), (5, out)):
         put(k, src)
+    pass_on(range(2, 5))
     rows, part, tile = query.shape[0], outs[8].shape[0], down.shape[0]
     made[8][...] = down[...][:part]
     put(8, made[8])
@@ -1426,9 +1448,7 @@
     made[10][...] = own[1:2]
     put(9, made[9])
     put(10, made[10])
-    for k in range(2):
-        gets[k].wait()
-        put(k, held[k])
+    pass_on(range(5, 8))
     for copy in puts:
         copy.wait()
 
@@ -1446,7 +1466,7 @@
         in_specs=[anywhere] * len(ins),
         out_specs=[anywhere] * len(outs),
         scratch_shapes=[pltpu.VMEM(a.shape, a.dtype) for a in ins + outs]
-        + [pltpu.SemaphoreType.DMA((len(ins),)), pltpu.SemaphoreType.DMA((len(outs),))],
+        + [pltpu.SemaphoreType.DMA((len(ins) + 8,)), pltpu.SemaphoreType.DMA((len(outs) + 8,))],
         compiler_params=pltpu.CompilerParams(vmem_limit_bytes=62 * 2**20),
         name="finish_all",
     )(*ins)

time: 235 us -> 235 us (level)
  no operation moved by 1% of the time
where the time goes in v8:
time: 235 us; the launch traced here: 234 us
  Pallas kernels  232 us (99%)
    pallas_call x1, Pallas kernels, block_all(): pl.pallas_call(functools.partial(block_kernel, ahead, back), out_shape=[s...  228 us

profile of v8, /device:TPU:0, one launch (start us, length us, event | category | flops | bytes accessed | tf_op | source)
XLA Modules:
  0.0 234.1 jit_solution(3085676973692140551)
XLA Ops:
  0.6 1.2 pad_maximum_fusion.refs_3_
  1.8 227.9 %block_all.1 = (bf16[2,4,2,2,64,512]{5,4,3,2,1,0:T(8,128)(2,1)}, bf16[2,4,2,2,64,512]{5,4,3,2,1,0:T(8,128)(2,1)}, bf16[2,4,2,2,64,512]{5,4,3,2,1,0:T(8,128)(2,1)...) custom-call(s32[1,3]{1,0:T(1,128)} %refs_0_.1, ...), custom_call_target="tpu_custom_call" | custom-call | tf_op jit(solution)/shard_map/block_all/pallas_call | solution.py:1385
  229.7 4.2 %finish_all.1 = (bf16[512,1024]{1,0:T(8,128)(2,1)}, f32[512,1024]{1,0:T(8,128)}, f32[64,512]{1,0:T(8,128)}, f32[64,512]{1,0:T(8,128)}, f32[64,512]{1,0:T(8,128)}...) custom-call(bf16[512,1024]{1,0:T(8,128)(2,1)} %get-tuple-element.32., ...), custom_call_target="tpu_custom_call" | custom-call | tf_op jit(solution)/shard_map/finish_all/pallas_call | solution.py:1463
